TPU v7x, 32 devices: a whole 2x2x4 slice. The times are simulated.
32 devices in a mesh: groups: 2 (over y), seq: 4 (over z), head: 2 (over x), sub: 2 (over core).
Axes of the slice: x: 2, y: 2, z: 4, core: 2. Of those that a mesh axis runs over, the one named last changes fastest.
Arguments:
- queries: bfloat16 [6144, 3072], P(('groups', 'seq', 'sub'), 'head'), parts along dimension 0, may hold values from -6 to 6
- keys: bfloat16 [6144, 3072], P(('groups', 'seq', 'sub'), 'head'), parts along dimension 0, may hold values from -6 to 6
- values: bfloat16 [6144, 3072], P(('groups', 'seq', 'sub'), 'head'), parts along dimension 0, may hold values from -6 to 6
- kv_list: int32 [16, 6], P(('groups', 'seq', 'sub')), parts along dimension 0, may hold values from -1 to 7, as said below
- kv_count: int32 [16], P(('groups', 'seq', 'sub')), parts along dimension 0, may hold values from 1 to 6, as said below
- out_weight: bfloat16 [3072, 3072], P('head'), may hold values from -0.5 to 0.5
- gate: float32 [3072], P('head'), may hold values from 1 to 4
Outputs:
- layer_out: bfloat16 [6144, 3072], P(('groups', 'seq', 'sub'), 'head'), parts along dimension 0
There are 2 independent parts, one for each index of `groups`. A program takes and returns all parts, laid end to end along the dimension named above; an argument that names none is the same for every part. Nothing has to cross between parts.
Inputs may be any that keep to these rules, and one draw needn't show every extreme that they name: `kv_list`: tile t lies at time t // 2 and height t % 2 of a slab of 4 x 2 x 1 tiles. Row t begins with t itself, then lists in a drawn order the other tiles of t's 3 x 3 x 3 window clipped to the slab (time within one of t's), then -1 in the entries left over. `kv_count`: at most the number of tiles in the row's clipped window; some tile has 6 and some tile has 1.
All inputs are finite; a program needn't handle non-finite values.
Results may differ from a plain program's by a relative error of at most 0.014.
Values may be sent and summed in bfloat16 or wider, within the bound.
No kernel may reach another device: no remote copies, remote signals or barrier semaphores. Data moves between devices by JAX's collectives and lax.ppermute only.
A program may use at most 128 MiB of HBM per device.

v0:
```python
import math

import jax
import jax.numpy as jnp
from jax import lax
from jax.sharding import PartitionSpec as P

HD = 128
REACH = 3


NEG_FILL = -1e30


def shifted(block, axis, distance):
    devices = range(lax.axis_size(axis))
    route = [(i - distance, i) for i in devices if i - distance in devices]
    return lax.ppermute(block, axis, route)


def tile_scores(query_tiles, key_tiles):
    scores = jnp.einsum(
        "aqhd,bkhd->abhqk", query_tiles, key_tiles, preferred_element_type=jnp.float32
    )
    return scores * (1.0 / math.sqrt(query_tiles.shape[-1]))


def local(queries, keys, values, kv_list, kv_count, out_weight, gate):
    tiles_here = kv_list.shape[0]
    tile_rows = queries.shape[0] // tiles_here
    width = queries.shape[1]
    heads_here = width // HD
    query_tiles = queries.reshape(tiles_here, tile_rows, heads_here, HD)
    kv_pair = jnp.stack([keys, values])
    position = lax.axis_index(("seq", "sub"))
    places = lax.axis_size(("seq", "sub"))
    blocks = [(position, kv_pair)]
    for offset in range(1, REACH + 1):
        for heading in (offset, -offset):
            blocks.append((position - heading, shifted(kv_pair, ("seq", "sub"), heading)))
    live_slots = jnp.arange(kv_list.shape[1])[None, :] < kv_count[:, None]

    def included(anchor):
        inside = (anchor >= 0) & (anchor < places)
        neighbour = anchor * tiles_here + jnp.arange(tiles_here, dtype=jnp.int32)
        hits = (kv_list[:, :, None] == neighbour[None, None, :]) & live_slots[:, :, None]
        return jnp.any(hits, axis=1) & inside

    peak = jnp.full((tiles_here, heads_here, tile_rows), NEG_FILL, jnp.float32)
    for anchor, fetched in blocks:
        block_mask = included(anchor)
        block_key_tiles = fetched[0].reshape(tiles_here, tile_rows, heads_here, HD)
        scores = jnp.where(
            block_mask[:, :, None, None, None], tile_scores(query_tiles, block_key_tiles), NEG_FILL
        )
        peak = jnp.maximum(peak, jnp.max(scores, axis=(1, 4)))
    state = (
        jnp.zeros((tiles_here, tile_rows, heads_here, HD), jnp.float32),
        jnp.zeros((tiles_here, heads_here, tile_rows), jnp.float32),
    )
    for anchor, fetched in blocks:
        mask = included(anchor)
        key_tiles = fetched[0].reshape(tiles_here, tile_rows, heads_here, HD)
        value_tiles = fetched[1].reshape(tiles_here, tile_rows, heads_here, HD)
        compute_accum, compute_total = state
        compute_scores = jnp.where(
            mask[:, :, None, None, None], tile_scores(query_tiles, key_tiles), NEG_FILL
        )
        weights = jnp.exp(compute_scores - peak[:, None, :, :, None])
        compute_total = compute_total + jnp.sum(weights, axis=(1, 4))
        compute_accum = compute_accum + jnp.einsum(
            "abhqk,bkhd->aqhd",
            weights.astype(jnp.bfloat16),
            value_tiles,
            preferred_element_type=jnp.float32,
        )
        state = (compute_accum, compute_total)
    accum, total = state
    attention = (
        (accum / jnp.transpose(total, (0, 2, 1))[:, :, :, None])
        .reshape(tiles_here * tile_rows, width)
        .astype(jnp.bfloat16)
    )
    summed = lax.psum_scatter(
        lax.dot_general(
            out_weight, attention, (((0,), (1,)), ((), ())), preferred_element_type=jnp.float32
        ).astype(jnp.bfloat16),
        "head",
        scatter_dimension=0,
        tiled=True,
    ).astype(jnp.float32)
    return (jnp.transpose(summed) * gate[None, :]).astype(jnp.bfloat16)


def solution(mesh):
    return jax.shard_map(
        local,
        mesh=mesh,
        in_specs=(
            P(("groups", "seq", "sub"), "head"),
            P(("groups", "seq", "sub"), "head"),
            P(("groups", "seq", "sub"), "head"),
            P(("groups", "seq", "sub"), None),
            P(("groups", "seq", "sub")),
            P("head", None),
            P("head"),
        ),
        out_specs=P(("groups", "seq", "sub"), "head"),
        check_vma=False,
    )
```

profile of v0, /device:TPU:13, one launch (start us, length us, event | category | flops | bytes accessed | tf_op | source)
XLA Modules:
  0.0 281.1 jit_solution(356027137580236161)
XLA Ops:
  6.5 1.8 copy.30
  8.4 0.7 copy.35
  9.1 1.7 pad_maximum_fusion
  10.8 2.8 collective-permute-start.5
  13.6 1.9 collective-permute-start.3
  15.5 4.6 %collective-permute-start.2 = (bf16[2,384,1536]{1,2,0:T(8,128)(2,1)}, bf16[2,384,1536]{1,2,0:T(8,128)(2,1)}, u32[]{:S(2)}, u32[]{:S(2)}) collective-permute-start(bf16[2,384,1536]{1,2,0:T(8,128)(2,1)} %pad_maximum_fusion), channel_id=1, source_target_pairs={{0,4},{1,5},{4,8},{5,9},{8,12},{9,13},{2,6},{3,7},{6,10},{7,11},{1... | collective-permute-start | bytes 7077896 | tf_op jit(solution)/shard_map/ppermute | solution.py:18
  20.1 1.9 collective-permute-start.1
  22.0 3.9 %collective-permute-start = (bf16[2,384,1536]{1,2,0:T(8,128)(2,1)}, bf16[2,384,1536]{1,2,0:T(8,128)(2,1)}, u32[]{:S(2)}, u32[]{:S(2)}) collective-permute-start(bf16[2,384,1536]{1,2,0:T(8,128)(2,1)} %pad_maximum_fusion), channel_id=1, source_target_pairs={{0,1},{1,4},{4,5},{5,8},{8,9},{9,12},{12,13},{2,3},{3,6},{6,7},{7,... | collective-permute-start | bytes 7077896 | tf_op jit(solution)/shard_map/ppermute | solution.py:18
  26.6 1.7 copy.31
  28.3 0.8 and_reduce_fusion.6
  33.4 1.2 bitcast_reduce_fusion.6
  34.7 50.8 %collective-permute-done.5 = bf16[2,384,1536]{1,2,0:T(8,128)(2,1)} collective-permute-done((bf16[2,384,1536]{1,2,0:T(8,128)(2,1)}, bf16[2,384,1536]{1,2,0:T(8,128)(2,1)}, u32[]{:S(2)}, u32[]{:S(2)}) %collective-permute-start.5) | collective-permute-done | bytes 2359328 | tf_op jit(solution)/shard_map/ppermute | solution.py:18
  85.4 2.1 collective-permute-start.4
  87.5 1.9 fusion.94
  89.4 1.2 bitcast_reduce_fusion
  90.6 52.1 %collective-permute-done.3 = bf16[2,384,1536]{1,2,0:T(8,128)(2,1)} collective-permute-done((bf16[2,384,1536]{1,2,0:T(8,128)(2,1)}, bf16[2,384,1536]{1,2,0:T(8,128)(2,1)}, u32[]{:S(2)}, u32[]{:S(2)}) %collective-permute-start.3) | collective-permute-done | bytes 2359328 | tf_op jit(solution)/shard_map/ppermute | solution.py:18
  142.7 1.9 fusion.98
  144.5 1.2 bitcast_reduce_fusion.2
  145.7 0.0 copy-start
  145.8 0.0 collective-permute-done.2
  145.8 3.6 %fusion.97 = (bf16[1,384,1536]{1,2,0:T(8,128)(2,1)S(1)}, bf16[1,384,1536]{1,2,0:T(8,128)(2,1)S(1)}) fusion(bf16[2,384,1536]{1,2,0:T(8,128)(2,1)} %collective-permute-done.2), kind=kLoop, calls=%fused_computation.124 | loop fusion | bytes 4718592 | tf_op jit(solution)/shard_map/slice | solution.py:64
  149.4 1.2 bitcast_reduce_fusion.3
  150.6 17.2 %collective-permute-done.1 = bf16[2,384,1536]{1,2,0:T(8,128)(2,1)} collective-permute-done((bf16[2,384,1536]{1,2,0:T(8,128)(2,1)}, bf16[2,384,1536]{1,2,0:T(8,128)(2,1)}, u32[]{:S(2)}, u32[]{:S(2)}) %collective-permute-start.1) | collective-permute-done | bytes 2359328 | tf_op jit(solution)/shard_map/ppermute | solution.py:18
  167.8 1.9 fusion.96
  169.7 4.0 %bitcast_reduce_fusion.4 = (f32[12,384]{1,0:T(8,128)S(1)}, f32[12,384,384]{2,1,0:T(8,128)}) fusion(pred[]{:T(512)S(6)} %and.136, bf16[384,12,128]{0,2,1:T(8,128)(2,1)S(1)} %bitcast.212, bf16[384,12,128]{0,2,1:T(8,128)(2,1)S(1)} %bitcast.200), kind=kOutput, calls=%fused_computation.13 | convolution fusion | flops 458288640 | bytes 9455617 | tf_op jit(solution)/shard_map/aqhd,bkhd->abhqk/dot_general | solution.py:22
  173.7 0.0 collective-permute-done
  173.7 2.9 %fusion.95 = (bf16[1,384,1536]{1,2,0:T(8,128)(2,1)}, bf16[1,384,1536]{1,2,0:T(8,128)(2,1)S(1)}) fusion(bf16[2,384,1536]{1,2,0:T(8,128)(2,1)} %collective-permute-done), kind=kLoop, calls=%fused_computation.122 | loop fusion | bytes 4718592 | tf_op jit(solution)/shard_map/slice | solution.py:64
  176.5 4.0 %bitcast_reduce_fusion.5 = (f32[12,384]{1,0:T(8,128)S(1)}, f32[12,384,384]{2,1,0:T(8,128)}) fusion(pred[]{:T(512)S(6)} %and.133, bf16[384,12,128]{0,2,1:T(8,128)(2,1)S(1)} %bitcast.213, bf16[384,12,128]{0,2,1:T(8,128)(2,1)S(1)} %bitcast.201), kind=kOutput, calls=%fused_computation.16 | convolution fusion | flops 458288640 | bytes 9455617 | tf_op jit(solution)/shard_map/aqhd,bkhd->abhqk/dot_general | solution.py:22
  180.6 0.0 collective-permute-done.4
  180.6 1.2 fusion.99
  181.8 4.1 %bitcast_reduce_fusion.1 = (f32[12,384]{1,0:T(8,128)S(1)}, f32[12,384,384]{2,1,0:T(8,128)}) fusion(pred[]{:T(512)S(6)} %and.145, bf16[384,12,128]{0,2,1:T(8,128)(2,1)S(1)} %bitcast.208, bf16[384,12,128]{0,2,1:T(8,128)(2,1)S(1)} %bitcast.202), kind=kOutput, calls=%fused_computation.4 | convolution fusion | flops 458288640 | bytes 9455617 | tf_op jit(solution)/shard_map/aqhd,bkhd->abhqk/dot_general | solution.py:22
  186.0 1.7 fusion.41
  187.7 4.7 %fusion.38 = f32[12,128,384]{2,1,0:T(8,128)S(1)} fusion(bf16[384,12,128]{0,2,1:T(8,128)(2,1)S(1)} %bitcast.219, f32[12,384,384]{2,1,0:T(8,128)} %get-tuple-element.42, f32[12,384]{1,0:T(8,128)S(1)} %maximum_maximum_fusion, pred[]{:T(512)S(6)} %and.133), kind=kOutput, calls=%fused_computation.55 | convolution fusion | flops 460062720 | bytes 10635265 | tf_op jit(solution)/shard_map/abhqk,bkhd->aqhd/dot_general | solution.py:71
  192.5 6.4 %fusion.35 = f32[12,128,384]{2,1,0:T(8,128)} fusion(bf16[384,12,128]{0,2,1:T(8,128)(2,1)S(1)} %bitcast.218, f32[12,384,384]{2,1,0:T(8,128)} %get-tuple-element.40, f32[12,384]{1,0:T(8,128)S(1)} %maximum_maximum_fusion, pred[]{:T(512)S(6)} %and.136), kind=kOutput, calls=%fused_computation.53 | convolution fusion | flops 460062720 | bytes 10635265 | tf_op jit(solution)/shard_map/abhqk,bkhd->aqhd/dot_general | solution.py:71
  198.9 3.1 %fusion.32 = f32[12,128,384]{2,1,0:T(8,128)} fusion(bf16[384,12,128]{0,2,1:T(8,128)(2,1)S(1)} %bitcast.216, f32[12,384,384]{2,1,0:T(8,128)S(1)} %get-tuple-element.38, f32[12,384]{1,0:T(8,128)S(1)} %maximum_maximum_fusion, pred[]{:T(512)S(6)} %and.139), kind=kOutput, calls=%fused_computation.51 | convolution fusion | flops 460062720 | bytes 10635265 | tf_op jit(solution)/shard_map/abhqk,bkhd->aqhd/dot_general | solution.py:71
  202.0 3.1 %fusion.29 = f32[12,128,384]{2,1,0:T(8,128)} fusion(bf16[384,12,128]{0,2,1:T(8,128)(2,1)S(1)} %bitcast.215, f32[12,384,384]{2,1,0:T(8,128)S(1)} %get-tuple-element.36, f32[12,384]{1,0:T(8,128)S(1)} %maximum_maximum_fusion, pred[]{:T(512)S(6)} %and.142), kind=kOutput, calls=%fused_computation.49 | convolution fusion | flops 460062720 | bytes 10635265 | tf_op jit(solution)/shard_map/abhqk,bkhd->aqhd/dot_general | solution.py:71
  205.1 16.3 %fusion.9 = (f32[12,384]{1,0:T(8,128)S(1)}, f32[12,384]{1,0:T(8,128)S(1)}, f32[12,384]{1,0:T(8,128)S(1)}, f32[12,384]{1,0:T(8,128)S(1)}, f32[12,384]{1,0:T(8,128...) fusion(f32[12,384,384]{2,1,0:T(8,128)} %get-tuple-element.42, f32[12,384]{1,0:T(8,128)} %copy-done.7, pred[]{:T(512)S(6)} %and.133, ...), kind=kLoop, calls=%fused_computation.30 | loop fusion | flops 49512960 | bytes 49692680 | tf_op jit(solution)/shard_map/reduce_sum | solution.py:70
  221.4 0.0 copy-done.8
  221.4 0.0 copy-start.2
  221.4 0.0 copy-start.3
  221.4 0.0 copy-start.4
  221.4 5.2 %fusion.26 = f32[12,128,384]{2,1,0:T(8,128)S(1)} fusion(bf16[384,12,128]{0,2,1:T(8,128)(2,1)} %bitcast.217, f32[12,384,384]{2,1,0:T(8,128)} %get-tuple-element.34, f32[12,384]{1,0:T(8,128)S(1)} %copy-done.8, pred[]{:T(512)S(6)} %and.145), kind=kOutput, calls=%fused_computation.47 | convolution fusion | flops 460062720 | bytes 10635265 | tf_op jit(solution)/shard_map/abhqk,bkhd->aqhd/dot_general | solution.py:71
  226.7 0.2 copy-done.4
  226.9 2.5 fusion.71
  229.3 8.9 %fusion.21 = bf16[3072,384]{0,1:T(8,128)(2,1)} fusion(bf16[384,1536]{0,1:T(8,128)(2,1)S(1)} %bitcast.214, bf16[1536,3072]{1,0:T(8,128)(2,1)} %param.12), kind=kOutput, calls=%fused_computation.43 | convolution fusion | flops 3625058304 | bytes 12976128 | tf_op jit(solution)/shard_map/dot_general | solution.py:85
  238.3 0.0 reduce-scatter.2.cloned.1.call-update
  238.3 33.4 %reduce-scatter.2.cloned.1.call-done = bf16[1536,384]{0,1:T(8,128)(2,1)} async-done(((bf16[3072,384]{0,1:T(8,128)(2,1)}), bf16[1536,384]{0,1:T(8,128)(2,1)}) %reduce-scatter.2.cloned.1.call-update) | async-done | bytes 1179664 | tf_op jit(solution)/shard_map/reduce_scatter | solution.py:84
  271.7 2.5 fusion.77
  (19 shorter events, 0.1 us)
Async XLA Ops:
  6.5 1.8 copy-start.5
  6.5 265.2 %reduce-scatter.2.cloned.1.call-start = ((), (), s32[]{:S(2)}) async-start(), calls=%async_computation.1 | async-start | bytes 3538944 | tf_op jit(solution)/shard_map/reduce_scatter | solution.py:84
  10.8 17.5 %copy-start.10 = (s32[1,6]{1,0:T(1,128)S(1)}, s32[1,6]{1,0:T(1,128)}, u32[]{:S(2)}) copy-start(s32[1,6]{1,0:T(1,128)} %param.10) | copy-start | bytes 76
  10.8 74.6 %collective-permute-start.5 = (bf16[2,384,1536]{1,2,0:T(8,128)(2,1)}, bf16[2,384,1536]{1,2,0:T(8,128)(2,1)}, u32[]{:S(2)}, u32[]{:S(2)}) collective-permute-start(bf16[2,384,1536]{1,2,0:T(8,128)(2,1)} %pad_maximum_fusion), channel_id=1, source_target_pairs={{5,0},{8,1},{9,4},{12,5},{13,8},{7,2},{10,3},{11,6},{14,7},{15,10}... | collective-permute-start | bytes 7077896 | tf_op jit(solution)/shard_map/ppermute | solution.py:18
  13.6 129.1 %collective-permute-start.3 = (bf16[2,384,1536]{1,2,0:T(8,128)(2,1)}, bf16[2,384,1536]{1,2,0:T(8,128)(2,1)}, u32[]{:S(2)}, u32[]{:S(2)}) collective-permute-start(bf16[2,384,1536]{1,2,0:T(8,128)(2,1)} %pad_maximum_fusion), channel_id=1, source_target_pairs={{4,0},{5,1},{8,4},{9,5},{12,8},{13,9},{6,2},{7,3},{10,6},{11,7},{1... | collective-permute-start | bytes 7077896 | tf_op jit(solution)/shard_map/ppermute | solution.py:18
  15.5 130.2 %collective-permute-start.2 = (bf16[2,384,1536]{1,2,0:T(8,128)(2,1)}, bf16[2,384,1536]{1,2,0:T(8,128)(2,1)}, u32[]{:S(2)}, u32[]{:S(2)}) collective-permute-start(bf16[2,384,1536]{1,2,0:T(8,128)(2,1)} %pad_maximum_fusion), channel_id=1, source_target_pairs={{0,4},{1,5},{4,8},{5,9},{8,12},{9,13},{2,6},{3,7},{6,10},{7,11},{1... | collective-permute-start | bytes 7077896 | tf_op jit(solution)/shard_map/ppermute | solution.py:18
  20.1 147.7 %collective-permute-start.1 = (bf16[2,384,1536]{1,2,0:T(8,128)(2,1)}, bf16[2,384,1536]{1,2,0:T(8,128)(2,1)}, u32[]{:S(2)}, u32[]{:S(2)}) collective-permute-start(bf16[2,384,1536]{1,2,0:T(8,128)(2,1)} %pad_maximum_fusion), channel_id=1, source_target_pairs={{1,0},{4,1},{5,4},{8,5},{9,8},{12,9},{13,12},{3,2},{6,3},{7,6},{10... | collective-permute-start | bytes 7077896 | tf_op jit(solution)/shard_map/ppermute | solution.py:18
  22.0 151.6 %collective-permute-start = (bf16[2,384,1536]{1,2,0:T(8,128)(2,1)}, bf16[2,384,1536]{1,2,0:T(8,128)(2,1)}, u32[]{:S(2)}, u32[]{:S(2)}) collective-permute-start(bf16[2,384,1536]{1,2,0:T(8,128)(2,1)} %pad_maximum_fusion), channel_id=1, source_target_pairs={{0,1},{1,4},{4,5},{5,8},{8,9},{9,12},{12,13},{2,3},{3,6},{6,7},{7,... | collective-permute-start | bytes 7077896 | tf_op jit(solution)/shard_map/ppermute | solution.py:18
  85.4 95.2 %collective-permute-start.4 = (bf16[2,384,1536]{1,2,0:T(8,128)(2,1)}, bf16[2,384,1536]{1,2,0:T(8,128)(2,1)S(1)}, u32[]{:S(2)}, u32[]{:S(2)}) collective-permute-start(bf16[2,384,1536]{1,2,0:T(8,128)(2,1)} %pad_maximum_fusion), channel_id=1, source_target_pairs={{0,5},{1,8},{4,9},{5,12},{8,13},{2,7},{3,10},{6,11},{7,14},{10,15}... | collective-permute-start | bytes 7077896 | tf_op jit(solution)/shard_map/ppermute | solution.py:18
  145.7 56.2 %copy-start = (f32[12,384,384]{2,1,0:T(8,128)}, f32[12,384,384]{2,1,0:T(8,128)S(1)}, u32[]{:S(2)}) copy-start(f32[12,384,384]{2,1,0:T(8,128)S(1)} %get-tuple-element.36) | copy-start | bytes 21233668
  150.6 48.3 %copy-start.1 = (f32[12,384,384]{2,1,0:T(8,128)}, f32[12,384,384]{2,1,0:T(8,128)S(1)}, u32[]{:S(2)}) copy-start(f32[12,384,384]{2,1,0:T(8,128)S(1)} %get-tuple-element.38) | copy-start | bytes 21233668
  186.0 16.0 %copy-start.7 = (f32[12,384]{1,0:T(8,128)}, f32[12,384]{1,0:T(8,128)S(1)}, u32[]{:S(2)}) copy-start(f32[12,384]{1,0:T(8,128)S(1)} %maximum_maximum_fusion) | copy-start | bytes 55300
  186.0 1.7 copy-start.6
  205.1 16.3 %copy-start.8 = (f32[12,384]{1,0:T(8,128)S(1)}, f32[12,384]{1,0:T(8,128)}, u32[]{:S(2)}) copy-start(f32[12,384]{1,0:T(8,128)} %copy-done.7) | copy-start | bytes 55300
  221.4 5.3 %copy-start.2 = (f32[12,128,384]{2,1,0:T(8,128)S(1)}, f32[12,128,384]{2,1,0:T(8,128)}, u32[]{:S(2)}) copy-start(f32[12,128,384]{2,1,0:T(8,128)} %fusion.35) | copy-start | bytes 7077892
  221.4 5.3 %copy-start.3 = (f32[12,128,384]{2,1,0:T(8,128)S(1)}, f32[12,128,384]{2,1,0:T(8,128)}, u32[]{:S(2)}) copy-start(f32[12,128,384]{2,1,0:T(8,128)} %fusion.32) | copy-start | bytes 7077892
  221.4 5.4 %copy-start.4 = (f32[12,128,384]{2,1,0:T(8,128)S(1)}, f32[12,128,384]{2,1,0:T(8,128)}, u32[]{:S(2)}) copy-start(f32[12,128,384]{2,1,0:T(8,128)} %fusion.29) | copy-start | bytes 7077892
  238.3 33.5 %copy-start.9 = (f32[1536]{0:T(1024)S(1)}, f32[1536]{0:T(1024)}, u32[]{:S(2)}) copy-start(f32[1536]{0:T(1024)} %param.13) | copy-start | bytes 18436
Sparse Core Ops, SparseCore 0:
  238.4 33.2 reduce-scatter.1
where the time goes:
time: 283 us; the launch traced here: 281 us
  waiting for transfers between devices  153 us (54%)
  matrix products  52.7 us (19%)
  other arithmetic  21.3 us (8%)
  between operations  18.7 us (7%)
  local copies, waits for them, and re-layouts  17.8 us (6%)
  starting transfers between devices  17.1 us (6%)
    ppermute x6, waiting for transfers between devices, shifted(): return lax.ppermute(block, axis, route)  120 us
    reduce_scatter x1, waiting for transfers between devices, local(): lax.psum_scatter(lax.dot_general(out_weight, attention, (((0,), (1,)), ((...  33.4 us
    dot_general x7, matrix products, local(): jnp.einsum('abhqk,bkhd->aqhd', weights.astype(jnp.bfloat16), value_tiles,...  26.8 us
    ppermute x6, starting transfers between devices, shifted(): return lax.ppermute(block, axis, route)  17.1 us
    dot_general x7, matrix products, tile_scores(): jnp.einsum('aqhd,bkhd->abhqk', query_tiles, key_tiles, preferred_element_...  17 us
    reduce_sum x1, other arithmetic, local(): compute_total = compute_total + jnp.sum(weights, axis=(1, 4))  16.3 us
    slice x5, local copies, waits for them, and re-layouts, local(): value_tiles = fetched[1].reshape(tiles_here, tile_rows, heads_here, HD)  12.1 us
    dot_general x1, matrix products, local(): lax.dot_general(out_weight, attention, (((0,), (1,)), ((), ())), preferre...  8.94 us
  transfers between devices with their start and end apart: 7, of which 4 were waited for; matrix products, arithmetic and copies ran while one was open for 10% of the time, Pallas kernels for 0%

commit v1 on v0

v1 whole, which is shorter than its diff:
```python
import functools
import math

import jax
import jax.numpy as jnp
from jax import lax
from jax.experimental import pallas as pl
from jax.experimental.pallas import tpu as pltpu
from jax.sharding import PartitionSpec as P

HD = 128
LOG2E = 1.4426950408889634
FAR = 1e30
ATTEND_BYTES = 16 * 2**20
SHARES = (4, 4, 4)
SMEM_SPEC = pl.BlockSpec(memory_space=pltpu.SMEM)
VMEM_SPEC = pl.BlockSpec(memory_space=pltpu.VMEM)
HBM_SPEC = pl.BlockSpec(memory_space=pltpu.HBM)
BRIEF = pl.CostEstimate(flops=1, bytes_accessed=1, transcendentals=0)


def head_chunks(heads):
    whole = sum(SHARES)
    edges = sorted({(sum(SHARES[:i]) * heads) // whole for i in range(len(SHARES) + 1)})
    return [(low, high - low) for low, high in zip(edges[:-1], edges[1:])]


def pairing(length, first):
    pairs = [(i, i + 1) for i in range(first, length - 1, 2)]
    return pairs + [(b, a) for a, b in pairs]


def ring(length, distance):
    return [(i, (i + distance) % length) for i in range(length)]


def other_core(block):
    return lax.ppermute(block, "sub", [(0, 1), (1, 0)])


def to_neighbours(block):
    length = lax.axis_size("seq")
    return [lax.ppermute(block, "seq", pairing(length, start)) for start in (0, 1)]


def after(value, *earlier):
    return lax.optimization_barrier((value, *earlier))[0]


def pack_kernel(cuts, place_ref, *refs):
    operands, refs = refs[: cuts[0]], refs[cuts[0] :]
    outputs, sems = refs[:-1], refs[-1]
    copies = []
    for out, runs in zip(outputs, cuts[1]):
        at = 0
        for index, row, column, depth, width in runs:
            if isinstance(column, tuple):
                column = pl.multiple_of(place_ref[column[0]], HD)
            source = operands[index].at[row : row + depth, pl.ds(column, width)]
            copies.append(pltpu.make_async_copy(source, out.at[:, at : at + width], sems.at[len(copies)]))
            at += width
    for copy in copies:
        copy.start()
    for copy in copies:
        copy.wait()


def pack(places, operands, cuts):
    shapes = [
        jax.ShapeDtypeStruct((runs[0][3], sum(run[4] for run in runs)), jnp.bfloat16) for runs in cuts
    ]
    return pl.pallas_call(
        functools.partial(pack_kernel, (len(operands), cuts)),
        in_specs=[SMEM_SPEC] + [HBM_SPEC] * len(operands),
        out_specs=[VMEM_SPEC] * len(shapes),
        out_shape=shapes,
        scratch_shapes=[pltpu.SemaphoreType.DMA((sum(len(runs) for runs in cuts),))],
        cost_estimate=BRIEF,
    )(places, *operands)


def attention_kernel(count, columns, base, merge, tiles_ref, list_ref, live_ref, *refs):
    arrays = max(index for index, _ in columns) + 1
    sources = (len(columns) - 1) // 2
    operands, refs = refs[:arrays], refs[arrays:]
    if merge:
        prior_ref, mass_ref, out = refs
    else:
        out, mass_ref = refs
    scale = LOG2E / math.sqrt(HD)
    live = live_ref[0]

    def included(tile):
        found = False
        for j in range(list_ref.shape[1]):
            found = found | ((list_ref[0, j] == tile) & (j < live))
        return found & (tile >= 0)

    flags = [included(tiles_ref[base + s]) for s in range(sources)]

    def cols(head, first=0):
        return slice(first + head * HD, first + (head + 1) * HD)

    def held(i, head):
        index, first = columns[i]
        return operands[index][:, cols(head, first)]

    def scores(head):
        query = held(0, head)
        return [
            lax.dot_general(
                held(1 + 2 * s, head), query, (((1,), (1,)), ((), ())), preferred_element_type=jnp.float32
            )
            for s in range(sources)
        ]

    def finish(head, logits):
        peak = mass_ref[head : head + 1, :] if merge else None
        for s in range(sources):
            top = jnp.max(logits[s], axis=0, keepdims=True) * scale
            if base + s:
                top = jnp.where(flags[s], top, -FAR)
            peak = top if peak is None else jnp.maximum(peak, top)
        accum = total = None
        for s in range(sources):
            shift = jnp.where(flags[s], peak, FAR) if base + s else peak
            weights = jnp.exp2(logits[s] * scale - shift)
            sum_here = jnp.sum(weights, axis=0, keepdims=True)
            term = lax.dot_general(
                held(2 + 2 * s, head),
                weights.astype(jnp.bfloat16),
                (((0,), (0,)), ((), ())),
                preferred_element_type=jnp.float32,
            )
            total = sum_here if total is None else total + sum_here
            accum = term if accum is None else accum + term
        if merge:
            share = jnp.exp2(mass_ref[head : head + 1, :] - peak)
            accum = accum + share * prior_ref[cols(head), :]
            total = total + share
            out[:, cols(head)] = jnp.transpose(accum * (1.0 / total)).astype(out.dtype)
        else:
            out[cols(head), :] = accum * (1.0 / total)
            mass_ref[head : head + 1, :] = peak + jnp.log2(total)

    logits = scores(0)
    for head in range(count):
        following = scores(head + 1) if head + 1 < count else None
        finish(head, logits)
        logits = following


def attend(count, columns, base, scalars, operands, prior=None):
    rows = operands[0].shape[0]
    merge = prior is not None
    sources = (len(columns) - 1) // 2
    whole = jax.ShapeDtypeStruct((rows, count * HD), jnp.bfloat16)
    alone = [
        jax.ShapeDtypeStruct((count * HD, rows), jnp.float32),
        jax.ShapeDtypeStruct((-(-count // 8) * 8, rows), jnp.float32),
    ]
    return pl.pallas_call(
        functools.partial(attention_kernel, count, columns, base, merge),
        in_specs=[SMEM_SPEC] * 3 + [VMEM_SPEC] * (len(operands) + (2 if merge else 0)),
        out_specs=VMEM_SPEC if merge else [VMEM_SPEC] * 2,
        out_shape=whole if merge else alone,
        compiler_params=pltpu.CompilerParams(vmem_limit_bytes=ATTEND_BYTES),
        cost_estimate=BRIEF,
    )(*scalars, *operands, *(prior or ()))


def project_kernel(parts, splits, place_ref, mine_ref, *refs):
    *refs, out = refs
    block = out.shape[1] // splits
    for j in range(splits):
        where = pl.ds(pl.multiple_of(place_ref[j] * block, HD), block)
        total = None
        at = 0
        for i, (chunks, pieces) in enumerate(parts):
            row = 0
            for chunk in refs[at : at + chunks]:
                rows = slice(row, row + chunk.shape[1])
                right = refs[at + chunks + j][rows, :] if i else mine_ref[rows, where]
                term = jnp.dot(chunk[...], right, preferred_element_type=jnp.float32)
                total = term if total is None else total + term
                row += chunk.shape[1]
            at += chunks + pieces
        out[:, where] = total


def project(places, splits, mine, parts):
    operands = [mine]
    for lefts, rights in parts:
        operands += [*lefts, *rights]
    return pl.pallas_call(
        functools.partial(project_kernel, [(len(a), len(b)) for a, b in parts], splits),
        in_specs=[SMEM_SPEC] + [VMEM_SPEC] * len(operands),
        out_specs=VMEM_SPEC,
        out_shape=jax.ShapeDtypeStruct((parts[0][0][0].shape[0], mine.shape[1]), jnp.float32),
        compiler_params=pltpu.CompilerParams(vmem_limit_bytes=ATTEND_BYTES),
        cost_estimate=BRIEF,
    )(places, *operands)


def close_kernel(splits, place_ref, gate_ref, total_ref, *refs):
    *refs, out = refs
    block = out.shape[1] // splits
    for j in range(splits):
        where = pl.ds(pl.multiple_of(place_ref[j] * block, HD), block)
        total = total_ref[:, where]
        for i in range(0, len(refs), 1 + splits):
            total = total + jnp.dot(refs[i][...], refs[i + 1 + j][...], preferred_element_type=jnp.float32)
        out[:, where] = (total * gate_ref[:, where]).astype(out.dtype)


def close(places, splits, gate, total, parts):
    operands = [gate, total]
    for left, rights in parts:
        operands += [left, *rights]
    rows, width = total.shape
    return pl.pallas_call(
        functools.partial(close_kernel, splits),
        in_specs=[SMEM_SPEC] + [VMEM_SPEC] * len(operands),
        out_specs=VMEM_SPEC,
        out_shape=jax.ShapeDtypeStruct((rows, width), jnp.bfloat16),
        compiler_params=pltpu.CompilerParams(vmem_limit_bytes=ATTEND_BYTES),
        cost_estimate=BRIEF,
    )(places, *operands)


def local(queries, keys, values, kv_list, kv_count, out_weight, gate):
    features = queries.shape[1]
    length, subs = lax.axis_size("seq"), lax.axis_size("sub")
    n_head, n_groups = lax.axis_size("head"), lax.axis_size("groups")
    z, c = lax.axis_index("seq"), lax.axis_index("sub")
    x, g = lax.axis_index("head"), lax.axis_index("groups")
    width = out_weight.shape[1] // n_head
    chunks = head_chunks(features // HD)
    last = len(chunks) - 1
    spans = [slice(first * HD, (first + count) * HD) for first, count in chunks]

    even = z + 1 - 2 * lax.rem(z, 2)
    odd = z - 1 + 2 * lax.rem(z, 2)
    tiles = []
    for place in (z, even, odd):
        inside = (place >= 0) & (place < length)
        tiles += [jnp.where(inside, place * subs + c, -1), jnp.where(inside, place * subs + 1 - c, -1)]
    scalars = (jnp.stack(tiles).astype(jnp.int32), kv_list, kv_count)

    splits = n_groups * subs
    if width % (splits * HD):
        splits = 1
    block = width // splits
    if splits > 1:
        places = [lax.rem(g + d, n_groups) * subs + s for d in range(n_groups) for s in (c, 1 - c)]
    else:
        places = [0]
    piece = places[0]
    places = jnp.stack(places).astype(jnp.int32)
    edges = [0, chunks[last][0] * HD, features]

    def cross(sent):
        return [lax.ppermute(block, "head", ring(n_head, d + 1)) for d, block in enumerate(sent)]

    def spread(got):
        if splits == 1:
            return [got]
        found = []
        for e in range(n_groups):
            near = got if e == 0 else lax.ppermute(got, "groups", ring(n_groups, n_groups - e))
            found += [near, other_core(near)]
        return found

    def along_head(done):
        return [lax.ppermute(done, "head", ring(n_head, d)) for d in range(1, n_head)]

    starts = [lax.rem(x + d, n_head) * width + piece * block for d in range(1, n_head)]
    starts = jnp.stack([x * width, *starts]).astype(jnp.int32)

    def pair_cut(i):
        first, count = chunks[i]
        return tuple((index, 0, first * HD, keys.shape[0], count * HD) for index in (0, 1))

    def weight_cut(part, d):
        return ((2, edges[part], (d,), edges[part + 1] - edges[part], block),)

    blocks = list(pack(starts, (keys, values), (pair_cut(0),)))
    near = [to_neighbours(blocks[0])]
    sib_keys, sib_values = other_core(keys), other_core(values)
    cuts = [pair_cut(i) for i in range(1, len(chunks))]
    cuts += [weight_cut(part, d) for part in (0, 1) for d in range(1, n_head)]
    cuts.append(((2, 0, (0,), features, width),))
    packed = list(pack(starts, (keys, values, out_weight), tuple(cuts)))
    sib_keys, sib_values, packed = lax.optimization_barrier((sib_keys, sib_values, packed))
    blocks += packed[:last]
    sent, mine = packed[last:-1], packed[-1]
    near.append(to_neighbours(blocks[1]))
    crossed = [cross(sent[: n_head - 1])]

    prior = []
    for first, count in chunks:
        at = first * HD
        columns = tuple((index, at) for index in range(5))
        prior.append(attend(count, columns, 0, scalars, (queries, keys, values, sib_keys, sib_values)))
    near[0] = list(lax.optimization_barrier((near[0], prior))[0])

    crossed.append(cross(after(sent[n_head - 1 :], crossed[0])))
    mixed, moved = [], []
    for i, (first, count) in enumerate(chunks):
        fetched = []
        for part in near[i]:
            fetched += [part, other_core(part)]
        columns = [(0, first * HD)]
        for index in range(len(fetched)):
            columns += [(1 + index, 0), (1 + index, count * HD)]
        done = attend(count, tuple(columns), 2, scalars, (queries, *fetched), prior[i])
        if i + 2 < len(chunks):
            near.append(to_neighbours(after(blocks[i + 2], done, crossed[1])))
        if i + 1 < len(chunks):
            near[i + 1] = list(after(near[i + 1], done))
        mixed.append(done)
        moved.append(along_head(done))

    pieces = [[spread(got) for got in crossed[part]] for part in (0, 1)]
    parts = [(mixed, [])]
    parts += [([moved[i][d] for i in range(last)], pieces[0][d]) for d in range(n_head - 1)]
    total = project(places, splits, mine, parts)
    parts = [(moved[last][d], pieces[1][d]) for d in range(n_head - 1)]
    return close(places, splits, gate.reshape(1, width), total, parts)


def solution(mesh):
    return jax.shard_map(
        local,
        mesh=mesh,
        in_specs=(
            P(("groups", "seq", "sub"), "head"),
            P(("groups", "seq", "sub"), "head"),
            P(("groups", "seq", "sub"), "head"),
            P(("groups", "seq", "sub"), None),
            P(("groups", "seq", "sub")),
            P("head", None),
            P("head"),
        ),
        out_specs=P(("groups", "seq", "sub"), "head"),
        check_vma=False,
    )
```

time: 283 us -> 107 us (0.38)
  waiting for transfers between devices: 153 us -> 36.6 us
  matrix products: 52.7 us -> 0 us
  Pallas kernels: 0 us -> 43.2 us
  other arithmetic: 21.3 us -> 0.74 us
  between operations: 18.7 us -> 0.92 us
  local copies, waits for them, and re-layouts: 17.8 us -> 4.49 us
  starting transfers between devices: 17.1 us -> 20 us
    ppermute x6 -> x25, waiting for transfers between devices: 120 us -> 36.6 us  [the longest x6 23.4 us: to_neighbours(): lax.ppermute(block, 'seq', pairing(length, start))]
    dot_general x15 -> x0, matrix products: 52.7 us -> none  [the longest x7 26.8 us: local(): jnp.einsum('abhqk,bkhd->aqhd', weights.astype(jnp.bfloat16), value_tiles,...]
    pallas_call x0 -> x10, Pallas kernels: none -> 43.2 us  [the longest x6 24.7 us: attend(): pl.pallas_call(functools.partial(attention_kernel, count, columns, base,...]
    reduce_scatter x1 -> x0, waiting for transfers between devices: 33.4 us -> none  [local(): lax.psum_scatter(lax.dot_general(out_weight, attention, (((0,), (1,)), ((...]
    reduce_sum x1 -> x0, other arithmetic: 16.3 us -> none  [local(): compute_total = compute_total + jnp.sum(weights, axis=(1, 4))]
    slice x6 -> x0, local copies, waits for them, and re-layouts: 13.3 us -> none  [the longest x5 12.1 us: local(): value_tiles = fetched[1].reshape(tiles_here, tile_rows, heads_here, HD)]
    ppermute x6 -> x25, starting transfers between devices: 17.1 us -> 20 us  [the longest x6 8.64 us: to_neighbours(): lax.ppermute(block, 'seq', pairing(length, start))]
  transfers between devices with their start and end apart: 7 -> 25, of which waited for: 4 -> 11; matrix products, arithmetic and copies ran while one was open for 10% -> 1% of each run, Pallas kernels for 0% -> 38%
where the time goes in v1:
time: 107 us; the launch traced here: 106 us
  Pallas kernels  43.2 us (40%)
  waiting for transfers between devices  36.6 us (34%)
  starting transfers between devices  20 us (19%)
  local copies, waits for them, and re-layouts  4.49 us (4%)
    pallas_call x6, Pallas kernels, attend(): pl.pallas_call(functools.partial(attention_kernel, count, columns, base,...  24.7 us
    ppermute x6, waiting for transfers between devices, to_neighbours(): lax.ppermute(block, 'seq', pairing(length, start))  23.4 us
    pallas_call x2, Pallas kernels, pack(): pl.pallas_call(functools.partial(pack_kernel, (len(operands), cuts)), in_...  9.7 us
    ppermute x6, starting transfers between devices, to_neighbours(): lax.ppermute(block, 'seq', pairing(length, start))  8.64 us
    ppermute x12, starting transfers between devices, other_core(): return lax.ppermute(block, 'sub', [(0, 1), (1, 0)])  7.78 us
    ppermute x3, waiting for transfers between devices, along_head(): lax.ppermute(done, 'head', ring(n_head, d))  6.38 us
    pallas_call x1, Pallas kernels, project(): pl.pallas_call(functools.partial(project_kernel, [(len(a), len(b)) for a,...  5.72 us
    ppermute x12, waiting for transfers between devices, other_core(): return lax.ppermute(block, 'sub', [(0, 1), (1, 0)])  4.58 us
  transfers between devices with their start and end apart: 25, of which 11 were waited for; matrix products, arithmetic and copies ran while one was open for 1% of the time, Pallas kernels for 38%

profile of v1, /device:TPU:13, one launch (start us, length us, event | category | flops | bytes accessed | tf_op | source)
XLA Modules:
  0.0 106.0 jit_solution(14735133241124179969)
XLA Ops:
  0.0 0.7 collective-permute-start
  0.7 0.7 pad_add_fusion.1.place_ref
  1.3 2.7 %shard_map.74 = bf16[384,1024]{1,0:T(8,128)(2,1)} custom-call(s32[2]{0:T(128)} %pad_add_fusion.1.place_ref, bf16[384,1536]{1,0:T(8,128)(2,1)} %refs_1_.9, bf16[384,1536]{1,0:T(8,128)(2,1)} %refs_2_.7), custom_call_target="tpu_custom_call" | custom-call | flops 1 | bytes 1 | tf_op jit(solution)/shard_map/pallas_call | solution.py:72
  4.1 0.0 copy-start
  4.1 0.2 collective-permute-start.2
  4.3 4.3 %collective-permute-start.3 = (bf16[384,1024]{1,0:T(8,128)(2,1)}, bf16[384,1024]{1,0:T(8,128)(2,1)}, u32[]{:S(2)}, u32[]{:S(2)}) collective-permute-start(bf16[384,1024]{1,0:T(8,128)(2,1)} %shard_map.74), channel_id=1, source_target_pairs={{4,8},{8,4},{5,9},{9,5},{6,10},{10,6},{7,11},{11,7},{20,24},{24,20... | collective-permute-start | bytes 2359304 | tf_op jit(solution)/shard_map/ppermute | solution.py:43
  8.7 7.0 %shard_map.73 = (bf16[384,1024]{1,0:T(8,128)(2,1)}, bf16[384,1024]{1,0:T(8,128)(2,1)}, bf16[1024,384]{1,0:T(8,128)(2,1)}, bf16[512,384]{1,0:T(8,128)(2,1)}, bf16[1536,1536]{1,0:T(8,128)(2,1)}) custom-call(s32[2]{0:T(128)} %pad_add_fusion.1.place_ref, bf16[384,1536]{1,0:T(8,128)(2,1)} %refs_1_.9, bf16[384,1536]{1,0:T(8,128)(2,1)} %refs_2_.7, ...), custom_call_target="tpu_custom_call" | custom-call | flops 1 | bytes 1 | tf_op jit(solution)/shard_map/pallas_call | solution.py:72
  15.7 1.3 %collective-permute-start.10 = (bf16[1024,384]{1,0:T(8,128)(2,1)}, bf16[1024,384]{1,0:T(8,128)(2,1)}, u32[]{:S(2)}, u32[]{:S(2)}) collective-permute-start(bf16[1024,384]{1,0:T(8,128)(2,1)} %get-tuple-element.52), channel_id=1, source_target_pairs={{0,2},{2,0},{1,3},{3,1},{4,6},{6,4},{5,7},{7,5},{8,10},{10,8},{9,1... | collective-permute-start | bytes 2359304 | tf_op jit(solution)/shard_map/ppermute | solution.py:263
  17.6 0.1 stack.59.tiles_ref
  17.7 3.6 %shard_map.77 = (f32[512,384]{1,0:T(8,128)S(1)}, f32[8,384]{1,0:T(8,128)S(1)}) custom-call(s32[6]{0:T(128)S(1)} %stack.59.tiles_ref, s32[1,6]{1,0:T(1,128)S(1)} %copy-done.6, s32[1]{0:T(128)S(6)} %copy.8.live_ref, bf16[384,1536]{1,0:T(8,128)(2,1)S(1)} %copy-done, bf16[384,1536]{1,0:T(8,128)(2,1)S(1)} %copy-done.1, bf16[384,1536]{1,0:T(8,128)(2,1)S(1)} %copy-done.2, ...), custom_call_target="tpu_custom_call" | custom-call | flops 1 | bytes 1 | tf_op jit(solution)/shard_map/pallas_call | solution.py:162
  21.3 3.5 %shard_map.76 = (f32[512,384]{1,0:T(8,128)S(1)}, f32[8,384]{1,0:T(8,128)S(1)}) custom-call(s32[6]{0:T(128)S(1)} %stack.59.tiles_ref, s32[1,6]{1,0:T(1,128)S(1)} %copy-done.6, s32[1]{0:T(128)S(6)} %copy.8.live_ref, bf16[384,1536]{1,0:T(8,128)(2,1)S(1)} %copy-done, bf16[384,1536]{1,0:T(8,128)(2,1)S(1)} %copy-done.1, bf16[384,1536]{1,0:T(8,128)(2,1)S(1)} %copy-done.2, ...), custom_call_target="tpu_custom_call" | custom-call | flops 1 | bytes 1 | tf_op jit(solution)/shard_map/pallas_call | solution.py:162
  24.9 3.6 %shard_map.75 = (f32[512,384]{1,0:T(8,128)S(1)}, f32[8,384]{1,0:T(8,128)S(1)}) custom-call(s32[6]{0:T(128)S(1)} %stack.59.tiles_ref, s32[1,6]{1,0:T(1,128)S(1)} %copy-done.6, s32[1]{0:T(128)S(6)} %copy.8.live_ref, bf16[384,1536]{1,0:T(8,128)(2,1)S(1)} %copy-done, bf16[384,1536]{1,0:T(8,128)(2,1)S(1)} %copy-done.1, bf16[384,1536]{1,0:T(8,128)(2,1)S(1)} %copy-done.2, ...), custom_call_target="tpu_custom_call" | custom-call | flops 1 | bytes 1 | tf_op jit(solution)/shard_map/pallas_call | solution.py:162
  28.6 1.4 %collective-permute-start.4 = (bf16[384,1024]{1,0:T(8,128)(2,1)}, bf16[384,1024]{1,0:T(8,128)(2,1)S(1)}, u32[]{:S(2)}, u32[]{:S(2)}) collective-permute-start(bf16[384,1024]{1,0:T(8,128)(2,1)} %collective-permute-done.2.refs_1_), channel_id=1, source_target_pairs={{0,1},{1,0},{2,3},{3,2},{4,5},{5,4},{6,7},{7,6},{8,9},{9,8},{10,11... | collective-permute-start | bytes 2359304 | tf_op jit(solution)/shard_map/ppermute | solution.py:38
  30.0 0.1 collective-permute-start.5
  30.1 1.9 %collective-permute-start.7 = (bf16[384,1024]{1,0:T(8,128)(2,1)S(1)}, bf16[384,1024]{1,0:T(8,128)(2,1)S(1)}, u32[]{:S(2)}, u32[]{:S(2)}) collective-permute-start(bf16[384,1024]{1,0:T(8,128)(2,1)S(1)} %copy-done.9), channel_id=1, source_target_pairs={{4,8},{8,4},{5,9},{9,5},{6,10},{10,6},{7,11},{11,7},{20,24},{24,20... | collective-permute-start | bytes 2359304 | tf_op jit(solution)/shard_map/ppermute | solution.py:43
  32.0 2.1 %collective-permute-done.10.refs_5_ = bf16[1024,384]{1,0:T(8,128)(2,1)} collective-permute-done((bf16[1024,384]{1,0:T(8,128)(2,1)}, bf16[1024,384]{1,0:T(8,128)(2,1)}, u32[]{:S(2)}, u32[]{:S(2)}) %collective-permute-start.10) | collective-permute-done | bytes 786464 | tf_op jit(solution)/shard_map/ppermute | solution.py:263
  34.0 1.2 %collective-permute-start.11 = (bf16[512,384]{1,0:T(8,128)(2,1)S(1)}, bf16[512,384]{1,0:T(8,128)(2,1)}, u32[]{:S(2)}, u32[]{:S(2)}) collective-permute-start(bf16[512,384]{1,0:T(8,128)(2,1)S(1)} %copy-done.10), channel_id=1, source_target_pairs={{0,2},{2,0},{1,3},{3,1},{4,6},{6,4},{5,7},{7,5},{8,10},{10,8},{9,1... | collective-permute-start | bytes 1179656 | tf_op jit(solution)/shard_map/ppermute | solution.py:263
  35.3 5.2 %shard_map.78.refs_0_ = bf16[384,512]{1,0:T(8,128)(2,1)S(1)} custom-call(s32[6]{0:T(128)S(1)} %stack.59.tiles_ref, s32[1,6]{1,0:T(1,128)S(1)} %copy-done.6, s32[1]{0:T(128)S(6)} %copy.8.live_ref, bf16[384,1536]{1,0:T(8,128)(2,1)S(1)} %copy-done, bf16[384,1024]{1,0:T(8,128)(2,1)} %collective-permute-done.2.refs_1_, ...), custom_call_target="tpu_custom_call" | custom-call | flops 1 | bytes 1 | tf_op jit(solution)/shard_map/pallas_call | solution.py:162
  40.4 8.3 %collective-permute-done.6.refs_1_ = bf16[384,1024]{1,0:T(8,128)(2,1)S(1)} collective-permute-done((bf16[384,1024]{1,0:T(8,128)(2,1)S(1)}, bf16[384,1024]{1,0:T(8,128)(2,1)S(1)}, u32[]{:S(2)}, u32[]{:S(2)}) %collective-permute-start.6) | collective-permute-done | bytes 786464 | tf_op jit(solution)/shard_map/ppermute | solution.py:43
  48.7 1.9 %collective-permute-done.7.refs_3_ = bf16[384,1024]{1,0:T(8,128)(2,1)S(1)} collective-permute-done((bf16[384,1024]{1,0:T(8,128)(2,1)S(1)}, bf16[384,1024]{1,0:T(8,128)(2,1)S(1)}, u32[]{:S(2)}, u32[]{:S(2)}) %collective-permute-start.7) | collective-permute-done | bytes 786464 | tf_op jit(solution)/shard_map/ppermute | solution.py:43
  50.6 1.3 %collective-permute-start.8 = (bf16[384,1024]{1,0:T(8,128)(2,1)S(1)}, bf16[384,1024]{1,0:T(8,128)(2,1)S(1)}, u32[]{:S(2)}, u32[]{:S(2)}) collective-permute-start(bf16[384,1024]{1,0:T(8,128)(2,1)S(1)} %collective-permute-done.6.refs_1_), channel_id=1, source_target_pairs={{0,1},{1,0},{2,3},{3,2},{4,5},{5,4},{6,7},{7,6},{8,9},{9,8},{10,11... | collective-permute-start | bytes 2359304 | tf_op jit(solution)/shard_map/ppermute | solution.py:38
  51.9 0.1 collective-permute-start.12
  52.0 2.1 %collective-permute-start.13 = (bf16[384,1024]{1,0:T(8,128)(2,1)S(1)}, bf16[384,1024]{1,0:T(8,128)(2,1)S(1)}, u32[]{:S(2)}, u32[]{:S(2)}) collective-permute-start(bf16[384,1024]{1,0:T(8,128)(2,1)S(1)} %copy-done.8), channel_id=1, source_target_pairs={{4,8},{8,4},{5,9},{9,5},{6,10},{10,6},{7,11},{11,7},{20,24},{24,20... | collective-permute-start | bytes 2359304 | tf_op jit(solution)/shard_map/ppermute | solution.py:43
  54.1 0.3 collective-permute-start.19
  54.4 0.5 collective-permute-done.9.refs_4_
  54.9 4.4 %shard_map.79.refs_1_ = bf16[384,512]{1,0:T(8,128)(2,1)S(1)} custom-call(s32[6]{0:T(128)S(1)} %stack.59.tiles_ref, s32[1,6]{1,0:T(1,128)S(1)} %copy-done.6, s32[1]{0:T(128)S(6)} %copy.8.live_ref, bf16[384,1536]{1,0:T(8,128)(2,1)S(1)} %copy-done, bf16[384,1024]{1,0:T(8,128)(2,1)S(1)} %collective-permute-done.6.refs_1_, ...), custom_call_target="tpu_custom_call" | custom-call | flops 1 | bytes 1 | tf_op jit(solution)/shard_map/pallas_call | solution.py:162
  59.3 11.3 %collective-permute-done.12.refs_1_ = bf16[384,1024]{1,0:T(8,128)(2,1)S(1)} collective-permute-done((bf16[384,1024]{1,0:T(8,128)(2,1)S(1)}, bf16[384,1024]{1,0:T(8,128)(2,1)S(1)}, u32[]{:S(2)}, u32[]{:S(2)}) %collective-permute-start.12) | collective-permute-done | bytes 786464 | tf_op jit(solution)/shard_map/ppermute | solution.py:43
  70.7 1.9 %collective-permute-done.13.refs_3_ = bf16[384,1024]{1,0:T(8,128)(2,1)S(1)} collective-permute-done((bf16[384,1024]{1,0:T(8,128)(2,1)S(1)}, bf16[384,1024]{1,0:T(8,128)(2,1)S(1)}, u32[]{:S(2)}, u32[]{:S(2)}) %collective-permute-start.13) | collective-permute-done | bytes 786464 | tf_op jit(solution)/shard_map/ppermute | solution.py:43
  72.6 1.3 %collective-permute-start.14 = (bf16[384,1024]{1,0:T(8,128)(2,1)S(1)}, bf16[384,1024]{1,0:T(8,128)(2,1)S(1)}, u32[]{:S(2)}, u32[]{:S(2)}) collective-permute-start(bf16[384,1024]{1,0:T(8,128)(2,1)S(1)} %collective-permute-done.12.refs_1_), channel_id=1, source_target_pairs={{0,1},{1,0},{2,3},{3,2},{4,5},{5,4},{6,7},{7,6},{8,9},{9,8},{10,11... | collective-permute-start | bytes 2359304 | tf_op jit(solution)/shard_map/ppermute | solution.py:38
  73.8 0.5 collective-permute-start.18
  74.4 0.2 collective-permute-start.16
  74.6 0.3 collective-permute-start.20
  74.9 0.9 collective-permute-done.14.refs_2_
  75.8 0.2 collective-permute-start.23
  76.0 3.1 %collective-permute-done.15.refs_4_ = bf16[384,1024]{1,0:T(8,128)(2,1)S(1)} collective-permute-done((bf16[384,1024]{1,0:T(8,128)(2,1)S(1)}, bf16[384,1024]{1,0:T(8,128)(2,1)S(1)}, u32[]{:S(2)}, u32[]{:S(2)}) %collective-permute-start.15) | collective-permute-done | bytes 786464 | tf_op jit(solution)/shard_map/ppermute | solution.py:38
  79.1 4.4 %shard_map.80.refs_2_ = bf16[384,512]{1,0:T(8,128)(2,1)S(1)} custom-call(s32[6]{0:T(128)S(1)} %stack.59.tiles_ref, s32[1,6]{1,0:T(1,128)S(1)} %copy-done.6, s32[1]{0:T(128)S(6)} %copy.8.live_ref, bf16[384,1536]{1,0:T(8,128)(2,1)S(1)} %copy-done, bf16[384,1024]{1,0:T(8,128)(2,1)S(1)} %collective-permute-done.12.refs_1_, ...), custom_call_target="tpu_custom_call" | custom-call | flops 1 | bytes 1 | tf_op jit(solution)/shard_map/pallas_call | solution.py:162
  83.5 1.7 %collective-permute-done.16.refs_3_ = bf16[384,512]{1,0:T(8,128)(2,1)S(1)} collective-permute-done((bf16[384,512]{1,0:T(8,128)(2,1)S(1)}, bf16[384,512]{1,0:T(8,128)(2,1)S(1)}, u32[]{:S(2)}, u32[]{:S(2)}) %collective-permute-start.16) | collective-permute-done | bytes 393248 | tf_op jit(solution)/shard_map/ppermute | solution.py:275
  85.2 1.1 %collective-permute-start.22 = (bf16[512,384]{1,0:T(8,128)(2,1)}, bf16[512,384]{1,0:T(8,128)(2,1)S(1)}, u32[]{:S(2)}, u32[]{:S(2)}) collective-permute-start(bf16[512,384]{1,0:T(8,128)(2,1)} %collective-permute-done.11.refs_1_), channel_id=1, source_target_pairs={{0,1},{1,0},{2,3},{3,2},{4,5},{5,4},{6,7},{7,6},{8,9},{9,8},{10,11... | collective-permute-start | bytes 1179656 | tf_op jit(solution)/shard_map/ppermute | solution.py:38
  86.3 0.1 collective-permute-done.23.refs_3_
  86.4 1.2 %collective-permute-start.24 = (bf16[512,384]{1,0:T(8,128)(2,1)}, bf16[512,384]{1,0:T(8,128)(2,1)S(1)}, u32[]{:S(2)}, u32[]{:S(2)}) collective-permute-start(bf16[512,384]{1,0:T(8,128)(2,1)} %collective-permute-done.23.refs_3_), channel_id=1, source_target_pairs={{0,1},{1,0},{2,3},{3,2},{4,5},{5,4},{6,7},{7,6},{8,9},{9,8},{10,11... | collective-permute-start | bytes 1179656 | tf_op jit(solution)/shard_map/ppermute | solution.py:38
  87.6 0.9 copy-done.4
  88.5 0.4 collective-permute-start.21
  88.9 0.1 pad_add_fusion.place_ref
  88.9 4.7 %collective-permute-done.17.refs_4_ = bf16[384,512]{1,0:T(8,128)(2,1)} collective-permute-done((bf16[384,512]{1,0:T(8,128)(2,1)S(1)}, bf16[384,512]{1,0:T(8,128)(2,1)}, u32[]{:S(2)}, u32[]{:S(2)}) %collective-permute-start.17) | collective-permute-done | bytes 393248 | tf_op jit(solution)/shard_map/ppermute | solution.py:275
  93.6 2.3 %copy-done.3 = bf16[1536,1536]{1,0:T(8,128)(2,1)S(1)} copy-done((bf16[1536,1536]{1,0:T(8,128)(2,1)S(1)}, bf16[1536,1536]{1,0:T(8,128)(2,1)}, u32[]{:S(2)}) %copy-start.3) | copy-done | bytes 4718616
  96.0 1.1 %copy-done.5 = bf16[1024,384]{1,0:T(8,128)(2,1)S(1)} copy-done((bf16[1024,384]{1,0:T(8,128)(2,1)S(1)}, bf16[1024,384]{1,0:T(8,128)(2,1)}, u32[]{:S(2)}) %copy-start.5) | copy-done | bytes 786456
  97.1 5.7 %shard_map.81.total_ref = f32[384,1536]{1,0:T(8,128)S(1)} custom-call(s32[4]{0:T(128)S(1)} %pad_add_fusion.place_ref, bf16[1536,1536]{1,0:T(8,128)(2,1)S(1)} %copy-done.3, bf16[384,512]{1,0:T(8,128)(2,1)S(1)} %shard_map.78.refs_0_, bf16[384,512]{1,0:T(8,128)(2,1)S(1)} %shard_map.79.refs_1_, bf16[384,512]{1,0:T(8,128)(2,1)S(1)} %shard_map.80.refs_2_, ...), custom_call_target="tpu_custom_call" | custom-call | flops 1 | bytes 1 | tf_op jit(solution)/shard_map/pallas_call | solution.py:195
  102.9 3.1 %shard_map.82 = bf16[384,1536]{1,0:T(8,128)(2,1)} custom-call(s32[4]{0:T(128)S(1)} %pad_add_fusion.place_ref, f32[1,1536]{1,0:T(1,128)S(1)} %reshape.3.gate_ref, f32[384,1536]{1,0:T(8,128)S(1)} %shard_map.81.total_ref, bf16[384,512]{1,0:T(8,128)(2,1)S(1)} %collective-permute-done.21.refs_0_, bf16[512,384]{1,0:T(8,128)(2,1)} %collective-permute-done.11.refs_1_, ...), custom_call_target="tpu_custom_call" | custom-call | flops 1 | bytes 1 | tf_op jit(solution)/shard_map/pallas_call | solution.py:221
  (38 shorter events, 0.1 us)
Async XLA Ops:
  0.0 15.7 %collective-permute-start = (bf16[384,1536]{1,0:T(8,128)(2,1)}, bf16[384,1536]{1,0:T(8,128)(2,1)}, u32[]{:S(2)}, u32[]{:S(2)}) collective-permute-start(bf16[384,1536]{1,0:T(8,128)(2,1)} %refs_1_.9), channel_id=1, source_target_pairs={{0,1},{1,0},{2,3},{3,2},{4,5},{5,4},{6,7},{7,6},{8,9},{9,8},{10,11... | collective-permute-start | bytes 3538952 | tf_op jit(solution)/shard_map/ppermute | solution.py:38
  0.7 15.0 %collective-permute-start.1 = (bf16[384,1536]{1,0:T(8,128)(2,1)}, bf16[384,1536]{1,0:T(8,128)(2,1)}, u32[]{:S(2)}, u32[]{:S(2)}) collective-permute-start(bf16[384,1536]{1,0:T(8,128)(2,1)} %refs_2_.7), channel_id=1, source_target_pairs={{0,1},{1,0},{2,3},{3,2},{4,5},{5,4},{6,7},{7,6},{8,9},{9,8},{10,11... | collective-permute-start | bytes 3538952 | tf_op jit(solution)/shard_map/ppermute | solution.py:38
  4.1 13.7 %copy-start = (bf16[384,1536]{1,0:T(8,128)(2,1)S(1)}, bf16[384,1536]{1,0:T(8,128)(2,1)}, u32[]{:S(2)}) copy-start(bf16[384,1536]{1,0:T(8,128)(2,1)} %refs_0_.15) | copy-start | bytes 3538948
  4.1 13.6 %copy-start.1 = (bf16[384,1536]{1,0:T(8,128)(2,1)S(1)}, bf16[384,1536]{1,0:T(8,128)(2,1)}, u32[]{:S(2)}) copy-start(bf16[384,1536]{1,0:T(8,128)(2,1)} %refs_1_.9) | copy-start | bytes 3538948
  4.1 13.6 %copy-start.2 = (bf16[384,1536]{1,0:T(8,128)(2,1)S(1)}, bf16[384,1536]{1,0:T(8,128)(2,1)}, u32[]{:S(2)}) copy-start(bf16[384,1536]{1,0:T(8,128)(2,1)} %refs_2_.7) | copy-start | bytes 3538948
  4.1 13.6 %copy-start.6 = (s32[1,6]{1,0:T(1,128)S(1)}, s32[1,6]{1,0:T(1,128)}, u32[]{:S(2)}) copy-start(s32[1,6]{1,0:T(1,128)} %list_ref.11) | copy-start | bytes 76
  4.1 24.4 %collective-permute-start.2 = (bf16[384,1024]{1,0:T(8,128)(2,1)}, bf16[384,1024]{1,0:T(8,128)(2,1)}, u32[]{:S(2)}, u32[]{:S(2)}) collective-permute-start(bf16[384,1024]{1,0:T(8,128)(2,1)} %shard_map.74), channel_id=1, source_target_pairs={{0,4},{8,12},{4,0},{12,8},{1,5},{9,13},{5,1},{13,9},{2,6},{10,14},... | collective-permute-start | bytes 2359304 | tf_op jit(solution)/shard_map/ppermute | solution.py:43
  4.3 24.2 %collective-permute-start.3 = (bf16[384,1024]{1,0:T(8,128)(2,1)}, bf16[384,1024]{1,0:T(8,128)(2,1)}, u32[]{:S(2)}, u32[]{:S(2)}) collective-permute-start(bf16[384,1024]{1,0:T(8,128)(2,1)} %shard_map.74), channel_id=1, source_target_pairs={{4,8},{8,4},{5,9},{9,5},{6,10},{10,6},{7,11},{11,7},{20,24},{24,20... | collective-permute-start | bytes 2359304 | tf_op jit(solution)/shard_map/ppermute | solution.py:43
  15.7 18.3 %collective-permute-start.10 = (bf16[1024,384]{1,0:T(8,128)(2,1)}, bf16[1024,384]{1,0:T(8,128)(2,1)}, u32[]{:S(2)}, u32[]{:S(2)}) collective-permute-start(bf16[1024,384]{1,0:T(8,128)(2,1)} %get-tuple-element.52), channel_id=1, source_target_pairs={{0,2},{2,0},{1,3},{3,1},{4,6},{6,4},{5,7},{7,5},{8,10},{10,8},{9,1... | collective-permute-start | bytes 2359304 | tf_op jit(solution)/shard_map/ppermute | solution.py:263
  24.9 5.2 %copy-start.9 = (bf16[384,1024]{1,0:T(8,128)(2,1)S(1)}, bf16[384,1024]{1,0:T(8,128)(2,1)}, u32[]{:S(2)}) copy-start(bf16[384,1024]{1,0:T(8,128)(2,1)} %get-tuple-element.47) | copy-start | bytes 2359300
  24.9 9.2 %copy-start.10 = (bf16[512,384]{1,0:T(8,128)(2,1)S(1)}, bf16[512,384]{1,0:T(8,128)(2,1)}, u32[]{:S(2)}) copy-start(bf16[512,384]{1,0:T(8,128)(2,1)} %get-tuple-element.53) | copy-start | bytes 1179652
  28.5 23.4 %copy-start.8 = (bf16[384,1024]{1,0:T(8,128)(2,1)S(1)}, bf16[384,1024]{1,0:T(8,128)(2,1)}, u32[]{:S(2)}) copy-start(bf16[384,1024]{1,0:T(8,128)(2,1)} %get-tuple-element.54) | copy-start | bytes 2359300
  28.6 6.7 %collective-permute-start.4 = (bf16[384,1024]{1,0:T(8,128)(2,1)}, bf16[384,1024]{1,0:T(8,128)(2,1)S(1)}, u32[]{:S(2)}, u32[]{:S(2)}) collective-permute-start(bf16[384,1024]{1,0:T(8,128)(2,1)} %collective-permute-done.2.refs_1_), channel_id=1, source_target_pairs={{0,1},{1,0},{2,3},{3,2},{4,5},{5,4},{6,7},{7,6},{8,9},{9,8},{10,11... | collective-permute-start | bytes 2359304 | tf_op jit(solution)/shard_map/ppermute | solution.py:38
  30.0 5.3 %collective-permute-start.5 = (bf16[384,1024]{1,0:T(8,128)(2,1)}, bf16[384,1024]{1,0:T(8,128)(2,1)S(1)}, u32[]{:S(2)}, u32[]{:S(2)}) collective-permute-start(bf16[384,1024]{1,0:T(8,128)(2,1)} %collective-permute-done.3.refs_3_), channel_id=1, source_target_pairs={{0,1},{1,0},{2,3},{3,2},{4,5},{5,4},{6,7},{7,6},{8,9},{9,8},{10,11... | collective-permute-start | bytes 2359304 | tf_op jit(solution)/shard_map/ppermute | solution.py:38
  30.1 18.7 %collective-permute-start.6 = (bf16[384,1024]{1,0:T(8,128)(2,1)S(1)}, bf16[384,1024]{1,0:T(8,128)(2,1)S(1)}, u32[]{:S(2)}, u32[]{:S(2)}) collective-permute-start(bf16[384,1024]{1,0:T(8,128)(2,1)S(1)} %copy-done.9), channel_id=1, source_target_pairs={{0,4},{8,12},{4,0},{12,8},{1,5},{9,13},{5,1},{13,9},{2,6},{10,14},... | collective-permute-start | bytes 2359304 | tf_op jit(solution)/shard_map/ppermute | solution.py:43
  30.1 20.6 %collective-permute-start.7 = (bf16[384,1024]{1,0:T(8,128)(2,1)S(1)}, bf16[384,1024]{1,0:T(8,128)(2,1)S(1)}, u32[]{:S(2)}, u32[]{:S(2)}) collective-permute-start(bf16[384,1024]{1,0:T(8,128)(2,1)S(1)} %copy-done.9), channel_id=1, source_target_pairs={{4,8},{8,4},{5,9},{9,5},{6,10},{10,6},{7,11},{11,7},{20,24},{24,20... | collective-permute-start | bytes 2359304 | tf_op jit(solution)/shard_map/ppermute | solution.py:43
  34.0 17.9 %collective-permute-start.11 = (bf16[512,384]{1,0:T(8,128)(2,1)S(1)}, bf16[512,384]{1,0:T(8,128)(2,1)}, u32[]{:S(2)}, u32[]{:S(2)}) collective-permute-start(bf16[512,384]{1,0:T(8,128)(2,1)S(1)} %copy-done.10), channel_id=1, source_target_pairs={{0,2},{2,0},{1,3},{3,1},{4,6},{6,4},{5,7},{7,5},{8,10},{10,8},{9,1... | collective-permute-start | bytes 1179656 | tf_op jit(solution)/shard_map/ppermute | solution.py:263
  50.6 3.8 %collective-permute-start.8 = (bf16[384,1024]{1,0:T(8,128)(2,1)S(1)}, bf16[384,1024]{1,0:T(8,128)(2,1)S(1)}, u32[]{:S(2)}, u32[]{:S(2)}) collective-permute-start(bf16[384,1024]{1,0:T(8,128)(2,1)S(1)} %collective-permute-done.6.refs_1_), channel_id=1, source_target_pairs={{0,1},{1,0},{2,3},{3,2},{4,5},{5,4},{6,7},{7,6},{8,9},{9,8},{10,11... | collective-permute-start | bytes 2359304 | tf_op jit(solution)/shard_map/ppermute | solution.py:38
  51.9 3.0 %collective-permute-start.9 = (bf16[384,1024]{1,0:T(8,128)(2,1)S(1)}, bf16[384,1024]{1,0:T(8,128)(2,1)S(1)}, u32[]{:S(2)}, u32[]{:S(2)}) collective-permute-start(bf16[384,1024]{1,0:T(8,128)(2,1)S(1)} %collective-permute-done.7.refs_3_), channel_id=1, source_target_pairs={{0,1},{1,0},{2,3},{3,2},{4,5},{5,4},{6,7},{7,6},{8,9},{9,8},{10,11... | collective-permute-start | bytes 2359304 | tf_op jit(solution)/shard_map/ppermute | solution.py:38
  51.9 18.7 %collective-permute-start.12 = (bf16[384,1024]{1,0:T(8,128)(2,1)S(1)}, bf16[384,1024]{1,0:T(8,128)(2,1)S(1)}, u32[]{:S(2)}, u32[]{:S(2)}) collective-permute-start(bf16[384,1024]{1,0:T(8,128)(2,1)S(1)} %copy-done.8), channel_id=1, source_target_pairs={{0,4},{8,12},{4,0},{12,8},{1,5},{9,13},{5,1},{13,9},{2,6},{10,14},... | collective-permute-start | bytes 2359304 | tf_op jit(solution)/shard_map/ppermute | solution.py:43
  52.0 20.6 %collective-permute-start.13 = (bf16[384,1024]{1,0:T(8,128)(2,1)S(1)}, bf16[384,1024]{1,0:T(8,128)(2,1)S(1)}, u32[]{:S(2)}, u32[]{:S(2)}) collective-permute-start(bf16[384,1024]{1,0:T(8,128)(2,1)S(1)} %copy-done.8), channel_id=1, source_target_pairs={{4,8},{8,4},{5,9},{9,5},{6,10},{10,6},{7,11},{11,7},{20,24},{24,20... | collective-permute-start | bytes 2359304 | tf_op jit(solution)/shard_map/ppermute | solution.py:43
  54.1 20.5 %collective-permute-start.19 = (bf16[1024,384]{1,0:T(8,128)(2,1)}, bf16[1024,384]{1,0:T(8,128)(2,1)S(1)}, u32[]{:S(2)}, u32[]{:S(2)}) collective-permute-start(bf16[1024,384]{1,0:T(8,128)(2,1)} %collective-permute-done.10.refs_5_), channel_id=1, source_target_pairs={{0,16},{16,0},{1,17},{17,1},{2,18},{18,2},{3,19},{19,3},{4,20},{20... | collective-permute-start | bytes 2359304 | tf_op jit(solution)/shard_map/ppermute | solution.py:270
  59.3 29.5 %copy-start.7 = (f32[1536]{0:T(1024)S(1)}, f32[1536]{0:T(1024)}, u32[]{:S(2)}) copy-start(f32[1536]{0:T(1024)} %param.13) | copy-start | bytes 18436
  72.6 3.2 %collective-permute-start.14 = (bf16[384,1024]{1,0:T(8,128)(2,1)S(1)}, bf16[384,1024]{1,0:T(8,128)(2,1)S(1)}, u32[]{:S(2)}, u32[]{:S(2)}) collective-permute-start(bf16[384,1024]{1,0:T(8,128)(2,1)S(1)} %collective-permute-done.12.refs_1_), channel_id=1, source_target_pairs={{0,1},{1,0},{2,3},{3,2},{4,5},{5,4},{6,7},{7,6},{8,9},{9,8},{10,11... | collective-permute-start | bytes 2359304 | tf_op jit(solution)/shard_map/ppermute | solution.py:38
  73.8 5.3 %collective-permute-start.15 = (bf16[384,1024]{1,0:T(8,128)(2,1)S(1)}, bf16[384,1024]{1,0:T(8,128)(2,1)S(1)}, u32[]{:S(2)}, u32[]{:S(2)}) collective-permute-start(bf16[384,1024]{1,0:T(8,128)(2,1)S(1)} %collective-permute-done.13.refs_3_), channel_id=1, source_target_pairs={{0,1},{1,0},{2,3},{3,2},{4,5},{5,4},{6,7},{7,6},{8,9},{9,8},{10,11... | collective-permute-start | bytes 2359304 | tf_op jit(solution)/shard_map/ppermute | solution.py:38
  73.8 13.8 %collective-permute-start.18 = (bf16[1024,384]{1,0:T(8,128)(2,1)}, bf16[1024,384]{1,0:T(8,128)(2,1)S(1)}, u32[]{:S(2)}, u32[]{:S(2)}) collective-permute-start(bf16[1024,384]{1,0:T(8,128)(2,1)} %collective-permute-done.10.refs_5_), channel_id=1, source_target_pairs={{0,1},{1,0},{2,3},{3,2},{4,5},{5,4},{6,7},{7,6},{8,9},{9,8},{10,11... | collective-permute-start | bytes 2359304 | tf_op jit(solution)/shard_map/ppermute | solution.py:38
  74.4 10.9 %collective-permute-start.16 = (bf16[384,512]{1,0:T(8,128)(2,1)S(1)}, bf16[384,512]{1,0:T(8,128)(2,1)S(1)}, u32[]{:S(2)}, u32[]{:S(2)}) collective-permute-start(bf16[384,512]{1,0:T(8,128)(2,1)S(1)} %shard_map.78.refs_0_), channel_id=1, source_target_pairs={{0,2},{2,0},{1,3},{3,1},{4,6},{6,4},{5,7},{7,5},{8,10},{10,8},{9,1... | collective-permute-start | bytes 1179656 | tf_op jit(solution)/shard_map/ppermute | solution.py:275
  74.6 19.0 %collective-permute-start.20 = (bf16[1024,384]{1,0:T(8,128)(2,1)S(1)}, bf16[1024,384]{1,0:T(8,128)(2,1)}, u32[]{:S(2)}, u32[]{:S(2)}) collective-permute-start(bf16[1024,384]{1,0:T(8,128)(2,1)S(1)} %collective-permute-done.19.refs_7_), channel_id=1, source_target_pairs={{0,1},{1,0},{2,3},{3,2},{4,5},{5,4},{6,7},{7,6},{8,9},{9,8},{10,11... | collective-permute-start | bytes 2359304 | tf_op jit(solution)/shard_map/ppermute | solution.py:38
  75.8 10.6 %collective-permute-start.23 = (bf16[512,384]{1,0:T(8,128)(2,1)}, bf16[512,384]{1,0:T(8,128)(2,1)}, u32[]{:S(2)}, u32[]{:S(2)}) collective-permute-start(bf16[512,384]{1,0:T(8,128)(2,1)} %collective-permute-done.11.refs_1_), channel_id=1, source_target_pairs={{0,16},{16,0},{1,17},{17,1},{2,18},{18,2},{3,19},{19,3},{4,20},{20... | collective-permute-start | bytes 1179656 | tf_op jit(solution)/shard_map/ppermute | solution.py:270
  79.1 14.5 %collective-permute-start.17 = (bf16[384,512]{1,0:T(8,128)(2,1)S(1)}, bf16[384,512]{1,0:T(8,128)(2,1)}, u32[]{:S(2)}, u32[]{:S(2)}) collective-permute-start(bf16[384,512]{1,0:T(8,128)(2,1)S(1)} %shard_map.79.refs_1_), channel_id=1, source_target_pairs={{0,2},{2,0},{1,3},{3,1},{4,6},{6,4},{5,7},{7,5},{8,10},{10,8},{9,1... | collective-permute-start | bytes 1179656 | tf_op jit(solution)/shard_map/ppermute | solution.py:275
  85.2 17.6 %collective-permute-start.22 = (bf16[512,384]{1,0:T(8,128)(2,1)}, bf16[512,384]{1,0:T(8,128)(2,1)S(1)}, u32[]{:S(2)}, u32[]{:S(2)}) collective-permute-start(bf16[512,384]{1,0:T(8,128)(2,1)} %collective-permute-done.11.refs_1_), channel_id=1, source_target_pairs={{0,1},{1,0},{2,3},{3,2},{4,5},{5,4},{6,7},{7,6},{8,9},{9,8},{10,11... | collective-permute-start | bytes 1179656 | tf_op jit(solution)/shard_map/ppermute | solution.py:38
  86.4 16.4 %collective-permute-start.24 = (bf16[512,384]{1,0:T(8,128)(2,1)}, bf16[512,384]{1,0:T(8,128)(2,1)S(1)}, u32[]{:S(2)}, u32[]{:S(2)}) collective-permute-start(bf16[512,384]{1,0:T(8,128)(2,1)} %collective-permute-done.23.refs_3_), channel_id=1, source_target_pairs={{0,1},{1,0},{2,3},{3,2},{4,5},{5,4},{6,7},{7,6},{8,9},{9,8},{10,11... | collective-permute-start | bytes 1179656 | tf_op jit(solution)/shard_map/ppermute | solution.py:38
  87.6 0.9 copy-start.4
  88.5 14.4 %collective-permute-start.21 = (bf16[384,512]{1,0:T(8,128)(2,1)S(1)}, bf16[384,512]{1,0:T(8,128)(2,1)S(1)}, u32[]{:S(2)}, u32[]{:S(2)}) collective-permute-start(bf16[384,512]{1,0:T(8,128)(2,1)S(1)} %shard_map.80.refs_2_), channel_id=1, source_target_pairs={{0,2},{2,0},{1,3},{3,1},{4,6},{6,4},{5,7},{7,5},{8,10},{10,8},{9,1... | collective-permute-start | bytes 1179656 | tf_op jit(solution)/shard_map/ppermute | solution.py:275
  93.6 2.3 %copy-start.3 = (bf16[1536,1536]{1,0:T(8,128)(2,1)S(1)}, bf16[1536,1536]{1,0:T(8,128)(2,1)}, u32[]{:S(2)}) copy-start(bf16[1536,1536]{1,0:T(8,128)(2,1)} %get-tuple-element.36.mine_ref) | copy-start | bytes 14155780
  96.0 1.1 %copy-start.5 = (bf16[1024,384]{1,0:T(8,128)(2,1)S(1)}, bf16[1024,384]{1,0:T(8,128)(2,1)}, u32[]{:S(2)}) copy-start(bf16[1024,384]{1,0:T(8,128)(2,1)} %copy-done.4) | copy-start | bytes 2359300

commit v2 on v0

v2 whole, which is shorter than its diff:
```python
import functools
import math

import jax
import jax.numpy as jnp
from jax import lax
from jax.experimental import pallas as pl
from jax.experimental.pallas import tpu as pltpu
from jax.sharding import PartitionSpec as P

HD = 128
LOG2E = 1.4426950408889634
FAR = 1e30
KERNEL_BYTES = 12 * 2**20
PROJECT_BYTES = 12 * 2**20
PACK_BYTES = 56 * 2**20
SHARES = (2, 2, 2)
SMEM_SPEC = pl.BlockSpec(memory_space=pltpu.SMEM)
VMEM_SPEC = pl.BlockSpec(memory_space=pltpu.VMEM)
HBM_SPEC = pl.BlockSpec(memory_space=pltpu.HBM)


def head_chunks(heads):
    whole = sum(SHARES)
    edges = sorted({(sum(SHARES[:i]) * heads) // whole for i in range(len(SHARES) + 1)})
    return [(low, high - low) for low, high in zip(edges[:-1], edges[1:])]


def pairing(length, first):
    pairs = [(i, i + 1) for i in range(first, length - 1, 2)]
    return pairs + [(b, a) for a, b in pairs]


def ring(length, distance):
    return [(i, (i + distance) % length) for i in range(length)]


def other_core(block):
    return lax.ppermute(block, "sub", [(0, 1), (1, 0)])


def to_neighbours(block):
    length = lax.axis_size("seq")
    return [lax.ppermute(block, "seq", pairing(length, start)) for start in (0, 1)]


def after(value, *earlier):
    return lax.optimization_barrier((value, *earlier))[0]


def pack_kernel(inputs, cuts, *refs):
    operands, outputs, sems = refs[:inputs], refs[inputs:-1], refs[-1]
    copies = []
    for out, runs in zip(outputs, cuts):
        at = 0
        for index, start_of, offset, width in runs:
            begin = start_of() + offset
            for step in range(0, width, HD):
                start = pl.multiple_of(begin + step, HD)
                copies.append(
                    pltpu.make_async_copy(
                        operands[index].at[:, pl.ds(start, HD)], out.at[:, at : at + HD], sems.at[len(copies)]
                    )
                )
                at += HD
    for copy in copies:
        copy.start()
    for copy in copies:
        copy.wait()


def pack(operands, cuts):
    shapes = [
        jax.ShapeDtypeStruct((operands[runs[0][0]].shape[0], sum(run[3] for run in runs)), jnp.bfloat16)
        for runs in cuts
    ]
    return pl.pallas_call(
        functools.partial(pack_kernel, len(operands), cuts),
        in_specs=[HBM_SPEC] * len(operands),
        out_specs=[VMEM_SPEC] * len(shapes),
        out_shape=shapes,
        scratch_shapes=[pltpu.SemaphoreType.DMA((sum(run[3] // HD for runs in cuts for run in runs),))],
        compiler_params=pltpu.CompilerParams(vmem_limit_bytes=PACK_BYTES),
    )(*operands)


def join_kernel(span, cuts, *refs):
    *operands, found = refs[: -len(cuts)]
    half = lax.axis_index("sub") * span
    for (low, runs), out in zip(cuts, refs[-len(cuts) :]):
        rows, width = found.shape[0], out.shape[1]
        at = 0
        for index, offset, size in runs:
            start = pl.multiple_of(half + offset, HD)
            out[:rows, at : at + size] = operands[index][:, pl.ds(start, size)]
            at += size
        out[rows:, :] = found[:, low : low + width]


def join(operands, found, span, cuts):
    rows = found.shape[0]
    widths = [sum(size for _, _, size in runs) for _, runs in cuts]
    return pl.pallas_call(
        functools.partial(join_kernel, span, cuts),
        in_specs=[VMEM_SPEC] * (len(operands) + 1),
        out_specs=[VMEM_SPEC] * len(cuts),
        out_shape=[jax.ShapeDtypeStruct((2 * rows, width), found.dtype) for width in widths],
        compiler_params=pltpu.CompilerParams(vmem_limit_bytes=PROJECT_BYTES),
    )(*operands, found)


def attention_kernel(first, plan, base, merge, tiles_ref, lists_ref, queries, *refs):
    arrays = max(index for held in plan for index, *_ in held) + 1
    operands, refs = refs[:arrays], refs[arrays:]
    if merge:
        prior_ref, mass_ref, *outs = refs
    else:
        out, mass_ref = refs
    rows = queries.shape[0] // 2
    entries = lists_ref.shape[1] - 1
    scale = LOG2E / math.sqrt(HD)
    early = lax.broadcasted_iota(jnp.int32, (1, 2 * rows), 1) < rows

    def included(query, tile):
        found = False
        for j in range(entries):
            found = found | ((lists_ref[query, j] == tile) & (j < lists_ref[query, entries]))
        return (found & (tile >= 0)).astype(jnp.int32)

    flags = []
    for s in range(len(plan[0])):
        tile = tiles_ref[base + s]
        flags.append(jnp.where(early, included(0, tile), included(1, tile)) > 0)

    def block(index, row, column):
        return operands[index][row : row + rows, column : column + HD]

    def scores(head):
        query = queries[:, (first + head) * HD : (first + head + 1) * HD]
        return [
            lax.dot_general(
                block(index, row, key), query, (((1,), (1,)), ((), ())), preferred_element_type=jnp.float32
            )
            for index, row, key, _ in plan[head]
        ]

    def finish(head, logits):
        cols = slice(head * HD, (head + 1) * HD)
        seen = slice((first + head) * HD, (first + head + 1) * HD)
        peak = before = mass_ref[first + head : first + head + 1, :] if merge else None
        for flag, logit in zip(flags, logits):
            top = jnp.where(flag, jnp.max(logit, axis=0, keepdims=True) * scale, -FAR)
            peak = top if peak is None else jnp.maximum(peak, top)
        accum = total = None
        for (index, row, _, value), flag, logit in zip(plan[head], flags, logits):
            weights = jnp.exp2(logit * scale - jnp.where(flag, peak, FAR))
            mass = jnp.sum(weights, axis=0, keepdims=True)
            term = lax.dot_general(
                block(index, row, value),
                weights.astype(jnp.bfloat16),
                (((0,), (0,)), ((), ())),
                preferred_element_type=jnp.float32,
            )
            total = mass if total is None else total + mass
            accum = term if accum is None else accum + term
        if merge:
            share = jnp.exp2(before - peak)
            accum = accum + share * prior_ref[seen, :]
            total = total + share
            result = accum * (1.0 / total)
            for i, out_i in enumerate(outs):
                out_i[:, cols] = jnp.transpose(result[:, i * rows : (i + 1) * rows]).astype(out_i.dtype)
        else:
            out[cols, :] = accum * (1.0 / total)
            mass_ref[head : head + 1, :] = peak + jnp.log2(total)

    logits = scores(0)
    for head in range(len(plan)):
        following = scores(head + 1) if head + 1 < len(plan) else None
        finish(head, logits)
        logits = following


def attend(first, plan, base, scalars, queries, operands, prior=None):
    rows = queries.shape[0] // 2
    count = len(plan)
    merge = prior is not None
    if merge:
        shapes = [jax.ShapeDtypeStruct((rows, count * HD), jnp.bfloat16)] * 2
    else:
        shapes = [
            jax.ShapeDtypeStruct((count * HD, 2 * rows), jnp.float32),
            jax.ShapeDtypeStruct((-(-count // 8) * 8, 2 * rows), jnp.float32),
        ]
    operands = (queries, *operands, *(prior or ()))
    return pl.pallas_call(
        functools.partial(attention_kernel, first, plan, base, merge),
        in_specs=[SMEM_SPEC] * 2 + [VMEM_SPEC] * len(operands),
        out_specs=[VMEM_SPEC] * 2,
        out_shape=shapes,
        compiler_params=pltpu.CompilerParams(vmem_limit_bytes=KERNEL_BYTES),
    )(*scalars, *operands)


def project_kernel(splits, groups, carried, gated, place_ref, *refs):
    refs = list(refs)
    if gated:
        held, sems = refs.pop(-2), refs.pop(-1)
    out = refs.pop()
    copies = []
    total_ref = refs.pop(0) if carried else None
    gate_ref = refs.pop(0) if gated else None
    block = out.shape[1] // splits
    for j in range(splits):
        where = pl.ds(pl.multiple_of(place_ref[j] * block, HD), block)
        total = total_ref[:, where] if carried else None
        at = 0
        for runs, arrays, pieces in groups:
            weights = refs[at + arrays : at + arrays + max(pieces, 1)]
            for index, column, place, offset, depth in runs:
                rows = pl.ds(pl.multiple_of(place_ref[place] + offset, HD), depth)
                right = weights[j][rows, :] if pieces else weights[0][rows, where]
                left = refs[at + index][:, column : column + depth]
                term = jnp.dot(left, right, preferred_element_type=jnp.float32)
                total = term if total is None else total + term
            at += arrays + max(pieces, 1)
        if gated:
            held[:, j * block : (j + 1) * block] = (total * gate_ref[:, where]).astype(out.dtype)
            source = held.at[:, j * block : (j + 1) * block]
            copies.append(pltpu.make_async_copy(source, out.at[:, where], sems.at[j]))
            copies[-1].start()
        else:
            out[:, where] = total
    for copy in copies:
        copy.wait()


def project(places, splits, groups, width, total=None, gate=None):
    operands = [a for a in (total, gate) if a is not None]
    plan = []
    for runs, arrays, weights, whole in groups:
        plan.append((runs, len(arrays), 0 if whole else len(weights)))
        operands += [*arrays, *weights]
    rows = groups[0][1][0].shape[0]
    scratch = [pltpu.VMEM((rows, width), jnp.bfloat16), pltpu.SemaphoreType.DMA((splits,))]
    return pl.pallas_call(
        functools.partial(project_kernel, splits, plan, total is not None, gate is not None),
        in_specs=[SMEM_SPEC] + [VMEM_SPEC] * len(operands),
        out_specs=VMEM_SPEC if gate is None else HBM_SPEC,
        out_shape=jax.ShapeDtypeStruct((rows, width), jnp.float32 if gate is None else jnp.bfloat16),
        scratch_shapes=scratch if gate is not None else [],
        compiler_params=pltpu.CompilerParams(vmem_limit_bytes=PROJECT_BYTES),
    )(places, *operands)


def local(queries, keys, values, kv_list, kv_count, out_weight, gate):
    rows = queries.shape[0]
    length, subs = lax.axis_size("seq"), lax.axis_size("sub")
    n_head, n_groups = lax.axis_size("head"), lax.axis_size("groups")
    z, c = lax.axis_index("seq"), lax.axis_index("sub")
    x, g = lax.axis_index("head"), lax.axis_index("groups")
    width = out_weight.shape[1] // n_head
    heads = queries.shape[1] // HD
    if heads % 2:
        queries, keys, values = (jnp.pad(a, ((0, 0), (0, HD))) for a in (queries, keys, values))
        out_weight = jnp.pad(out_weight, ((0, HD), (0, 0)))
    half = (heads + 1) // 2
    span = half * HD
    chunks = head_chunks(half)
    last = len(chunks) - 1

    even = z + 1 - 2 * lax.rem(z, 2)
    odd = z - 1 + 2 * lax.rem(z, 2)
    tiles = []
    for place in (z, even, odd):
        inside = (place >= 0) & (place < length)
        tiles += [jnp.where(inside, place * subs + c, -1), jnp.where(inside, place * subs + 1 - c, -1)]
    lists = jnp.concatenate([kv_list, kv_count.reshape(1, 1)], axis=1)

    splits = n_groups * subs
    if width % (splits * HD):
        splits = 1
    block = width // splits
    if splits > 1:
        places = [lax.rem(g + d, n_groups) * subs + s for d in range(n_groups) for s in (c, 1 - c)]
    else:
        places = [0]

    def piece_at(d):
        there = lax.rem(lax.axis_index("head") + d, n_head) * width
        return there + ((lax.axis_index("groups") * subs + lax.axis_index("sub")) * block if splits > 1 else 0)

    piece = places[0]
    places = jnp.stack([*places, c * span, (1 - c) * span]).astype(jnp.int32)

    runs_of = [((2, 0, span),)]
    for first, count in chunks:
        runs_of.append(tuple((index, first * HD, count * HD) for index in (0, 1)))
    cuts, low = [], 0
    for runs in runs_of:
        cuts.append((low, runs))
        low += sum(size for _, _, size in runs)

    def other_half():
        return (1 - lax.axis_index("sub")) * span

    cut = tuple((index, other_half, offset, size) for runs in runs_of for index, offset, size in runs)
    (other,) = pack((keys, values, queries), (cut,))
    found = other_core(other)
    sent = [
        lax.dynamic_slice(out_weight, (0, lax.rem(x + d, n_head) * width + piece * block), (2 * span, block))
        for d in range(1, n_head)
    ]
    first_message = join((keys, values), found, span, cuts[1:2])
    queries, *message = join((keys, values, queries), found, span, [cuts[0], *cuts[2:]])
    message = [*first_message, *message]
    near = [to_neighbours(message[0])]
    lists = jnp.concatenate([lists, other_core(lists)], axis=0)
    scalars = (jnp.stack(tiles).astype(jnp.int32), lists)

    near.append(to_neighbours(message[1]))
    crossed = [lax.ppermute(a, "head", ring(n_head, d + 1)) for d, a in enumerate(sent)]

    def runs(some):
        return [
            (index, side * chunks[i][1] * HD, splits + side, chunks[i][0] * HD, chunks[i][1] * HD)
            for index, i in enumerate(some)
            for side in (0, 1)
        ]

    def plan_of(i, sources):
        count = chunks[i][1]
        return [tuple((a, row, h * HD, (count + h) * HD) for a, row in sources) for h in range(count)]

    plan = sum((plan_of(i, ((i, 0), (i, rows))) for i in range(len(chunks))), [])
    prior = attend(0, plan, 0, scalars, queries, message)
    mine = lax.dynamic_slice(after(out_weight, prior), (0, x * width), (2 * span, width))
    near[0], crossed = lax.optimization_barrier((after(near[0], prior, mine), crossed))
    spread = [
        [got] + [lax.ppermute(got, "groups", ring(n_groups, n_groups - e)) for e in range(1, n_groups)]
        if splits > 1
        else [got]
        for got in crossed
    ]

    ours, moved = [], []
    for i, (first, _) in enumerate(chunks):
        plan = plan_of(i, [(index, row) for index in (0, 1) for row in (0, rows)])
        kept, given = attend(first, plan, 2, scalars, queries, near[i], prior)
        ours.append(jnp.concatenate([kept, other_core(given)], axis=1))
        leaving = after(ours[i], moved) if i else ours[i]
        moved.append([lax.ppermute(leaving, "head", ring(n_head, d)) for d in range(1, n_head)])
        if i + 2 < len(chunks):
            near.append(to_neighbours(after(message[i + 2], kept)))
        if i == 0:
            near[1] = after(near[1], kept, ours[0])
        if i == last - 1:
            total = project(places, splits, [(runs(range(last)), ours[:], [mine], True)], width)
            near[last], spread = lax.optimization_barrier((after(near[last], total, moved), spread))
    pieces = [[a for got in gots for a in (got, other_core(got))] if splits > 1 else gots for gots in spread]

    groups = [(runs([last]), [ours[last]], [mine], True)]
    groups += [(runs(range(last)), [moved[i][d] for i in range(last)], pieces[d], False) for d in range(n_head - 1)]
    total = project(places, splits, groups, width, total)
    groups = [(runs([last]), [moved[last][d]], pieces[d], False) for d in range(n_head - 1)]
    return project(places, splits, groups, width, total, gate.reshape(1, width))


def solution(mesh):
    return jax.shard_map(
        local,
        mesh=mesh,
        in_specs=(
            P(("groups", "seq", "sub"), "head"),
            P(("groups", "seq", "sub"), "head"),
            P(("groups", "seq", "sub"), "head"),
            P(("groups", "seq", "sub"), None),
            P(("groups", "seq", "sub")),
            P("head", None),
            P("head"),
        ),
        out_specs=P(("groups", "seq", "sub"), "head"),
        check_vma=False,
    )
```

time: 283 us -> 92.8 us (0.33)
  waiting for transfers between devices: 153 us -> 17.7 us
  matrix products: 52.7 us -> 0 us
  Pallas kernels: 0 us -> 40.1 us
  other arithmetic: 21.3 us -> 0.15 us
  between operations: 18.7 us -> 1.04 us
  local copies, waits for them, and re-layouts: 17.8 us -> 12.1 us
  starting transfers between devices: 17.1 us -> 20.2 us
    ppermute x6 -> x18, waiting for transfers between devices: 120 us -> 17.7 us  [the longest x3 8.09 us: local(): lax.ppermute(leaving, 'head', ring(n_head, d))]
    dot_general x15 -> x0, matrix products: 52.7 us -> none  [the longest x7 26.8 us: local(): jnp.einsum('abhqk,bkhd->aqhd', weights.astype(jnp.bfloat16), value_tiles,...]
    pallas_call x0 -> x10, Pallas kernels: none -> 40.1 us  [the longest x4 21.4 us: attend(): pl.pallas_call(functools.partial(attention_kernel, first, plan, base, mer...]
    reduce_scatter x1 -> x0, waiting for transfers between devices: 33.4 us -> none  [local(): lax.psum_scatter(lax.dot_general(out_weight, attention, (((0,), (1,)), ((...]
    reduce_sum x1 -> x0, other arithmetic: 16.3 us -> none  [local(): compute_total = compute_total + jnp.sum(weights, axis=(1, 4))]
    slice x6 -> x0, local copies, waits for them, and re-layouts: 13.3 us -> none  [the longest x5 12.1 us: local(): value_tiles = fetched[1].reshape(tiles_here, tile_rows, heads_here, HD)]
    dynamic_slice x0 -> x2, local copies, waits for them, and re-layouts: none -> 7.34 us  [the longest x1 4.79 us: local(): lax.dynamic_slice(after(out_weight, prior), (0, x * width), (2 * span, wi...]
    ppermute x6 -> x18, starting transfers between devices: 17.1 us -> 20.2 us  [the longest x6 9.95 us: to_neighbours(): lax.ppermute(block, 'seq', pairing(length, start))]
  transfers between devices with their start and end apart: 7 -> 18, of which waited for: 4 -> 11; matrix products, arithmetic and copies ran while one was open for 10% -> 10% of each run, Pallas kernels for 0% -> 37%
where the time goes in v2:
time: 92.8 us; the launch traced here: 91.3 us
  Pallas kernels  40.1 us (43%)
  starting transfers between devices  20.2 us (22%)
  waiting for transfers between devices  17.7 us (19%)
  local copies, waits for them, and re-layouts  12.1 us (13%)
  between operations  1.04 us (1%)
    pallas_call x4, Pallas kernels, attend(): pl.pallas_call(functools.partial(attention_kernel, first, plan, base, mer...  21.4 us
    pallas_call x3, Pallas kernels, project(): pl.pallas_call(functools.partial(project_kernel, splits, plan, total is n...  10.7 us
    ppermute x6, starting transfers between devices, to_neighbours(): lax.ppermute(block, 'seq', pairing(length, start))  9.95 us
    ppermute x3, waiting for transfers between devices, local(): lax.ppermute(leaving, 'head', ring(n_head, d))  8.09 us
    ppermute x7, starting transfers between devices, other_core(): return lax.ppermute(block, 'sub', [(0, 1), (1, 0)])  6.53 us
    ppermute x6, waiting for transfers between devices, to_neighbours(): lax.ppermute(block, 'seq', pairing(length, start))  5.13 us
    pallas_call x2, Pallas kernels, join(): pl.pallas_call(functools.partial(join_kernel, span, cuts), in_specs=[VMEM...  5.01 us
    dynamic_slice x1, local copies, waits for them, and re-layouts, local(): lax.dynamic_slice(after(out_weight, prior), (0, x * width), (2 * span, wi...  4.79 us
  transfers between devices with their start and end apart: 18, of which 11 were waited for; matrix products, arithmetic and copies ran while one was open for 10% of the time, Pallas kernels for 37%

profile of v2, /device:TPU:13, one launch (start us, length us, event | category | flops | bytes accessed | tf_op | source)
XLA Modules:
  0.0 91.3 jit_solution(3938915092483333835)
XLA Ops:
  0.0 2.9 %shard_map.73 = bf16[384,2304]{1,0:T(8,128)(2,1)} custom-call(bf16[384,1536]{1,0:T(8,128)(2,1)} %refs_0_.5, bf16[384,1536]{1,0:T(8,128)(2,1)} %refs_1_.5, bf16[384,1536]{1,0:T(8,128)(2,1)} %refs_2_.3), custom_call_target="tpu_custom_call" | custom-call | tf_op jit(solution)/shard_map/pallas_call | solution.py:77
  2.9 0.7 collective-permute-start.1
  3.7 2.6 %constant_dynamic-slice_fusion = bf16[1536,384]{1,0:T(8,128)(2,1)} fusion(bf16[1536,3072]{1,0:T(8,128)(2,1)} %param.12, s32[]{:T(128)S(6)} %select_n.32), kind=kLoop, calls=%fused_computation.8 | loop fusion | bytes 2359300 | tf_op jit(solution)/shard_map/dynamic_slice | solution.py:311
  6.2 1.2 %collective-permute-start.4 = (bf16[1536,384]{1,0:T(8,128)(2,1)}, bf16[1536,384]{1,0:T(8,128)(2,1)}, u32[]{:S(2)}, u32[]{:S(2)}) collective-permute-start(bf16[1536,384]{1,0:T(8,128)(2,1)} %constant_dynamic-slice_fusion), channel_id=1, source_target_pairs={{0,2},{2,0},{1,3},{3,1},{4,6},{6,4},{5,7},{7,5},{8,10},{10,8},{9,1... | collective-permute-start | bytes 3538952 | tf_op jit(solution)/shard_map/ppermute | solution.py:322
  8.1 0.0 copy-start.5
  8.1 2.5 %shard_map.75.refs_0_ = bf16[768,512]{1,0:T(8,128)(2,1)} custom-call(bf16[384,1536]{1,0:T(8,128)(2,1)S(1)} %copy-done.3, bf16[384,1536]{1,0:T(8,128)(2,1)S(1)} %copy-done.4, bf16[384,2304]{1,0:T(8,128)(2,1)} %collective-permute-done.1.refs_3_.refs_2_), custom_call_target="tpu_custom_call" | custom-call | tf_op jit(solution)/shard_map/pallas_call | solution.py:103
  10.7 0.2 collective-permute-start.2
  10.8 4.3 %collective-permute-start.3 = (bf16[768,512]{1,0:T(8,128)(2,1)}, bf16[768,512]{1,0:T(8,128)(2,1)}, u32[]{:S(2)}, u32[]{:S(2)}) collective-permute-start(bf16[768,512]{1,0:T(8,128)(2,1)} %shard_map.75.refs_0_), channel_id=1, source_target_pairs={{4,8},{8,4},{5,9},{9,5},{6,10},{10,6},{7,11},{11,7},{20,24},{24,20... | collective-permute-start | bytes 2359304 | tf_op jit(solution)/shard_map/ppermute | solution.py:44
  15.2 0.1 pad_add_fusion.1
  15.2 0.9 collective-permute-start
  16.2 0.1 stack.55.tiles_ref
  16.2 0.7 collective-permute-done
  17.0 0.1 pad_add_fusion.lists_ref
  17.1 2.5 %shard_map.74 = (bf16[768,768]{1,0:T(8,128)(2,1)S(1)}, bf16[768,512]{1,0:T(8,128)(2,1)S(1)}, bf16[768,512]{1,0:T(8,128)(2,1)}) custom-call(bf16[384,1536]{1,0:T(8,128)(2,1)S(1)} %copy-done.3, bf16[384,1536]{1,0:T(8,128)(2,1)S(1)} %copy-done.4, bf16[384,1536]{1,0:T(8,128)(2,1)S(1)} %copy-done.5, bf16[384,2304]{1,0:T(8,128)(2,1)} %collective-permute-done.1.refs_3_.refs_2_), custom_call_target="tpu_custom_call" | custom-call | tf_op jit(solution)/shard_map/pallas_call | solution.py:103
  19.5 1.9 %collective-permute-start.7 = (bf16[768,512]{1,0:T(8,128)(2,1)S(1)}, bf16[768,512]{1,0:T(8,128)(2,1)S(1)}, u32[]{:S(2)}, u32[]{:S(2)}) collective-permute-start(bf16[768,512]{1,0:T(8,128)(2,1)S(1)} %get-tuple-element.34.refs_1_), channel_id=1, source_target_pairs={{4,8},{8,4},{5,9},{9,5},{6,10},{10,6},{7,11},{11,7},{20,24},{24,20... | collective-permute-start | bytes 2359304 | tf_op jit(solution)/shard_map/ppermute | solution.py:44
  21.5 6.5 %shard_map.76 = (f32[768,768]{1,0:T(8,128)S(1)}, f32[8,768]{1,0:T(8,128)S(1)}) custom-call(s32[6]{0:T(128)S(1)} %stack.55.tiles_ref, s32[2,7]{1,0:T(2,128)S(1)} %pad_add_fusion.lists_ref, bf16[768,768]{1,0:T(8,128)(2,1)S(1)} %get-tuple-element.33.queries, bf16[768,512]{1,0:T(8,128)(2,1)} %shard_map.75.refs_0_, ...), custom_call_target="tpu_custom_call" | custom-call | tf_op jit(solution)/shard_map/pallas_call | solution.py:196
  27.9 4.8 %constant_dynamic-slice_fusion.1.refs_2_ = bf16[1536,1536]{1,0:T(8,128)(2,1)} fusion(bf16[1536,3072]{1,0:T(8,128)(2,1)} %param.12, s32[]{:T(128)S(6)} %select_n.31), kind=kLoop, calls=%fused_computation.9 | loop fusion | bytes 9437188 | tf_op jit(solution)/shard_map/dynamic_slice | solution.py:337
  32.7 0.1 collective-permute-done.3.refs_1_
  32.8 1.3 %collective-permute-done.4.refs_5_.refs_3_ = bf16[1536,384]{1,0:T(8,128)(2,1)} collective-permute-done((bf16[1536,384]{1,0:T(8,128)(2,1)}, bf16[1536,384]{1,0:T(8,128)(2,1)}, u32[]{:S(2)}, u32[]{:S(2)}) %collective-permute-start.4) | collective-permute-done | bytes 1179680 | tf_op jit(solution)/shard_map/ppermute | solution.py:322
  34.1 0.2 collective-permute-start.13
  34.3 5.2 %shard_map.77 = (bf16[384,256]{1,0:T(8,128)(2,1)S(1)}, bf16[384,256]{1,0:T(8,128)(2,1)S(1)}) custom-call(s32[6]{0:T(128)S(1)} %stack.55.tiles_ref, s32[2,7]{1,0:T(2,128)S(1)} %pad_add_fusion.lists_ref, bf16[768,768]{1,0:T(8,128)(2,1)S(1)} %get-tuple-element.33.queries, bf16[768,512]{1,0:T(8,128)(2,1)} %collective-permute-done.2.refs_0_, ...), custom_call_target="tpu_custom_call" | custom-call | tf_op jit(solution)/shard_map/pallas_call | solution.py:196
  39.5 1.2 %collective-permute-start.5 = (bf16[384,256]{1,0:T(8,128)(2,1)S(1)}, bf16[384,256]{1,0:T(8,128)(2,1)S(1)}, u32[]{:S(2)}, u32[]{:S(2)}) collective-permute-start(bf16[384,256]{1,0:T(8,128)(2,1)S(1)} %get-tuple-element.44), channel_id=1, source_target_pairs={{0,1},{1,0},{2,3},{3,2},{4,5},{5,4},{6,7},{7,6},{8,9},{9,8},{10,11... | collective-permute-start | bytes 589832 | tf_op jit(solution)/shard_map/ppermute | solution.py:39
  40.8 1.1 %collective-permute-done.5 = bf16[384,256]{1,0:T(8,128)(2,1)S(1)} collective-permute-done((bf16[384,256]{1,0:T(8,128)(2,1)S(1)}, bf16[384,256]{1,0:T(8,128)(2,1)S(1)}, u32[]{:S(2)}, u32[]{:S(2)}) %collective-permute-start.5) | collective-permute-done | bytes 196640 | tf_op jit(solution)/shard_map/ppermute | solution.py:39
  41.8 1.3 %collective-permute-start.11 = (bf16[384,512]{1,0:T(8,128)(2,1)S(1)}, bf16[384,512]{1,0:T(8,128)(2,1)S(1)}, u32[]{:S(2)}, u32[]{:S(2)}) collective-permute-start(bf16[384,512]{1,0:T(8,128)(2,1)S(1)} %constant_dynamic-update-slice_fusion.refs_0_), channel_id=1, source_target_pairs={{0,2},{2,0},{1,3},{3,1},{4,6},{6,4},{5,7},{7,5},{8,10},{10,8},{9,1... | collective-permute-start | bytes 1179656 | tf_op jit(solution)/shard_map/ppermute | solution.py:352
  43.1 3.4 %collective-permute-start.10 = (bf16[768,512]{1,0:T(8,128)(2,1)}, bf16[768,512]{1,0:T(8,128)(2,1)}, u32[]{:S(2)}, u32[]{:S(2)}) collective-permute-start(bf16[768,512]{1,0:T(8,128)(2,1)} %get-tuple-element.49.refs_2_), channel_id=1, source_target_pairs={{4,8},{8,4},{5,9},{9,5},{6,10},{10,6},{7,11},{11,7},{20,24},{24,20... | collective-permute-start | bytes 2359304 | tf_op jit(solution)/shard_map/ppermute | solution.py:44
  46.5 0.1 collective-permute-done.6.refs_0_
  46.6 0.2 collective-permute-start.9
  46.8 2.9 %collective-permute-done.7.refs_1_ = bf16[768,512]{1,0:T(8,128)(2,1)S(1)} collective-permute-done((bf16[768,512]{1,0:T(8,128)(2,1)S(1)}, bf16[768,512]{1,0:T(8,128)(2,1)S(1)}, u32[]{:S(2)}, u32[]{:S(2)}) %collective-permute-start.7) | collective-permute-done | bytes 786464 | tf_op jit(solution)/shard_map/ppermute | solution.py:44
  49.6 4.5 %shard_map.78 = (bf16[384,256]{1,0:T(8,128)(2,1)S(1)}, bf16[384,256]{1,0:T(8,128)(2,1)S(1)}) custom-call(s32[6]{0:T(128)S(1)} %stack.55.tiles_ref, s32[2,7]{1,0:T(2,128)S(1)} %pad_add_fusion.lists_ref, bf16[768,768]{1,0:T(8,128)(2,1)S(1)} %get-tuple-element.33.queries, bf16[768,512]{1,0:T(8,128)(2,1)S(1)} %collective-permute-done.6.refs_0_, ...), custom_call_target="tpu_custom_call" | custom-call | tf_op jit(solution)/shard_map/pallas_call | solution.py:196
  54.1 1.9 %collective-permute-start.8 = (bf16[384,256]{1,0:T(8,128)(2,1)S(1)}, bf16[384,256]{1,0:T(8,128)(2,1)S(1)}, u32[]{:S(2)}, u32[]{:S(2)}) collective-permute-start(bf16[384,256]{1,0:T(8,128)(2,1)S(1)} %get-tuple-element.48), channel_id=1, source_target_pairs={{0,1},{1,0},{2,3},{3,2},{4,5},{5,4},{6,7},{7,6},{8,9},{9,8},{10,11... | collective-permute-start | bytes 589832 | tf_op jit(solution)/shard_map/ppermute | solution.py:39
  56.0 0.7 constant_dynamic-update-slice_fusion.3
  56.7 0.4 collective-permute-done.8
  57.1 0.7 constant_dynamic-update-slice_fusion.2.refs_1_
  57.8 0.7 copy-done.6
  58.6 0.5 collective-permute-start.12
  59.0 0.1 stack.48.place_ref
  59.1 2.3 %copy-done = bf16[1536,1536]{1,0:T(8,128)(2,1)S(1)} copy-done((bf16[1536,1536]{1,0:T(8,128)(2,1)S(1)}, bf16[1536,1536]{1,0:T(8,128)(2,1)}, u32[]{:S(2)}) %copy-start) | copy-done | bytes 4718616
  61.4 2.9 %shard_map.79.refs_0_ = f32[384,1536]{1,0:T(8,128)S(1)} custom-call(s32[6]{0:T(128)S(1)} %stack.48.place_ref, bf16[384,512]{1,0:T(8,128)(2,1)S(1)} %constant_dynamic-update-slice_fusion.refs_0_, bf16[384,512]{1,0:T(8,128)(2,1)} %constant_dynamic-update-slice_fusion.2.refs_1_, bf16[1536,1536]{1,0:T(8,128)(2,1)S(1)} %copy-done), custom_call_target="tpu_custom_call" | custom-call | tf_op jit(solution)/shard_map/pallas_call | solution.py:246
  64.4 2.1 %collective-permute-done.10.refs_1_ = bf16[768,512]{1,0:T(8,128)(2,1)} collective-permute-done((bf16[768,512]{1,0:T(8,128)(2,1)}, bf16[768,512]{1,0:T(8,128)(2,1)}, u32[]{:S(2)}, u32[]{:S(2)}) %collective-permute-start.10) | collective-permute-done | bytes 786464 | tf_op jit(solution)/shard_map/ppermute | solution.py:44
  66.5 2.7 %collective-permute-done.12.refs_4_ = bf16[384,512]{1,0:T(8,128)(2,1)} collective-permute-done((bf16[384,512]{1,0:T(8,128)(2,1)}, bf16[384,512]{1,0:T(8,128)(2,1)}, u32[]{:S(2)}, u32[]{:S(2)}) %collective-permute-start.12) | collective-permute-done | bytes 393248 | tf_op jit(solution)/shard_map/ppermute | solution.py:352
  69.2 1.2 %collective-permute-start.15 = (bf16[1536,384]{1,0:T(8,128)(2,1)}, bf16[1536,384]{1,0:T(8,128)(2,1)S(1)}, u32[]{:S(2)}, u32[]{:S(2)}) collective-permute-start(bf16[1536,384]{1,0:T(8,128)(2,1)} %collective-permute-done.4.refs_5_.refs_3_), channel_id=1, source_target_pairs={{0,1},{1,0},{2,3},{3,2},{4,5},{5,4},{6,7},{7,6},{8,9},{9,8},{10,11... | collective-permute-start | bytes 3538952 | tf_op jit(solution)/shard_map/ppermute | solution.py:39
  70.4 5.2 %shard_map.80 = (bf16[384,256]{1,0:T(8,128)(2,1)S(1)}, bf16[384,256]{1,0:T(8,128)(2,1)S(1)}) custom-call(s32[6]{0:T(128)S(1)} %stack.55.tiles_ref, s32[2,7]{1,0:T(2,128)S(1)} %pad_add_fusion.lists_ref, bf16[768,768]{1,0:T(8,128)(2,1)S(1)} %copy-done.2, bf16[768,512]{1,0:T(8,128)(2,1)} %collective-permute-done.9.refs_0_, ...), custom_call_target="tpu_custom_call" | custom-call | tf_op jit(solution)/shard_map/pallas_call | solution.py:196
  75.7 0.6 collective-permute-start.14
  76.2 1.1 %collective-permute-done.14 = bf16[384,256]{1,0:T(8,128)(2,1)S(1)} collective-permute-done((bf16[384,256]{1,0:T(8,128)(2,1)S(1)}, bf16[384,256]{1,0:T(8,128)(2,1)S(1)}, u32[]{:S(2)}, u32[]{:S(2)}) %collective-permute-start.14) | collective-permute-done | bytes 196640 | tf_op jit(solution)/shard_map/ppermute | solution.py:39
  77.3 0.5 collective-permute-start.17
  77.9 4.4 %shard_map.81.refs_0_ = f32[384,1536]{1,0:T(8,128)S(1)} custom-call(s32[6]{0:T(128)S(1)} %stack.48.place_ref, f32[384,1536]{1,0:T(8,128)S(1)} %shard_map.79.refs_0_, bf16[384,512]{1,0:T(8,128)(2,1)S(1)} %constant_dynamic-update-slice_fusion.4.refs_1_, bf16[1536,1536]{1,0:T(8,128)(2,1)S(1)} %bitcast.16, bf16[384,512]{1,0:T(8,128)(2,1)S(1)} %copy-done.7, ...), custom_call_target="tpu_custom_call" | custom-call | tf_op jit(solution)/shard_map/pallas_call | solution.py:246
  82.3 5.4 %collective-permute-done.17.refs_2_ = bf16[384,512]{1,0:T(8,128)(2,1)S(1)} collective-permute-done((bf16[384,512]{1,0:T(8,128)(2,1)S(1)}, bf16[384,512]{1,0:T(8,128)(2,1)S(1)}, u32[]{:S(2)}, u32[]{:S(2)}) %collective-permute-start.17) | collective-permute-done | bytes 393248 | tf_op jit(solution)/shard_map/ppermute | solution.py:352
  87.7 3.4 %shard_map.82 = bf16[384,1536]{1,0:T(8,128)(2,1)} custom-call(s32[6]{0:T(128)S(1)} %stack.48.place_ref, f32[384,1536]{1,0:T(8,128)S(1)} %shard_map.81.refs_0_, f32[1,1536]{1,0:T(1,128)S(1)} %reshape.7.refs_1_, bf16[384,512]{1,0:T(8,128)(2,1)S(1)} %collective-permute-done.17.refs_2_, bf16[1536,384]{1,0:T(8,128)(2,1)} %collective-permute-done.4.refs_5_.refs_3_, ...), custom_call_target="tpu_custom_call" | custom-call | tf_op jit(solution)/shard_map/pallas_call | solution.py:246
  (36 shorter events, 0.1 us)
Async XLA Ops:
  2.9 5.2 %collective-permute-start.1 = (bf16[384,2304]{1,0:T(8,128)(2,1)}, bf16[384,2304]{1,0:T(8,128)(2,1)}, u32[]{:S(2)}, u32[]{:S(2)}) collective-permute-start(bf16[384,2304]{1,0:T(8,128)(2,1)} %shard_map.73), channel_id=1, source_target_pairs={{0,1},{1,0},{2,3},{3,2},{4,5},{5,4},{6,7},{7,6},{8,9},{9,8},{10,11... | collective-permute-start | bytes 5308424 | tf_op jit(solution)/shard_map/ppermute | solution.py:39
  3.7 4.5 %copy-start.3 = (bf16[384,1536]{1,0:T(8,128)(2,1)S(1)}, bf16[384,1536]{1,0:T(8,128)(2,1)}, u32[]{:S(2)}) copy-start(bf16[384,1536]{1,0:T(8,128)(2,1)} %refs_0_.5) | copy-start | bytes 3538948
  3.7 4.5 %copy-start.4 = (bf16[384,1536]{1,0:T(8,128)(2,1)S(1)}, bf16[384,1536]{1,0:T(8,128)(2,1)}, u32[]{:S(2)}) copy-start(bf16[384,1536]{1,0:T(8,128)(2,1)} %refs_1_.5) | copy-start | bytes 3538948
  6.2 27.8 %collective-permute-start.4 = (bf16[1536,384]{1,0:T(8,128)(2,1)}, bf16[1536,384]{1,0:T(8,128)(2,1)}, u32[]{:S(2)}, u32[]{:S(2)}) collective-permute-start(bf16[1536,384]{1,0:T(8,128)(2,1)} %constant_dynamic-slice_fusion), channel_id=1, source_target_pairs={{0,2},{2,0},{1,3},{3,1},{4,6},{6,4},{5,7},{7,5},{8,10},{10,8},{9,1... | collective-permute-start | bytes 3538952 | tf_op jit(solution)/shard_map/ppermute | solution.py:322
  8.1 7.1 %copy-start.9 = (s32[1,6]{1,0:T(1,128)S(1)}, s32[1,6]{1,0:T(1,128)}, u32[]{:S(2)}) copy-start(s32[1,6]{1,0:T(1,128)} %param.10) | copy-start | bytes 76
  8.1 9.0 %copy-start.5 = (bf16[384,1536]{1,0:T(8,128)(2,1)S(1)}, bf16[384,1536]{1,0:T(8,128)(2,1)}, u32[]{:S(2)}) copy-start(bf16[384,1536]{1,0:T(8,128)(2,1)} %refs_2_.3) | copy-start | bytes 3538948
  10.7 22.0 %collective-permute-start.2 = (bf16[768,512]{1,0:T(8,128)(2,1)}, bf16[768,512]{1,0:T(8,128)(2,1)}, u32[]{:S(2)}, u32[]{:S(2)}) collective-permute-start(bf16[768,512]{1,0:T(8,128)(2,1)} %shard_map.75.refs_0_), channel_id=1, source_target_pairs={{0,4},{8,12},{4,0},{12,8},{1,5},{9,13},{5,1},{13,9},{2,6},{10,14},... | collective-permute-start | bytes 2359304 | tf_op jit(solution)/shard_map/ppermute | solution.py:44
  10.8 22.0 %collective-permute-start.3 = (bf16[768,512]{1,0:T(8,128)(2,1)}, bf16[768,512]{1,0:T(8,128)(2,1)}, u32[]{:S(2)}, u32[]{:S(2)}) collective-permute-start(bf16[768,512]{1,0:T(8,128)(2,1)} %shard_map.75.refs_0_), channel_id=1, source_target_pairs={{4,8},{8,4},{5,9},{9,5},{6,10},{10,6},{7,11},{11,7},{20,24},{24,20... | collective-permute-start | bytes 2359304 | tf_op jit(solution)/shard_map/ppermute | solution.py:44
  15.2 1.7 %collective-permute-start = (s32[1,7]{1,0:T(1,128)S(1)}, s32[1,7]{1,0:T(1,128)S(1)}, u32[]{:S(2)}, u32[]{:S(2)}) collective-permute-start(s32[1,7]{1,0:T(1,128)S(1)} %pad_add_fusion.1), channel_id=1, source_target_pairs={{0,1},{1,0},{2,3},{3,2},{4,5},{5,4},{6,7},{7,6},{8,9},{9,8},{10,11... | collective-permute-start | bytes 92 | tf_op jit(solution)/shard_map/ppermute | solution.py:39
  19.5 30.1 %copy-start.1 = (bf16[768,768]{1,0:T(8,128)(2,1)}, bf16[768,768]{1,0:T(8,128)(2,1)S(1)}, u32[]{:S(2)}) copy-start(bf16[768,768]{1,0:T(8,128)(2,1)S(1)} %get-tuple-element.33.queries) | copy-start | bytes 3538948
  19.5 27.1 %collective-permute-start.6 = (bf16[768,512]{1,0:T(8,128)(2,1)S(1)}, bf16[768,512]{1,0:T(8,128)(2,1)S(1)}, u32[]{:S(2)}, u32[]{:S(2)}) collective-permute-start(bf16[768,512]{1,0:T(8,128)(2,1)S(1)} %get-tuple-element.34.refs_1_), channel_id=1, source_target_pairs={{0,4},{8,12},{4,0},{12,8},{1,5},{9,13},{5,1},{13,9},{2,6},{10,14},... | collective-permute-start | bytes 2359304 | tf_op jit(solution)/shard_map/ppermute | solution.py:44
  19.5 30.1 %collective-permute-start.7 = (bf16[768,512]{1,0:T(8,128)(2,1)S(1)}, bf16[768,512]{1,0:T(8,128)(2,1)S(1)}, u32[]{:S(2)}, u32[]{:S(2)}) collective-permute-start(bf16[768,512]{1,0:T(8,128)(2,1)S(1)} %get-tuple-element.34.refs_1_), channel_id=1, source_target_pairs={{4,8},{8,4},{5,9},{9,5},{6,10},{10,6},{7,11},{11,7},{20,24},{24,20... | collective-permute-start | bytes 2359304 | tf_op jit(solution)/shard_map/ppermute | solution.py:44
  34.1 35.1 %collective-permute-start.13 = (bf16[1536,384]{1,0:T(8,128)(2,1)}, bf16[1536,384]{1,0:T(8,128)(2,1)}, u32[]{:S(2)}, u32[]{:S(2)}) collective-permute-start(bf16[1536,384]{1,0:T(8,128)(2,1)} %collective-permute-done.4.refs_5_.refs_3_), channel_id=1, source_target_pairs={{0,16},{16,0},{1,17},{17,1},{2,18},{18,2},{3,19},{19,3},{4,20},{20... | collective-permute-start | bytes 3538952 | tf_op jit(solution)/shard_map/ppermute | solution.py:340
  39.5 2.3 %collective-permute-start.5 = (bf16[384,256]{1,0:T(8,128)(2,1)S(1)}, bf16[384,256]{1,0:T(8,128)(2,1)S(1)}, u32[]{:S(2)}, u32[]{:S(2)}) collective-permute-start(bf16[384,256]{1,0:T(8,128)(2,1)S(1)} %get-tuple-element.44), channel_id=1, source_target_pairs={{0,1},{1,0},{2,3},{3,2},{4,5},{5,4},{6,7},{7,6},{8,9},{9,8},{10,11... | collective-permute-start | bytes 589832 | tf_op jit(solution)/shard_map/ppermute | solution.py:39
  41.8 16.0 %collective-permute-start.11 = (bf16[384,512]{1,0:T(8,128)(2,1)S(1)}, bf16[384,512]{1,0:T(8,128)(2,1)S(1)}, u32[]{:S(2)}, u32[]{:S(2)}) collective-permute-start(bf16[384,512]{1,0:T(8,128)(2,1)S(1)} %constant_dynamic-update-slice_fusion.refs_0_), channel_id=1, source_target_pairs={{0,2},{2,0},{1,3},{3,1},{4,6},{6,4},{5,7},{7,5},{8,10},{10,8},{9,1... | collective-permute-start | bytes 1179656 | tf_op jit(solution)/shard_map/ppermute | solution.py:352
  43.1 23.4 %collective-permute-start.10 = (bf16[768,512]{1,0:T(8,128)(2,1)}, bf16[768,512]{1,0:T(8,128)(2,1)}, u32[]{:S(2)}, u32[]{:S(2)}) collective-permute-start(bf16[768,512]{1,0:T(8,128)(2,1)} %get-tuple-element.49.refs_2_), channel_id=1, source_target_pairs={{4,8},{8,4},{5,9},{9,5},{6,10},{10,6},{7,11},{11,7},{20,24},{24,20... | collective-permute-start | bytes 2359304 | tf_op jit(solution)/shard_map/ppermute | solution.py:44
  46.6 19.9 %collective-permute-start.9 = (bf16[768,512]{1,0:T(8,128)(2,1)}, bf16[768,512]{1,0:T(8,128)(2,1)}, u32[]{:S(2)}, u32[]{:S(2)}) collective-permute-start(bf16[768,512]{1,0:T(8,128)(2,1)} %get-tuple-element.49.refs_2_), channel_id=1, source_target_pairs={{0,4},{8,12},{4,0},{12,8},{1,5},{9,13},{5,1},{13,9},{2,6},{10,14},... | collective-permute-start | bytes 2359304 | tf_op jit(solution)/shard_map/ppermute | solution.py:44
  49.6 28.2 %slice-start = ((s8[4718592]{0:T(1024)(128)(4,1)}), s8[524288]{0:T(1024)(128)(4,1)S(1)}, s32[]{:S(2)}) async-start(s8[4718592]{0:T(1024)(128)(4,1)} %bitcast.15), calls=%async_computation | async-start | bytes 1048576
  54.1 3.0 %collective-permute-start.8 = (bf16[384,256]{1,0:T(8,128)(2,1)S(1)}, bf16[384,256]{1,0:T(8,128)(2,1)S(1)}, u32[]{:S(2)}, u32[]{:S(2)}) collective-permute-start(bf16[384,256]{1,0:T(8,128)(2,1)S(1)} %get-tuple-element.48), channel_id=1, source_target_pairs={{0,1},{1,0},{2,3},{3,2},{4,5},{5,4},{6,7},{7,6},{8,9},{9,8},{10,11... | collective-permute-start | bytes 589832 | tf_op jit(solution)/shard_map/ppermute | solution.py:39
  57.8 0.7 copy-start.6
  58.6 10.6 %collective-permute-start.12 = (bf16[384,512]{1,0:T(8,128)(2,1)}, bf16[384,512]{1,0:T(8,128)(2,1)}, u32[]{:S(2)}, u32[]{:S(2)}) collective-permute-start(bf16[384,512]{1,0:T(8,128)(2,1)} %constant_dynamic-update-slice_fusion.2.refs_1_), channel_id=1, source_target_pairs={{0,2},{2,0},{1,3},{3,1},{4,6},{6,4},{5,7},{7,5},{8,10},{10,8},{9,1... | collective-permute-start | bytes 1179656 | tf_op jit(solution)/shard_map/ppermute | solution.py:352
  59.1 2.3 %copy-start = (bf16[1536,1536]{1,0:T(8,128)(2,1)S(1)}, bf16[1536,1536]{1,0:T(8,128)(2,1)}, u32[]{:S(2)}) copy-start(bf16[1536,1536]{1,0:T(8,128)(2,1)} %constant_dynamic-slice_fusion.1.refs_2_) | copy-start | bytes 14155780
  61.4 9.0 %copy-start.2 = (bf16[768,768]{1,0:T(8,128)(2,1)S(1)}, bf16[768,768]{1,0:T(8,128)(2,1)}, u32[]{:S(2)}) copy-start(bf16[768,768]{1,0:T(8,128)(2,1)} %copy-done.1) | copy-start | bytes 3538948
  61.4 16.4 %slice-start.1 = ((s8[4718592]{0:T(1024)(128)(4,1)}), s8[4194304]{0:T(1024)(128)(4,1)S(1)}, s32[]{:S(2)}) async-start(s8[4718592]{0:T(1024)(128)(4,1)} %bitcast.15), calls=%async_computation.1 | async-start | bytes 8388608
  64.4 13.5 %copy-start.8 = (f32[1536]{0:T(1024)S(1)}, f32[1536]{0:T(1024)}, u32[]{:S(2)}) copy-start(f32[1536]{0:T(1024)} %param.13) | copy-start | bytes 18436
  64.4 13.5 %copy-start.7 = (bf16[384,512]{1,0:T(8,128)(2,1)S(1)}, bf16[384,512]{1,0:T(8,128)(2,1)}, u32[]{:S(2)}) copy-start(bf16[384,512]{1,0:T(8,128)(2,1)} %copy-done.6) | copy-start | bytes 1179652
  69.2 8.7 %collective-permute-start.15 = (bf16[1536,384]{1,0:T(8,128)(2,1)}, bf16[1536,384]{1,0:T(8,128)(2,1)S(1)}, u32[]{:S(2)}, u32[]{:S(2)}) collective-permute-start(bf16[1536,384]{1,0:T(8,128)(2,1)} %collective-permute-done.4.refs_5_.refs_3_), channel_id=1, source_target_pairs={{0,1},{1,0},{2,3},{3,2},{4,5},{5,4},{6,7},{7,6},{8,9},{9,8},{10,11... | collective-permute-start | bytes 3538952 | tf_op jit(solution)/shard_map/ppermute | solution.py:39
  70.4 7.5 %collective-permute-start.16 = (bf16[1536,384]{1,0:T(8,128)(2,1)}, bf16[1536,384]{1,0:T(8,128)(2,1)S(1)}, u32[]{:S(2)}, u32[]{:S(2)}) collective-permute-start(bf16[1536,384]{1,0:T(8,128)(2,1)} %collective-permute-done.13.refs_7_.refs_5_), channel_id=1, source_target_pairs={{0,1},{1,0},{2,3},{3,2},{4,5},{5,4},{6,7},{7,6},{8,9},{9,8},{10,11... | collective-permute-start | bytes 3538952 | tf_op jit(solution)/shard_map/ppermute | solution.py:39
  75.7 1.6 %collective-permute-start.14 = (bf16[384,256]{1,0:T(8,128)(2,1)S(1)}, bf16[384,256]{1,0:T(8,128)(2,1)S(1)}, u32[]{:S(2)}, u32[]{:S(2)}) collective-permute-start(bf16[384,256]{1,0:T(8,128)(2,1)S(1)} %get-tuple-element.57), channel_id=1, source_target_pairs={{0,1},{1,0},{2,3},{3,2},{4,5},{5,4},{6,7},{7,6},{8,9},{9,8},{10,11... | collective-permute-start | bytes 589832 | tf_op jit(solution)/shard_map/ppermute | solution.py:39
  77.3 10.4 %collective-permute-start.17 = (bf16[384,512]{1,0:T(8,128)(2,1)S(1)}, bf16[384,512]{1,0:T(8,128)(2,1)S(1)}, u32[]{:S(2)}, u32[]{:S(2)}) collective-permute-start(bf16[384,512]{1,0:T(8,128)(2,1)S(1)} %constant_dynamic-update-slice_fusion.4.refs_1_), channel_id=1, source_target_pairs={{0,2},{2,0},{1,3},{3,1},{4,6},{6,4},{5,7},{7,5},{8,10},{10,8},{9,1... | collective-permute-start | bytes 1179656 | tf_op jit(solution)/shard_map/ppermute | solution.py:352

commit v3 on v2

--- a/solution.py
+++ b/solution.py
@@ -48,38 +48,36 @@
     return lax.optimization_barrier((value, *earlier))[0]
 
 
-def pack_kernel(inputs, cuts, *refs):
-    operands, outputs, sems = refs[:inputs], refs[inputs:-1], refs[-1]
-    copies = []
-    for out, runs in zip(outputs, cuts):
-        at = 0
-        for index, start_of, offset, width in runs:
-            begin = start_of() + offset
-            for step in range(0, width, HD):
-                start = pl.multiple_of(begin + step, HD)
-                copies.append(
-                    pltpu.make_async_copy(
-                        operands[index].at[:, pl.ds(start, HD)], out.at[:, at : at + HD], sems.at[len(copies)]
-                    )
-                )
-                at += HD
-    for copy in copies:
+def pack_kernel(inputs, runs, *refs):
+    operands, out, held, sems = refs[:inputs], *refs[inputs:]
+    arriving, leaving = [], []
+    other_half = (1 - lax.axis_index("sub")) * (operands[0].shape[1] // 2)
+    for index, offset, width in runs:
+        for step in range(0, width, HD):
+            n = len(arriving)
+            start = pl.multiple_of(other_half + (offset + step), HD)
+            place = (slice(None), slice(n * HD, (n + 1) * HD))
+            arriving.append(
+                pltpu.make_async_copy(operands[index].at[:, pl.ds(start, HD)], held.at[place], sems.at[0, n])
+            )
+            leaving.append(pltpu.make_async_copy(held.at[place], out.at[place], sems.at[1, n]))
+    for copy in arriving:
         copy.start()
-    for copy in copies:
+    for arrival, departure in zip(arriving, leaving):
+        arrival.wait()
+        departure.start()
+    for copy in leaving:
         copy.wait()
 
 
-def pack(operands, cuts):
-    shapes = [
-        jax.ShapeDtypeStruct((operands[runs[0][0]].shape[0], sum(run[3] for run in runs)), jnp.bfloat16)
-        for runs in cuts
-    ]
+def pack(operands, runs):
+    shape = (operands[0].shape[0], sum(width for _, _, width in runs))
     return pl.pallas_call(
-        functools.partial(pack_kernel, len(operands), cuts),
+        functools.partial(pack_kernel, len(operands), runs),
         in_specs=[HBM_SPEC] * len(operands),
-        out_specs=[VMEM_SPEC] * len(shapes),
-        out_shape=shapes,
-        scratch_shapes=[pltpu.SemaphoreType.DMA((sum(run[3] // HD for runs in cuts for run in runs),))],
+        out_specs=HBM_SPEC,
+        out_shape=jax.ShapeDtypeStruct(shape, jnp.bfloat16),
+        scratch_shapes=[pltpu.VMEM(shape, jnp.bfloat16), pltpu.SemaphoreType.DMA((2, shape[1] // HD))],
         compiler_params=pltpu.CompilerParams(vmem_limit_bytes=PACK_BYTES),
     )(*operands)
 
@@ -202,19 +200,16 @@
     )(*scalars, *operands)
 
 
-def project_kernel(splits, groups, carried, gated, place_ref, *refs):
+def project_kernel(splits, groups, carried, late, place_ref, *refs):
     refs = list(refs)
-    if gated:
-        held, sems = refs.pop(-2), refs.pop(-1)
+    weights_out = refs.pop() if late else None
     out = refs.pop()
-    copies = []
     total_ref = refs.pop(0) if carried else None
-    gate_ref = refs.pop(0) if gated else None
     block = out.shape[1] // splits
     for j in range(splits):
         where = pl.ds(pl.multiple_of(place_ref[j] * block, HD), block)
         total = total_ref[:, where] if carried else None
-        at = 0
+        at = row = 0
         for runs, arrays, pieces in groups:
             weights = refs[at + arrays : at + arrays + max(pieces, 1)]
             for index, column, place, offset, depth in runs:
@@ -223,34 +218,65 @@
                 left = refs[at + index][:, column : column + depth]
                 term = jnp.dot(left, right, preferred_element_type=jnp.float32)
                 total = term if total is None else total + term
+            for place, offset, depth in late if pieces else ():
+                rows = pl.ds(pl.multiple_of(place_ref[place] + offset, HD), depth)
+                weights_out[row : row + depth, where] = weights[j][rows, :]
+                row += depth
             at += arrays + max(pieces, 1)
-        if gated:
-            held[:, j * block : (j + 1) * block] = (total * gate_ref[:, where]).astype(out.dtype)
-            source = held.at[:, j * block : (j + 1) * block]
-            copies.append(pltpu.make_async_copy(source, out.at[:, where], sems.at[j]))
-            copies[-1].start()
-        else:
-            out[:, where] = total
-    for copy in copies:
-        copy.wait()
-
-
-def project(places, splits, groups, width, total=None, gate=None):
-    operands = [a for a in (total, gate) if a is not None]
+        out[:, where] = total
+
+
+def project(places, splits, groups, width, total=None, late=()):
+    operands = [] if total is None else [total]
     plan = []
     for runs, arrays, weights, whole in groups:
         plan.append((runs, len(arrays), 0 if whole else len(weights)))
         operands += [*arrays, *weights]
     rows = groups[0][1][0].shape[0]
-    scratch = [pltpu.VMEM((rows, width), jnp.bfloat16), pltpu.SemaphoreType.DMA((splits,))]
+    shapes = [jax.ShapeDtypeStruct((rows, width), jnp.float32)]
+    if late:
+        depth = sum(depth for _, _, depth in late) * sum(not whole for *_, whole in groups)
+        shapes.append(jax.ShapeDtypeStruct((depth, width), jnp.bfloat16))
     return pl.pallas_call(
-        functools.partial(project_kernel, splits, plan, total is not None, gate is not None),
+        functools.partial(project_kernel, splits, plan, total is not None, late),
         in_specs=[SMEM_SPEC] + [VMEM_SPEC] * len(operands),
-        out_specs=VMEM_SPEC if gate is None else HBM_SPEC,
-        out_shape=jax.ShapeDtypeStruct((rows, width), jnp.float32 if gate is None else jnp.bfloat16),
-        scratch_shapes=scratch if gate is not None else [],
+        out_specs=[VMEM_SPEC] * len(shapes),
+        out_shape=shapes,
         compiler_params=pltpu.CompilerParams(vmem_limit_bytes=PROJECT_BYTES),
     )(places, *operands)
+
+
+def close_kernel(blocks, total_ref, weights_ref, gate_ref, *refs):
+    *parts, out, held, sems = refs
+    block = out.shape[1] // blocks
+    copies = []
+    for j in range(blocks):
+        where = slice(j * block, (j + 1) * block)
+        total = total_ref[:, where]
+        row = 0
+        for part in parts:
+            depth = part.shape[1]
+            right = weights_ref[row : row + depth, where]
+            total = total + jnp.dot(part[...], right, preferred_element_type=jnp.float32)
+            row += depth
+        held[:, where] = (total * gate_ref[:, where]).astype(out.dtype)
+        copies.append(pltpu.make_async_copy(held.at[:, where], out.at[:, where], sems.at[j]))
+        copies[-1].start()
+    for copy in copies:
+        copy.wait()
+
+
+def close(total, weights, parts, gate):
+    rows, width = total.shape
+    blocks = max(width // (4 * HD), 1)
+    return pl.pallas_call(
+        functools.partial(close_kernel, blocks),
+        in_specs=[VMEM_SPEC] * (3 + len(parts)),
+        out_specs=HBM_SPEC,
+        out_shape=jax.ShapeDtypeStruct((rows, width), jnp.bfloat16),
+        scratch_shapes=[pltpu.VMEM((rows, width), jnp.bfloat16), pltpu.SemaphoreType.DMA((blocks,))],
+        compiler_params=pltpu.CompilerParams(vmem_limit_bytes=PROJECT_BYTES),
+    )(total, weights, gate, *parts)
 
 
 def local(queries, keys, values, kv_list, kv_count, out_weight, gate):
@@ -296,24 +322,18 @@
     runs_of = [((2, 0, span),)]
     for first, count in chunks:
         runs_of.append(tuple((index, first * HD, count * HD) for index in (0, 1)))
-    cuts, low = [], 0
-    for runs in runs_of:
-        cuts.append((low, runs))
-        low += sum(size for _, _, size in runs)
-
-    def other_half():
-        return (1 - lax.axis_index("sub")) * span
-
-    cut = tuple((index, other_half, offset, size) for runs in runs_of for index, offset, size in runs)
-    (other,) = pack((keys, values, queries), (cut,))
-    found = other_core(other)
+    wide = [sum(size for _, _, size in runs) for runs in runs_of]
+    lows = [sum(wide[:i]) for i in range(len(wide))]
+
+    found = other_core(pack((keys, values, queries), sum(runs_of, ())))
     sent = [
         lax.dynamic_slice(out_weight, (0, lax.rem(x + d, n_head) * width + piece * block), (2 * span, block))
         for d in range(1, n_head)
     ]
-    first_message = join((keys, values), found, span, cuts[1:2])
-    queries, *message = join((keys, values, queries), found, span, [cuts[0], *cuts[2:]])
-    message = [*first_message, *message]
+    cuts = list(zip(lows, runs_of))
+    message = join((keys, values), found, span, cuts[1:2])
+    queries, *late = join((keys, values, queries), found, span, [cuts[0], *cuts[2:]])
+    message = [*message, *late]
     near = [to_neighbours(message[0])]
     lists = jnp.concatenate([lists, other_core(lists)], axis=0)
     scalars = (jnp.stack(tiles).astype(jnp.int32), lists)
@@ -347,6 +367,8 @@
     for i, (first, _) in enumerate(chunks):
         plan = plan_of(i, [(index, row) for index in (0, 1) for row in (0, rows)])
         kept, given = attend(first, plan, 2, scalars, queries, near[i], prior)
+        if i == last:
+            break
         ours.append(jnp.concatenate([kept, other_core(given)], axis=1))
         leaving = after(ours[i], moved) if i else ours[i]
         moved.append([lax.ppermute(leaving, "head", ring(n_head, d)) for d in range(1, n_head)])
@@ -355,15 +377,19 @@
         if i == 0:
             near[1] = after(near[1], kept, ours[0])
         if i == last - 1:
-            total = project(places, splits, [(runs(range(last)), ours[:], [mine], True)], width)
+            (total,) = project(places, splits, [(runs(range(last)), ours, [mine], True)], width)
             near[last], spread = lax.optimization_barrier((after(near[last], total, moved), spread))
     pieces = [[a for got in gots for a in (got, other_core(got))] if splits > 1 else gots for gots in spread]
 
-    groups = [(runs([last]), [ours[last]], [mine], True)]
+    parts = []
+    for d in range(1, n_head):
+        across = [(h * subs + s, ((h + d) % n_head) * subs + 1 - s) for h in range(n_head) for s in range(subs)]
+        parts += [lax.ppermute(kept, "head", ring(n_head, d)), lax.ppermute(given, ("head", "sub"), across)]
+    late = [(side, 0, splits + side, chunks[last][0] * HD, chunks[last][1] * HD) for side in (0, 1)]
+    groups = [(late, [kept, other_core(given)], [mine], True)]
     groups += [(runs(range(last)), [moved[i][d] for i in range(last)], pieces[d], False) for d in range(n_head - 1)]
-    total = project(places, splits, groups, width, total)
-    groups = [(runs([last]), [moved[last][d]], pieces[d], False) for d in range(n_head - 1)]
-    return project(places, splits, groups, width, total, gate.reshape(1, width))
+    total, weights = project(places, splits, groups, width, total, [late_run[2:] for late_run in late])
+    return close(total, weights, parts, gate.reshape(1, width))
 
 
 def solution(mesh):

time: 92.8 us -> 89.7 us (0.967); the launches traced: 91.3 us -> 89.2 us
  Pallas kernels: 40.1 us -> 38 us
  starting transfers between devices: 20.2 us -> 22.2 us
  waiting for transfers between devices: 17.7 us -> 15.8 us
    ppermute x0 -> x2, waiting for transfers between devices: none -> 4.62 us  [the longest x1 4.37 us: local(): lax.ppermute(given, ('head', 'sub'), across)]
    ppermute x3 -> x2, waiting for transfers between devices: 8.09 us -> 4.47 us  [local(): lax.ppermute(leaving, 'head', ring(n_head, d))]
    pallas_call x3 -> x2, Pallas kernels: 10.7 us -> 7.38 us  [project(): pl.pallas_call(functools.partial(project_kernel, splits, plan, total is n...]
    ppermute x0 -> x2, starting transfers between devices: none -> 1.71 us  [the longest x1 1.23 us: local(): lax.ppermute(given, ('head', 'sub'), across)]
    ppermute x6, waiting for transfers between devices: 5.13 us -> 3.52 us  [to_neighbours(): lax.ppermute(block, 'seq', pairing(length, start))]
    pallas_call x1 -> x2, Pallas kernels: 2.91 us -> 4.15 us  [the longest x1 2.59 us: pack(): pl.pallas_call(functools.partial(pack_kernel, len(operands), runs), in_sp...]
    ppermute x7, waiting for transfers between devices: 3.22 us -> 2.16 us  [other_core(): return lax.ppermute(block, 'sub', [(0, 1), (1, 0)])]
    ppermute x3 -> x2, starting transfers between devices: 2.26 us -> 1.74 us  [local(): lax.ppermute(leaving, 'head', ring(n_head, d))]
  transfers between devices with their start and end apart: 18 -> 19, of which waited for: 11 -> 9; matrix products, arithmetic and copies ran while one was open for 10% -> 10% of each run, Pallas kernels for 37% -> 38%
where the time goes in v3:
time: 89.7 us; the launch traced here: 89.2 us
  Pallas kernels  38 us (42%)
  starting transfers between devices  22.2 us (25%)
  waiting for transfers between devices  15.8 us (18%)
  local copies, waits for them, and re-layouts  12 us (13%)
  between operations  1.08 us (1%)
    pallas_call x4, Pallas kernels, attend(): pl.pallas_call(functools.partial(attention_kernel, first, plan, base, mer...  21.4 us
    ppermute x6, starting transfers between devices, to_neighbours(): lax.ppermute(block, 'seq', pairing(length, start))  9.94 us
    pallas_call x2, Pallas kernels, project(): pl.pallas_call(functools.partial(project_kernel, splits, plan, total is n...  7.38 us
    ppermute x7, starting transfers between devices, other_core(): return lax.ppermute(block, 'sub', [(0, 1), (1, 0)])  7.35 us
    pallas_call x2, Pallas kernels, join(): pl.pallas_call(functools.partial(join_kernel, span, cuts), in_specs=[VMEM...  5.02 us
    dynamic_slice x1, local copies, waits for them, and re-layouts, local(): lax.dynamic_slice(after(out_weight, prior), (0, x * width), (2 * span, wi...  4.8 us
    ppermute x2, waiting for transfers between devices, local(): lax.ppermute(leaving, 'head', ring(n_head, d))  4.47 us
    ppermute x1, waiting for transfers between devices, local(): lax.ppermute(given, ('head', 'sub'), across)  4.37 us
  transfers between devices with their start and end apart: 19, of which 9 were waited for; matrix products, arithmetic and copies ran while one was open for 10% of the time, Pallas kernels for 38%

profile of v3, /device:TPU:13, one launch (start us, length us, event | category | flops | bytes accessed | tf_op | source)
XLA Modules:
  0.0 89.2 jit_solution(12868222661489590386)
XLA Ops:
  0.0 2.6 %shard_map.73 = bf16[384,2304]{1,0:T(8,128)(2,1)} custom-call(bf16[384,1536]{1,0:T(8,128)(2,1)} %refs_0_.5, bf16[384,1536]{1,0:T(8,128)(2,1)} %refs_1_.5, bf16[384,1536]{1,0:T(8,128)(2,1)} %refs_2_.3), custom_call_target="tpu_custom_call" | custom-call | tf_op jit(solution)/shard_map/pallas_call | solution.py:75
  2.6 0.0 copy-start.3
  2.6 0.0 copy-start.4
  2.6 0.7 collective-permute-start.1
  3.4 2.4 %constant_dynamic-slice_fusion = bf16[1536,384]{1,0:T(8,128)(2,1)} fusion(bf16[1536,3072]{1,0:T(8,128)(2,1)} %param.12, s32[]{:T(128)S(6)} %select_n.32), kind=kLoop, calls=%fused_computation.6 | loop fusion | bytes 2359300 | tf_op jit(solution)/shard_map/dynamic_slice | solution.py:330
  5.8 1.2 %collective-permute-start.4 = (bf16[1536,384]{1,0:T(8,128)(2,1)}, bf16[1536,384]{1,0:T(8,128)(2,1)}, u32[]{:S(2)}, u32[]{:S(2)}) collective-permute-start(bf16[1536,384]{1,0:T(8,128)(2,1)} %constant_dynamic-slice_fusion), channel_id=1, source_target_pairs={{0,2},{2,0},{1,3},{3,1},{4,6},{6,4},{5,7},{7,5},{8,10},{10,8},{9,1... | collective-permute-start | bytes 3538952 | tf_op jit(solution)/shard_map/ppermute | solution.py:342
  7.7 2.5 %shard_map.75.refs_0_ = bf16[768,512]{1,0:T(8,128)(2,1)} custom-call(bf16[384,1536]{1,0:T(8,128)(2,1)S(1)} %copy-done.3, bf16[384,1536]{1,0:T(8,128)(2,1)S(1)} %copy-done.4, bf16[384,2304]{1,0:T(8,128)(2,1)} %collective-permute-done.1.refs_3_.refs_2_), custom_call_target="tpu_custom_call" | custom-call | tf_op jit(solution)/shard_map/pallas_call | solution.py:101
  10.2 0.2 collective-permute-start.2
  10.4 4.3 %collective-permute-start.3 = (bf16[768,512]{1,0:T(8,128)(2,1)}, bf16[768,512]{1,0:T(8,128)(2,1)}, u32[]{:S(2)}, u32[]{:S(2)}) collective-permute-start(bf16[768,512]{1,0:T(8,128)(2,1)} %shard_map.75.refs_0_), channel_id=1, source_target_pairs={{4,8},{8,4},{5,9},{9,5},{6,10},{10,6},{7,11},{11,7},{20,24},{24,20... | collective-permute-start | bytes 2359304 | tf_op jit(solution)/shard_map/ppermute | solution.py:44
  14.7 0.1 pad_add_fusion.1
  14.8 1.0 %collective-permute-start = (s32[1,7]{1,0:T(1,128)S(1)}, s32[1,7]{1,0:T(1,128)S(1)}, u32[]{:S(2)}, u32[]{:S(2)}) collective-permute-start(s32[1,7]{1,0:T(1,128)S(1)} %pad_add_fusion.1), channel_id=1, source_target_pairs={{0,1},{1,0},{2,3},{3,2},{4,5},{5,4},{6,7},{7,6},{8,9},{9,8},{10,11... | collective-permute-start | bytes 92 | tf_op jit(solution)/shard_map/ppermute | solution.py:39
  15.8 0.1 stack.55.tiles_ref
  15.9 0.7 collective-permute-done
  16.7 0.1 pad_add_fusion.lists_ref
  16.7 2.5 %shard_map.74 = (bf16[768,768]{1,0:T(8,128)(2,1)S(1)}, bf16[768,512]{1,0:T(8,128)(2,1)S(1)}, bf16[768,512]{1,0:T(8,128)(2,1)}) custom-call(bf16[384,1536]{1,0:T(8,128)(2,1)S(1)} %copy-done.3, bf16[384,1536]{1,0:T(8,128)(2,1)S(1)} %copy-done.4, bf16[384,1536]{1,0:T(8,128)(2,1)S(1)} %copy-done.5, bf16[384,2304]{1,0:T(8,128)(2,1)} %collective-permute-done.1.refs_3_.refs_2_), custom_call_target="tpu_custom_call" | custom-call | tf_op jit(solution)/shard_map/pallas_call | solution.py:101
  19.2 1.9 %collective-permute-start.7 = (bf16[768,512]{1,0:T(8,128)(2,1)S(1)}, bf16[768,512]{1,0:T(8,128)(2,1)S(1)}, u32[]{:S(2)}, u32[]{:S(2)}) collective-permute-start(bf16[768,512]{1,0:T(8,128)(2,1)S(1)} %get-tuple-element.35.refs_1_), channel_id=1, source_target_pairs={{4,8},{8,4},{5,9},{9,5},{6,10},{10,6},{7,11},{11,7},{20,24},{24,20... | collective-permute-start | bytes 2359304 | tf_op jit(solution)/shard_map/ppermute | solution.py:44
  21.1 6.4 %shard_map.76 = (f32[768,768]{1,0:T(8,128)S(1)}, f32[8,768]{1,0:T(8,128)S(1)}) custom-call(s32[6]{0:T(128)S(1)} %stack.55.tiles_ref, s32[2,7]{1,0:T(2,128)S(1)} %pad_add_fusion.lists_ref, bf16[768,768]{1,0:T(8,128)(2,1)S(1)} %get-tuple-element.34.queries, bf16[768,512]{1,0:T(8,128)(2,1)} %shard_map.75.refs_0_, ...), custom_call_target="tpu_custom_call" | custom-call | tf_op jit(solution)/shard_map/pallas_call | solution.py:194
  27.6 4.8 %constant_dynamic-slice_fusion.1.refs_2_.refs_3_ = bf16[1536,1536]{1,0:T(8,128)(2,1)} fusion(bf16[1536,3072]{1,0:T(8,128)(2,1)} %param.12, s32[]{:T(128)S(6)} %select_n.31), kind=kLoop, calls=%fused_computation.7 | loop fusion | bytes 9437188 | tf_op jit(solution)/shard_map/dynamic_slice | solution.py:357
  32.4 1.1 %collective-permute-done.4.refs_6_ = bf16[1536,384]{1,0:T(8,128)(2,1)} collective-permute-done((bf16[1536,384]{1,0:T(8,128)(2,1)}, bf16[1536,384]{1,0:T(8,128)(2,1)}, u32[]{:S(2)}, u32[]{:S(2)}) %collective-permute-start.4) | collective-permute-done | bytes 1179680 | tf_op jit(solution)/shard_map/ppermute | solution.py:342
  33.5 0.2 collective-permute-start.13
  33.7 5.2 %shard_map.77 = (bf16[384,256]{1,0:T(8,128)(2,1)S(1)}, bf16[384,256]{1,0:T(8,128)(2,1)S(1)}) custom-call(s32[6]{0:T(128)S(1)} %stack.55.tiles_ref, s32[2,7]{1,0:T(2,128)S(1)} %pad_add_fusion.lists_ref, bf16[768,768]{1,0:T(8,128)(2,1)S(1)} %get-tuple-element.34.queries, bf16[768,512]{1,0:T(8,128)(2,1)} %collective-permute-done.2.refs_0_, ...), custom_call_target="tpu_custom_call" | custom-call | tf_op jit(solution)/shard_map/pallas_call | solution.py:194
  39.0 1.3 %collective-permute-start.5 = (bf16[384,256]{1,0:T(8,128)(2,1)S(1)}, bf16[384,256]{1,0:T(8,128)(2,1)S(1)}, u32[]{:S(2)}, u32[]{:S(2)}) collective-permute-start(bf16[384,256]{1,0:T(8,128)(2,1)S(1)} %get-tuple-element.45), channel_id=1, source_target_pairs={{0,1},{1,0},{2,3},{3,2},{4,5},{5,4},{6,7},{7,6},{8,9},{9,8},{10,11... | collective-permute-start | bytes 589832 | tf_op jit(solution)/shard_map/ppermute | solution.py:39
  40.3 1.1 %collective-permute-done.5 = bf16[384,256]{1,0:T(8,128)(2,1)S(1)} collective-permute-done((bf16[384,256]{1,0:T(8,128)(2,1)S(1)}, bf16[384,256]{1,0:T(8,128)(2,1)S(1)}, u32[]{:S(2)}, u32[]{:S(2)}) %collective-permute-start.5) | collective-permute-done | bytes 196640 | tf_op jit(solution)/shard_map/ppermute | solution.py:39
  41.4 1.3 %collective-permute-start.11 = (bf16[384,512]{1,0:T(8,128)(2,1)S(1)}, bf16[384,512]{1,0:T(8,128)(2,1)S(1)}, u32[]{:S(2)}, u32[]{:S(2)}) collective-permute-start(bf16[384,512]{1,0:T(8,128)(2,1)S(1)} %constant_dynamic-update-slice_fusion.refs_0_), channel_id=1, source_target_pairs={{0,2},{2,0},{1,3},{3,1},{4,6},{6,4},{5,7},{7,5},{8,10},{10,8},{9,1... | collective-permute-start | bytes 1179656 | tf_op jit(solution)/shard_map/ppermute | solution.py:374
  42.7 0.2 collective-permute-start.9
  42.8 3.2 %collective-permute-done.6.refs_0_ = bf16[768,512]{1,0:T(8,128)(2,1)S(1)} collective-permute-done((bf16[768,512]{1,0:T(8,128)(2,1)S(1)}, bf16[768,512]{1,0:T(8,128)(2,1)S(1)}, u32[]{:S(2)}, u32[]{:S(2)}) %collective-permute-start.6) | collective-permute-done | bytes 786464 | tf_op jit(solution)/shard_map/ppermute | solution.py:44
  46.0 3.4 %collective-permute-start.10 = (bf16[768,512]{1,0:T(8,128)(2,1)}, bf16[768,512]{1,0:T(8,128)(2,1)}, u32[]{:S(2)}, u32[]{:S(2)}) collective-permute-start(bf16[768,512]{1,0:T(8,128)(2,1)} %get-tuple-element.50.refs_2_), channel_id=1, source_target_pairs={{4,8},{8,4},{5,9},{9,5},{6,10},{10,6},{7,11},{11,7},{20,24},{24,20... | collective-permute-start | bytes 2359304 | tf_op jit(solution)/shard_map/ppermute | solution.py:44
  49.4 4.5 %shard_map.78 = (bf16[384,256]{1,0:T(8,128)(2,1)S(1)}, bf16[384,256]{1,0:T(8,128)(2,1)S(1)}) custom-call(s32[6]{0:T(128)S(1)} %stack.55.tiles_ref, s32[2,7]{1,0:T(2,128)S(1)} %pad_add_fusion.lists_ref, bf16[768,768]{1,0:T(8,128)(2,1)S(1)} %get-tuple-element.34.queries, bf16[768,512]{1,0:T(8,128)(2,1)S(1)} %collective-permute-done.6.refs_0_, ...), custom_call_target="tpu_custom_call" | custom-call | tf_op jit(solution)/shard_map/pallas_call | solution.py:194
  53.9 2.5 %collective-permute-start.8 = (bf16[384,256]{1,0:T(8,128)(2,1)S(1)}, bf16[384,256]{1,0:T(8,128)(2,1)S(1)}, u32[]{:S(2)}, u32[]{:S(2)}) collective-permute-start(bf16[384,256]{1,0:T(8,128)(2,1)S(1)} %get-tuple-element.49), channel_id=1, source_target_pairs={{0,1},{1,0},{2,3},{3,2},{4,5},{5,4},{6,7},{7,6},{8,9},{9,8},{10,11... | collective-permute-start | bytes 589832 | tf_op jit(solution)/shard_map/ppermute | solution.py:39
  56.4 0.7 constant_dynamic-update-slice_fusion.3
  57.1 0.4 collective-permute-done.8
  57.5 0.7 constant_dynamic-update-slice_fusion.2.refs_1_
  58.2 0.8 copy-done.6
  59.0 0.5 collective-permute-start.12
  59.4 0.1 stack.48.place_ref
  59.5 2.3 %copy-done = bf16[1536,1536]{1,0:T(8,128)(2,1)S(1)} copy-done((bf16[1536,1536]{1,0:T(8,128)(2,1)S(1)}, bf16[1536,1536]{1,0:T(8,128)(2,1)}, u32[]{:S(2)}) %copy-start) | copy-done | bytes 4718616
  61.9 2.9 %shard_map.79.refs_0_ = f32[384,1536]{1,0:T(8,128)S(1)} custom-call(s32[6]{0:T(128)S(1)} %stack.48.place_ref, bf16[384,512]{1,0:T(8,128)(2,1)S(1)} %constant_dynamic-update-slice_fusion.refs_0_, bf16[384,512]{1,0:T(8,128)(2,1)} %constant_dynamic-update-slice_fusion.2.refs_1_, bf16[1536,1536]{1,0:T(8,128)(2,1)S(1)} %copy-done), custom_call_target="tpu_custom_call" | custom-call | tf_op jit(solution)/shard_map/pallas_call | solution.py:240
  64.9 0.3 collective-permute-done.10.refs_1_
  65.2 4.5 %collective-permute-done.12.refs_5_ = bf16[384,512]{1,0:T(8,128)(2,1)} collective-permute-done((bf16[384,512]{1,0:T(8,128)(2,1)}, bf16[384,512]{1,0:T(8,128)(2,1)}, u32[]{:S(2)}, u32[]{:S(2)}) %collective-permute-start.12) | collective-permute-done | bytes 393248 | tf_op jit(solution)/shard_map/ppermute | solution.py:374
  69.6 1.2 %collective-permute-start.15 = (bf16[1536,384]{1,0:T(8,128)(2,1)}, bf16[1536,384]{1,0:T(8,128)(2,1)S(1)}, u32[]{:S(2)}, u32[]{:S(2)}) collective-permute-start(bf16[1536,384]{1,0:T(8,128)(2,1)} %collective-permute-done.4.refs_6_), channel_id=1, source_target_pairs={{0,1},{1,0},{2,3},{3,2},{4,5},{5,4},{6,7},{7,6},{8,9},{9,8},{10,11... | collective-permute-start | bytes 3538952 | tf_op jit(solution)/shard_map/ppermute | solution.py:39
  70.8 5.2 %shard_map.80 = (bf16[384,256]{1,0:T(8,128)(2,1)S(1)}, bf16[384,256]{1,0:T(8,128)(2,1)S(1)}) custom-call(s32[6]{0:T(128)S(1)} %stack.55.tiles_ref, s32[2,7]{1,0:T(2,128)S(1)} %pad_add_fusion.lists_ref, bf16[768,768]{1,0:T(8,128)(2,1)S(1)} %copy-done.2, bf16[768,512]{1,0:T(8,128)(2,1)} %collective-permute-done.9.refs_0_, ...), custom_call_target="tpu_custom_call" | custom-call | tf_op jit(solution)/shard_map/pallas_call | solution.py:194
  76.1 0.6 collective-permute-start.14
  76.6 0.5 collective-permute-start.17
  77.1 1.2 %collective-permute-start.18 = (bf16[384,256]{1,0:T(8,128)(2,1)S(1)}, bf16[384,256]{1,0:T(8,128)(2,1)S(1)}, u32[]{:S(2)}, u32[]{:S(2)}) collective-permute-start(bf16[384,256]{1,0:T(8,128)(2,1)S(1)} %get-tuple-element.58), channel_id=1, source_target_pairs={{0,3},{1,2},{2,1},{3,0},{4,7},{5,6},{6,5},{7,4},{8,11},{9,10},{10,... | collective-permute-start | bytes 589832 | tf_op jit(solution)/shard_map/ppermute | solution.py:387
  78.4 4.4 %shard_map.81 = (f32[384,1536]{1,0:T(8,128)S(1)}, bf16[512,1536]{1,0:T(8,128)(2,1)S(1)}) custom-call(s32[6]{0:T(128)S(1)} %stack.48.place_ref, f32[384,1536]{1,0:T(8,128)S(1)} %shard_map.79.refs_0_, bf16[384,256]{1,0:T(8,128)(2,1)S(1)} %get-tuple-element.57.refs_1_, bf16[384,256]{1,0:T(8,128)(2,1)S(1)} %collective-permute-done.14.refs_2_, ...), custom_call_target="tpu_custom_call" | custom-call | tf_op jit(solution)/shard_map/pallas_call | solution.py:240
  82.9 0.2 collective-permute-done.17.refs_0_
  83.1 4.4 %collective-permute-done.18.refs_1_ = bf16[384,256]{1,0:T(8,128)(2,1)S(1)} collective-permute-done((bf16[384,256]{1,0:T(8,128)(2,1)S(1)}, bf16[384,256]{1,0:T(8,128)(2,1)S(1)}, u32[]{:S(2)}, u32[]{:S(2)}) %collective-permute-start.18) | collective-permute-done | bytes 196640 | tf_op jit(solution)/shard_map/ppermute | solution.py:387
  87.5 1.6 %shard_map.82 = bf16[384,1536]{1,0:T(8,128)(2,1)} custom-call(f32[384,1536]{1,0:T(8,128)S(1)} %get-tuple-element.61.total_ref, bf16[512,1536]{1,0:T(8,128)(2,1)S(1)} %get-tuple-element.62.weights_ref, f32[1,1536]{1,0:T(1,128)S(1)} %reshape.7.gate_ref, bf16[384,256]{1,0:T(8,128)(2,1)S(1)} %collective-permute-done.17.refs_0_, ...), custom_call_target="tpu_custom_call" | custom-call | tf_op jit(solution)/shard_map/pallas_call | solution.py:272
  (36 shorter events, 0.1 us)
Async XLA Ops:
  2.6 5.1 %copy-start.3 = (bf16[384,1536]{1,0:T(8,128)(2,1)S(1)}, bf16[384,1536]{1,0:T(8,128)(2,1)}, u32[]{:S(2)}) copy-start(bf16[384,1536]{1,0:T(8,128)(2,1)} %refs_0_.5) | copy-start | bytes 3538948
  2.6 5.1 %copy-start.4 = (bf16[384,1536]{1,0:T(8,128)(2,1)S(1)}, bf16[384,1536]{1,0:T(8,128)(2,1)}, u32[]{:S(2)}) copy-start(bf16[384,1536]{1,0:T(8,128)(2,1)} %refs_1_.5) | copy-start | bytes 3538948
  2.6 5.0 %collective-permute-start.1 = (bf16[384,2304]{1,0:T(8,128)(2,1)}, bf16[384,2304]{1,0:T(8,128)(2,1)}, u32[]{:S(2)}, u32[]{:S(2)}) collective-permute-start(bf16[384,2304]{1,0:T(8,128)(2,1)} %shard_map.73), channel_id=1, source_target_pairs={{0,1},{1,0},{2,3},{3,2},{4,5},{5,4},{6,7},{7,6},{8,9},{9,8},{10,11... | collective-permute-start | bytes 5308424 | tf_op jit(solution)/shard_map/ppermute | solution.py:39
  5.8 27.7 %collective-permute-start.4 = (bf16[1536,384]{1,0:T(8,128)(2,1)}, bf16[1536,384]{1,0:T(8,128)(2,1)}, u32[]{:S(2)}, u32[]{:S(2)}) collective-permute-start(bf16[1536,384]{1,0:T(8,128)(2,1)} %constant_dynamic-slice_fusion), channel_id=1, source_target_pairs={{0,2},{2,0},{1,3},{3,1},{4,6},{6,4},{5,7},{7,5},{8,10},{10,8},{9,1... | collective-permute-start | bytes 3538952 | tf_op jit(solution)/shard_map/ppermute | solution.py:342
  7.6 7.1 %copy-start.9 = (s32[1,6]{1,0:T(1,128)S(1)}, s32[1,6]{1,0:T(1,128)}, u32[]{:S(2)}) copy-start(s32[1,6]{1,0:T(1,128)} %param.10) | copy-start | bytes 76
  7.6 9.1 %copy-start.5 = (bf16[384,1536]{1,0:T(8,128)(2,1)S(1)}, bf16[384,1536]{1,0:T(8,128)(2,1)}, u32[]{:S(2)}) copy-start(bf16[384,1536]{1,0:T(8,128)(2,1)} %refs_2_.3) | copy-start | bytes 3538948
  10.2 22.2 %collective-permute-start.2 = (bf16[768,512]{1,0:T(8,128)(2,1)}, bf16[768,512]{1,0:T(8,128)(2,1)}, u32[]{:S(2)}, u32[]{:S(2)}) collective-permute-start(bf16[768,512]{1,0:T(8,128)(2,1)} %shard_map.75.refs_0_), channel_id=1, source_target_pairs={{0,4},{8,12},{4,0},{12,8},{1,5},{9,13},{5,1},{13,9},{2,6},{10,14},... | collective-permute-start | bytes 2359304 | tf_op jit(solution)/shard_map/ppermute | solution.py:44
  10.4 22.0 %collective-permute-start.3 = (bf16[768,512]{1,0:T(8,128)(2,1)}, bf16[768,512]{1,0:T(8,128)(2,1)}, u32[]{:S(2)}, u32[]{:S(2)}) collective-permute-start(bf16[768,512]{1,0:T(8,128)(2,1)} %shard_map.75.refs_0_), channel_id=1, source_target_pairs={{4,8},{8,4},{5,9},{9,5},{6,10},{10,6},{7,11},{11,7},{20,24},{24,20... | collective-permute-start | bytes 2359304 | tf_op jit(solution)/shard_map/ppermute | solution.py:44
  14.8 1.8 %collective-permute-start = (s32[1,7]{1,0:T(1,128)S(1)}, s32[1,7]{1,0:T(1,128)S(1)}, u32[]{:S(2)}, u32[]{:S(2)}) collective-permute-start(s32[1,7]{1,0:T(1,128)S(1)} %pad_add_fusion.1), channel_id=1, source_target_pairs={{0,1},{1,0},{2,3},{3,2},{4,5},{5,4},{6,7},{7,6},{8,9},{9,8},{10,11... | collective-permute-start | bytes 92 | tf_op jit(solution)/shard_map/ppermute | solution.py:39
  19.2 30.2 %copy-start.1 = (bf16[768,768]{1,0:T(8,128)(2,1)}, bf16[768,768]{1,0:T(8,128)(2,1)S(1)}, u32[]{:S(2)}) copy-start(bf16[768,768]{1,0:T(8,128)(2,1)S(1)} %get-tuple-element.34.queries) | copy-start | bytes 3538948
  19.2 26.8 %collective-permute-start.6 = (bf16[768,512]{1,0:T(8,128)(2,1)S(1)}, bf16[768,512]{1,0:T(8,128)(2,1)S(1)}, u32[]{:S(2)}, u32[]{:S(2)}) collective-permute-start(bf16[768,512]{1,0:T(8,128)(2,1)S(1)} %get-tuple-element.35.refs_1_), channel_id=1, source_target_pairs={{0,4},{8,12},{4,0},{12,8},{1,5},{9,13},{5,1},{13,9},{2,6},{10,14},... | collective-permute-start | bytes 2359304 | tf_op jit(solution)/shard_map/ppermute | solution.py:44
  19.2 30.2 %collective-permute-start.7 = (bf16[768,512]{1,0:T(8,128)(2,1)S(1)}, bf16[768,512]{1,0:T(8,128)(2,1)S(1)}, u32[]{:S(2)}, u32[]{:S(2)}) collective-permute-start(bf16[768,512]{1,0:T(8,128)(2,1)S(1)} %get-tuple-element.35.refs_1_), channel_id=1, source_target_pairs={{4,8},{8,4},{5,9},{9,5},{6,10},{10,6},{7,11},{11,7},{20,24},{24,20... | collective-permute-start | bytes 2359304 | tf_op jit(solution)/shard_map/ppermute | solution.py:44
  33.5 36.1 %collective-permute-start.13 = (bf16[1536,384]{1,0:T(8,128)(2,1)}, bf16[1536,384]{1,0:T(8,128)(2,1)}, u32[]{:S(2)}, u32[]{:S(2)}) collective-permute-start(bf16[1536,384]{1,0:T(8,128)(2,1)} %collective-permute-done.4.refs_6_), channel_id=1, source_target_pairs={{0,16},{16,0},{1,17},{17,1},{2,18},{18,2},{3,19},{19,3},{4,20},{20... | collective-permute-start | bytes 3538952 | tf_op jit(solution)/shard_map/ppermute | solution.py:360
  39.0 2.4 %collective-permute-start.5 = (bf16[384,256]{1,0:T(8,128)(2,1)S(1)}, bf16[384,256]{1,0:T(8,128)(2,1)S(1)}, u32[]{:S(2)}, u32[]{:S(2)}) collective-permute-start(bf16[384,256]{1,0:T(8,128)(2,1)S(1)} %get-tuple-element.45), channel_id=1, source_target_pairs={{0,1},{1,0},{2,3},{3,2},{4,5},{5,4},{6,7},{7,6},{8,9},{9,8},{10,11... | collective-permute-start | bytes 589832 | tf_op jit(solution)/shard_map/ppermute | solution.py:39
  41.4 16.8 %collective-permute-start.11 = (bf16[384,512]{1,0:T(8,128)(2,1)S(1)}, bf16[384,512]{1,0:T(8,128)(2,1)S(1)}, u32[]{:S(2)}, u32[]{:S(2)}) collective-permute-start(bf16[384,512]{1,0:T(8,128)(2,1)S(1)} %constant_dynamic-update-slice_fusion.refs_0_), channel_id=1, source_target_pairs={{0,2},{2,0},{1,3},{3,1},{4,6},{6,4},{5,7},{7,5},{8,10},{10,8},{9,1... | collective-permute-start | bytes 1179656 | tf_op jit(solution)/shard_map/ppermute | solution.py:374
  42.7 22.2 %collective-permute-start.9 = (bf16[768,512]{1,0:T(8,128)(2,1)}, bf16[768,512]{1,0:T(8,128)(2,1)}, u32[]{:S(2)}, u32[]{:S(2)}) collective-permute-start(bf16[768,512]{1,0:T(8,128)(2,1)} %get-tuple-element.50.refs_2_), channel_id=1, source_target_pairs={{0,4},{8,12},{4,0},{12,8},{1,5},{9,13},{5,1},{13,9},{2,6},{10,14},... | collective-permute-start | bytes 2359304 | tf_op jit(solution)/shard_map/ppermute | solution.py:44
  46.0 19.1 %collective-permute-start.10 = (bf16[768,512]{1,0:T(8,128)(2,1)}, bf16[768,512]{1,0:T(8,128)(2,1)}, u32[]{:S(2)}, u32[]{:S(2)}) collective-permute-start(bf16[768,512]{1,0:T(8,128)(2,1)} %get-tuple-element.50.refs_2_), channel_id=1, source_target_pairs={{4,8},{8,4},{5,9},{9,5},{6,10},{10,6},{7,11},{11,7},{20,24},{24,20... | collective-permute-start | bytes 2359304 | tf_op jit(solution)/shard_map/ppermute | solution.py:44
  49.4 29.0 %slice-start = ((s8[4718592]{0:T(1024)(128)(4,1)}), s8[524288]{0:T(1024)(128)(4,1)S(1)}, s32[]{:S(2)}) async-start(s8[4718592]{0:T(1024)(128)(4,1)} %bitcast.15), calls=%async_computation | async-start | bytes 1048576
  53.9 3.5 %collective-permute-start.8 = (bf16[384,256]{1,0:T(8,128)(2,1)S(1)}, bf16[384,256]{1,0:T(8,128)(2,1)S(1)}, u32[]{:S(2)}, u32[]{:S(2)}) collective-permute-start(bf16[384,256]{1,0:T(8,128)(2,1)S(1)} %get-tuple-element.49), channel_id=1, source_target_pairs={{0,1},{1,0},{2,3},{3,2},{4,5},{5,4},{6,7},{7,6},{8,9},{9,8},{10,11... | collective-permute-start | bytes 589832 | tf_op jit(solution)/shard_map/ppermute | solution.py:39
  58.2 0.8 copy-start.6
  59.0 10.6 %collective-permute-start.12 = (bf16[384,512]{1,0:T(8,128)(2,1)}, bf16[384,512]{1,0:T(8,128)(2,1)}, u32[]{:S(2)}, u32[]{:S(2)}) collective-permute-start(bf16[384,512]{1,0:T(8,128)(2,1)} %constant_dynamic-update-slice_fusion.2.refs_1_), channel_id=1, source_target_pairs={{0,2},{2,0},{1,3},{3,1},{4,6},{6,4},{5,7},{7,5},{8,10},{10,8},{9,1... | collective-permute-start | bytes 1179656 | tf_op jit(solution)/shard_map/ppermute | solution.py:374
  59.5 2.3 %copy-start = (bf16[1536,1536]{1,0:T(8,128)(2,1)S(1)}, bf16[1536,1536]{1,0:T(8,128)(2,1)}, u32[]{:S(2)}) copy-start(bf16[1536,1536]{1,0:T(8,128)(2,1)} %constant_dynamic-slice_fusion.1.refs_2_.refs_3_) | copy-start | bytes 14155780
  61.9 9.0 %copy-start.2 = (bf16[768,768]{1,0:T(8,128)(2,1)S(1)}, bf16[768,768]{1,0:T(8,128)(2,1)}, u32[]{:S(2)}) copy-start(bf16[768,768]{1,0:T(8,128)(2,1)} %copy-done.1) | copy-start | bytes 3538948
  61.9 16.5 %slice-start.1 = ((s8[4718592]{0:T(1024)(128)(4,1)}), s8[4194304]{0:T(1024)(128)(4,1)S(1)}, s32[]{:S(2)}) async-start(s8[4718592]{0:T(1024)(128)(4,1)} %bitcast.15), calls=%async_computation.1 | async-start | bytes 8388608
  64.8 13.5 %copy-start.8 = (f32[1536]{0:T(1024)S(1)}, f32[1536]{0:T(1024)}, u32[]{:S(2)}) copy-start(f32[1536]{0:T(1024)} %param.13) | copy-start | bytes 18436
  64.8 13.6 %copy-start.7 = (bf16[384,512]{1,0:T(8,128)(2,1)S(1)}, bf16[384,512]{1,0:T(8,128)(2,1)}, u32[]{:S(2)}) copy-start(bf16[384,512]{1,0:T(8,128)(2,1)} %copy-done.6) | copy-start | bytes 1179652
  69.6 8.8 %collective-permute-start.15 = (bf16[1536,384]{1,0:T(8,128)(2,1)}, bf16[1536,384]{1,0:T(8,128)(2,1)S(1)}, u32[]{:S(2)}, u32[]{:S(2)}) collective-permute-start(bf16[1536,384]{1,0:T(8,128)(2,1)} %collective-permute-done.4.refs_6_), channel_id=1, source_target_pairs={{0,1},{1,0},{2,3},{3,2},{4,5},{5,4},{6,7},{7,6},{8,9},{9,8},{10,11... | collective-permute-start | bytes 3538952 | tf_op jit(solution)/shard_map/ppermute | solution.py:39
  70.8 7.6 %collective-permute-start.16 = (bf16[1536,384]{1,0:T(8,128)(2,1)}, bf16[1536,384]{1,0:T(8,128)(2,1)S(1)}, u32[]{:S(2)}, u32[]{:S(2)}) collective-permute-start(bf16[1536,384]{1,0:T(8,128)(2,1)} %collective-permute-done.13.refs_8_), channel_id=1, source_target_pairs={{0,1},{1,0},{2,3},{3,2},{4,5},{5,4},{6,7},{7,6},{8,9},{9,8},{10,11... | collective-permute-start | bytes 3538952 | tf_op jit(solution)/shard_map/ppermute | solution.py:39
  76.1 2.3 %collective-permute-start.14 = (bf16[384,256]{1,0:T(8,128)(2,1)S(1)}, bf16[384,256]{1,0:T(8,128)(2,1)S(1)}, u32[]{:S(2)}, u32[]{:S(2)}) collective-permute-start(bf16[384,256]{1,0:T(8,128)(2,1)S(1)} %get-tuple-element.58), channel_id=1, source_target_pairs={{0,1},{1,0},{2,3},{3,2},{4,5},{5,4},{6,7},{7,6},{8,9},{9,8},{10,11... | collective-permute-start | bytes 589832 | tf_op jit(solution)/shard_map/ppermute | solution.py:39
  76.6 6.5 %collective-permute-start.17 = (bf16[384,256]{1,0:T(8,128)(2,1)S(1)}, bf16[384,256]{1,0:T(8,128)(2,1)S(1)}, u32[]{:S(2)}, u32[]{:S(2)}) collective-permute-start(bf16[384,256]{1,0:T(8,128)(2,1)S(1)} %get-tuple-element.57.refs_1_), channel_id=1, source_target_pairs={{0,2},{2,0},{1,3},{3,1},{4,6},{6,4},{5,7},{7,5},{8,10},{10,8},{9,1... | collective-permute-start | bytes 589832 | tf_op jit(solution)/shard_map/ppermute | solution.py:387
  77.1 10.4 %collective-permute-start.18 = (bf16[384,256]{1,0:T(8,128)(2,1)S(1)}, bf16[384,256]{1,0:T(8,128)(2,1)S(1)}, u32[]{:S(2)}, u32[]{:S(2)}) collective-permute-start(bf16[384,256]{1,0:T(8,128)(2,1)S(1)} %get-tuple-element.58), channel_id=1, source_target_pairs={{0,3},{1,2},{2,1},{3,0},{4,7},{5,6},{6,5},{7,4},{8,11},{9,10},{10,... | collective-permute-start | bytes 589832 | tf_op jit(solution)/shard_map/ppermute | solution.py:387

commit v4 on v3

--- a/solution.py
+++ b/solution.py
@@ -11,8 +11,8 @@
 HD = 128
 LOG2E = 1.4426950408889634
 FAR = 1e30
-KERNEL_BYTES = 12 * 2**20
-PROJECT_BYTES = 12 * 2**20
+KERNEL_BYTES = 10 * 2**20
+PROJECT_BYTES = 6 * 2**20
 PACK_BYTES = 56 * 2**20
 SHARES = (2, 2, 2)
 SMEM_SPEC = pl.BlockSpec(memory_space=pltpu.SMEM)
@@ -48,19 +48,22 @@
     return lax.optimization_barrier((value, *earlier))[0]
 
 
-def pack_kernel(inputs, runs, *refs):
-    operands, out, held, sems = refs[:inputs], *refs[inputs:]
+def pack_kernel(inputs, cuts, *refs):
+    operands, outs, helds, sems = refs[:inputs], refs[inputs : inputs + len(cuts)], refs[inputs + len(cuts) : -1], refs[-1]
     arriving, leaving = [], []
     other_half = (1 - lax.axis_index("sub")) * (operands[0].shape[1] // 2)
-    for index, offset, width in runs:
-        for step in range(0, width, HD):
-            n = len(arriving)
-            start = pl.multiple_of(other_half + (offset + step), HD)
-            place = (slice(None), slice(n * HD, (n + 1) * HD))
-            arriving.append(
-                pltpu.make_async_copy(operands[index].at[:, pl.ds(start, HD)], held.at[place], sems.at[0, n])
-            )
-            leaving.append(pltpu.make_async_copy(held.at[place], out.at[place], sems.at[1, n]))
+    for runs, out, held in zip(cuts, outs, helds):
+        at = 0
+        for index, offset, width in runs:
+            for step in range(0, width, HD):
+                n = len(arriving)
+                start = pl.multiple_of(other_half + (offset + step), HD)
+                place = (slice(None), slice(at, at + HD))
+                arriving.append(
+                    pltpu.make_async_copy(operands[index].at[:, pl.ds(start, HD)], held.at[place], sems.at[0, n])
+                )
+                leaving.append(pltpu.make_async_copy(held.at[place], out.at[place], sems.at[1, n]))
+                at += HD
     for copy in arriving:
         copy.start()
     for arrival, departure in zip(arriving, leaving):
@@ -70,14 +73,16 @@
         copy.wait()
 
 
-def pack(operands, runs):
-    shape = (operands[0].shape[0], sum(width for _, _, width in runs))
+def pack(operands, cuts):
+    rows = operands[0].shape[0]
+    shapes = [(rows, sum(width for _, _, width in runs)) for runs in cuts]
+    copies = sum(width for _, width in shapes) // HD
     return pl.pallas_call(
-        functools.partial(pack_kernel, len(operands), runs),
+        functools.partial(pack_kernel, len(operands), cuts),
         in_specs=[HBM_SPEC] * len(operands),
-        out_specs=HBM_SPEC,
-        out_shape=jax.ShapeDtypeStruct(shape, jnp.bfloat16),
-        scratch_shapes=[pltpu.VMEM(shape, jnp.bfloat16), pltpu.SemaphoreType.DMA((2, shape[1] // HD))],
+        out_specs=[HBM_SPEC] * len(cuts),
+        out_shape=[jax.ShapeDtypeStruct(shape, jnp.bfloat16) for shape in shapes],
+        scratch_shapes=[pltpu.VMEM(shape, jnp.bfloat16) for shape in shapes] + [pltpu.SemaphoreType.DMA((2, copies))],
         compiler_params=pltpu.CompilerParams(vmem_limit_bytes=PACK_BYTES),
     )(*operands)
 
@@ -323,17 +328,19 @@
     for first, count in chunks:
         runs_of.append(tuple((index, first * HD, count * HD) for index in (0, 1)))
     wide = [sum(size for _, _, size in runs) for runs in runs_of]
-    lows = [sum(wide[:i]) for i in range(len(wide))]
-
-    found = other_core(pack((keys, values, queries), sum(runs_of, ())))
+    lows = [0] + [sum(wide[1:i]) for i in range(1, len(wide))]
+
+    found, found_queries = (
+        other_core(packed) for packed in pack((keys, values, queries), (sum(runs_of[1:], ()), runs_of[0]))
+    )
     sent = [
         lax.dynamic_slice(out_weight, (0, lax.rem(x + d, n_head) * width + piece * block), (2 * span, block))
         for d in range(1, n_head)
     ]
     cuts = list(zip(lows, runs_of))
     message = join((keys, values), found, span, cuts[1:2])
-    queries, *late = join((keys, values, queries), found, span, [cuts[0], *cuts[2:]])
-    message = [*message, *late]
+    message += join((keys, values), found, span, cuts[2:])
+    (queries,) = join((queries,), found_queries, span, [(0, ((0, 0, span),))])
     near = [to_neighbours(message[0])]
     lists = jnp.concatenate([lists, other_core(lists)], axis=0)
     scalars = (jnp.stack(tiles).astype(jnp.int32), lists)

time: 89.7 us -> 87.6 us (0.977)
  local copies, waits for them, and re-layouts: 12 us -> 15.8 us
  Pallas kernels: 38 us -> 34.6 us
  waiting for transfers between devices: 15.8 us -> 13.7 us
    pallas_call x2 -> x3, Pallas kernels: 5.02 us -> 2.08 us  [join(): pl.pallas_call(functools.partial(join_kernel, span, cuts), in_specs=[VMEM...]
    unnamed x26 -> x32, local copies, waits for them, and re-layouts: 3.9 us -> 6.71 us
    ppermute x2, waiting for transfers between devices: 4.47 us -> 3.39 us  [local(): lax.ppermute(leaving, 'head', ring(n_head, d))]
    ppermute x1, waiting for transfers between devices: 1.08 us -> 0.01 us  [local(): lax.ppermute(a, 'head', ring(n_head, d + 1))]
    ppermute x7 -> x8, starting transfers between devices: 7.35 us -> 7.14 us  [other_core(): return lax.ppermute(block, 'sub', [(0, 1), (1, 0)])]
    ppermute x7 -> x8, waiting for transfers between devices: 2.16 us -> 2.17 us  [other_core(): return lax.ppermute(block, 'sub', [(0, 1), (1, 0)])]
  transfers between devices with their start and end apart: 19 -> 20, of which waited for: 9 -> 8; matrix products, arithmetic and copies ran while one was open for 10% -> 11% of each run, Pallas kernels for 38% -> 35%
where the time goes in v4:
time: 87.6 us; the launch traced here: 87.2 us
  Pallas kernels  34.6 us (39%)
  starting transfers between devices  21.9 us (25%)
  local copies, waits for them, and re-layouts  15.8 us (18%)
  waiting for transfers between devices  13.7 us (16%)
  between operations  1.09 us (1%)
    pallas_call x4, Pallas kernels, attend(): pl.pallas_call(functools.partial(attention_kernel, first, plan, base, mer...  21.4 us
    ppermute x6, starting transfers between devices, to_neighbours(): lax.ppermute(block, 'seq', pairing(length, start))  9.95 us
    ppermute x8, starting transfers between devices, other_core(): return lax.ppermute(block, 'sub', [(0, 1), (1, 0)])  7.14 us
    pallas_call x2, Pallas kernels, project(): pl.pallas_call(functools.partial(project_kernel, splits, plan, total is n...  7.04 us
    unnamed x32, local copies, waits for them, and re-layouts  6.71 us
    dynamic_slice x1, local copies, waits for them, and re-layouts, local(): lax.dynamic_slice(after(out_weight, prior), (0, x * width), (2 * span, wi...  5.63 us
    ppermute x1, waiting for transfers between devices, local(): lax.ppermute(given, ('head', 'sub'), across)  4.37 us
    ppermute x2, waiting for transfers between devices, local(): lax.ppermute(leaving, 'head', ring(n_head, d))  3.39 us
  transfers between devices with their start and end apart: 20, of which 8 were waited for; matrix products, arithmetic and copies ran while one was open for 11% of the time, Pallas kernels for 35%

profile of v4, /device:TPU:13, one launch (start us, length us, event | category | flops | bytes accessed | tf_op | source)
XLA Modules:
  0.0 87.2 jit_solution(15743799699913103067)
XLA Ops:
  0.0 2.5 %shard_map.73 = (bf16[384,1536]{1,0:T(8,128)(2,1)}, bf16[384,768]{1,0:T(8,128)(2,1)}) custom-call(bf16[384,1536]{1,0:T(8,128)(2,1)} %refs_0_.7, bf16[384,1536]{1,0:T(8,128)(2,1)} %refs_1_.5, bf16[384,1536]{1,0:T(8,128)(2,1)} %refs_0_.5), custom_call_target="tpu_custom_call" | custom-call | tf_op jit(solution)/shard_map/pallas_call | solution.py:80
  2.6 0.7 collective-permute-start.2
  3.4 2.6 %constant_dynamic-slice_fusion = bf16[1536,384]{1,0:T(8,128)(2,1)} fusion(bf16[1536,3072]{1,0:T(8,128)(2,1)} %param.12, s32[]{:T(128)S(6)} %select_n.32), kind=kLoop, calls=%fused_computation.6 | loop fusion | bytes 2359300 | tf_op jit(solution)/shard_map/dynamic_slice | solution.py:337
  5.9 1.2 %collective-permute-start.5 = (bf16[1536,384]{1,0:T(8,128)(2,1)}, bf16[1536,384]{1,0:T(8,128)(2,1)}, u32[]{:S(2)}, u32[]{:S(2)}) collective-permute-start(bf16[1536,384]{1,0:T(8,128)(2,1)} %constant_dynamic-slice_fusion), channel_id=1, source_target_pairs={{0,2},{2,0},{1,3},{3,1},{4,6},{6,4},{5,7},{7,5},{8,10},{10,8},{9,1... | collective-permute-start | bytes 3538952 | tf_op jit(solution)/shard_map/ppermute | solution.py:349
  7.9 1.0 %shard_map.75.refs_0_ = bf16[768,512]{1,0:T(8,128)(2,1)} custom-call(bf16[384,1536]{1,0:T(8,128)(2,1)S(1)} %copy-done.3, bf16[384,1536]{1,0:T(8,128)(2,1)S(1)} %copy-done.4, bf16[384,1536]{1,0:T(8,128)(2,1)S(1)} %collective-permute-done.2.refs_2_), custom_call_target="tpu_custom_call" | custom-call | tf_op jit(solution)/shard_map/pallas_call | solution.py:106
  8.9 0.2 copy-done.7
  9.1 0.2 collective-permute-start.3
  9.3 4.3 %collective-permute-start.4 = (bf16[768,512]{1,0:T(8,128)(2,1)}, bf16[768,512]{1,0:T(8,128)(2,1)}, u32[]{:S(2)}, u32[]{:S(2)}) collective-permute-start(bf16[768,512]{1,0:T(8,128)(2,1)} %shard_map.75.refs_0_), channel_id=1, source_target_pairs={{4,8},{8,4},{5,9},{9,5},{6,10},{10,6},{7,11},{11,7},{20,24},{24,20... | collective-permute-start | bytes 2359304 | tf_op jit(solution)/shard_map/ppermute | solution.py:44
  13.7 1.3 %collective-permute-start = (s32[1,7]{1,0:T(1,128)S(1)}, s32[1,7]{1,0:T(1,128)S(1)}, u32[]{:S(2)}, u32[]{:S(2)}) collective-permute-start(s32[1,7]{1,0:T(1,128)S(1)} %pad_add_fusion.1), channel_id=1, source_target_pairs={{0,1},{1,0},{2,3},{3,2},{4,5},{5,4},{6,7},{7,6},{8,9},{9,8},{10,11... | collective-permute-start | bytes 92 | tf_op jit(solution)/shard_map/ppermute | solution.py:39
  15.0 0.1 stack.55.tiles_ref
  15.1 0.7 collective-permute-done
  15.9 1.4 %copy-done.6 = bf16[384,1536]{1,0:T(8,128)(2,1)S(1)} copy-done((bf16[384,1536]{1,0:T(8,128)(2,1)S(1)}, bf16[384,1536]{1,0:T(8,128)(2,1)}, u32[]{:S(2)}) %copy-start.6) | copy-done | bytes 1179672
  17.3 0.1 shard_map.74.queries
  17.3 0.2 copy-done.5
  17.5 1.1 %copy-done.8 = bf16[384,1536]{1,0:T(8,128)(2,1)S(1)} copy-done((bf16[384,1536]{1,0:T(8,128)(2,1)S(1)}, bf16[384,1536]{1,0:T(8,128)(2,1)}, u32[]{:S(2)}) %copy-start.8) | copy-done | bytes 1179672
  18.6 1.0 %shard_map.76 = (bf16[768,512]{1,0:T(8,128)(2,1)S(1)}, bf16[768,512]{1,0:T(8,128)(2,1)}) custom-call(bf16[384,1536]{1,0:T(8,128)(2,1)S(1)} %copy-done.3, bf16[384,1536]{1,0:T(8,128)(2,1)S(1)} %copy-done.5, bf16[384,1536]{1,0:T(8,128)(2,1)S(1)} %copy-done.8), custom_call_target="tpu_custom_call" | custom-call | tf_op jit(solution)/shard_map/pallas_call | solution.py:106
  19.6 1.9 %collective-permute-start.8 = (bf16[768,512]{1,0:T(8,128)(2,1)S(1)}, bf16[768,512]{1,0:T(8,128)(2,1)S(1)}, u32[]{:S(2)}, u32[]{:S(2)}) collective-permute-start(bf16[768,512]{1,0:T(8,128)(2,1)S(1)} %get-tuple-element.37.refs_1_), channel_id=1, source_target_pairs={{4,8},{8,4},{5,9},{9,5},{6,10},{10,6},{7,11},{11,7},{20,24},{24,20... | collective-permute-start | bytes 2359304 | tf_op jit(solution)/shard_map/ppermute | solution.py:44
  21.5 6.4 %shard_map.77 = (f32[768,768]{1,0:T(8,128)S(1)}, f32[8,768]{1,0:T(8,128)S(1)}) custom-call(s32[6]{0:T(128)S(1)} %stack.55.tiles_ref, s32[2,7]{1,0:T(2,128)S(1)} %pad_add_fusion.lists_ref, bf16[768,768]{1,0:T(8,128)(2,1)S(1)} %shard_map.74.queries, bf16[768,512]{1,0:T(8,128)(2,1)} %shard_map.75.refs_0_, bf16[768,512]{1,0:T(8,128)(2,1)S(1)} %get-tuple-element.37.refs_1_, ...), custom_call_target="tpu_custom_call" | custom-call | tf_op jit(solution)/shard_map/pallas_call | solution.py:199
  27.9 5.6 %constant_dynamic-slice_fusion.1.refs_2_.refs_3_ = bf16[1536,1536]{1,0:T(8,128)(2,1)} fusion(bf16[1536,3072]{1,0:T(8,128)(2,1)} %param.12, s32[]{:T(128)S(6)} %select_n.31), kind=kLoop, calls=%fused_computation.7 | loop fusion | bytes 9437188 | tf_op jit(solution)/shard_map/dynamic_slice | solution.py:364
  33.6 0.3 collective-permute-start.14
  33.9 5.3 %shard_map.78 = (bf16[384,256]{1,0:T(8,128)(2,1)S(1)}, bf16[384,256]{1,0:T(8,128)(2,1)S(1)}) custom-call(s32[6]{0:T(128)S(1)} %stack.55.tiles_ref, s32[2,7]{1,0:T(2,128)S(1)} %pad_add_fusion.lists_ref, bf16[768,768]{1,0:T(8,128)(2,1)S(1)} %shard_map.74.queries, bf16[768,512]{1,0:T(8,128)(2,1)} %collective-permute-done.3.refs_0_, ...), custom_call_target="tpu_custom_call" | custom-call | tf_op jit(solution)/shard_map/pallas_call | solution.py:199
  39.1 1.3 %collective-permute-start.6 = (bf16[384,256]{1,0:T(8,128)(2,1)S(1)}, bf16[384,256]{1,0:T(8,128)(2,1)S(1)}, u32[]{:S(2)}, u32[]{:S(2)}) collective-permute-start(bf16[384,256]{1,0:T(8,128)(2,1)S(1)} %get-tuple-element.47), channel_id=1, source_target_pairs={{0,1},{1,0},{2,3},{3,2},{4,5},{5,4},{6,7},{7,6},{8,9},{9,8},{10,11... | collective-permute-start | bytes 589832 | tf_op jit(solution)/shard_map/ppermute | solution.py:39
  40.5 1.1 %collective-permute-done.6 = bf16[384,256]{1,0:T(8,128)(2,1)S(1)} collective-permute-done((bf16[384,256]{1,0:T(8,128)(2,1)S(1)}, bf16[384,256]{1,0:T(8,128)(2,1)S(1)}, u32[]{:S(2)}, u32[]{:S(2)}) %collective-permute-start.6) | collective-permute-done | bytes 196640 | tf_op jit(solution)/shard_map/ppermute | solution.py:39
  41.6 1.3 %collective-permute-start.12 = (bf16[384,512]{1,0:T(8,128)(2,1)S(1)}, bf16[384,512]{1,0:T(8,128)(2,1)S(1)}, u32[]{:S(2)}, u32[]{:S(2)}) collective-permute-start(bf16[384,512]{1,0:T(8,128)(2,1)S(1)} %constant_dynamic-update-slice_fusion.refs_0_), channel_id=1, source_target_pairs={{0,2},{2,0},{1,3},{3,1},{4,6},{6,4},{5,7},{7,5},{8,10},{10,8},{9,1... | collective-permute-start | bytes 1179656 | tf_op jit(solution)/shard_map/ppermute | solution.py:381
  42.8 0.2 collective-permute-start.10
  43.0 1.5 %collective-permute-done.7.refs_0_ = bf16[768,512]{1,0:T(8,128)(2,1)S(1)} collective-permute-done((bf16[768,512]{1,0:T(8,128)(2,1)S(1)}, bf16[768,512]{1,0:T(8,128)(2,1)S(1)}, u32[]{:S(2)}, u32[]{:S(2)}) %collective-permute-start.7) | collective-permute-done | bytes 786464 | tf_op jit(solution)/shard_map/ppermute | solution.py:44
  44.6 3.4 %collective-permute-start.11 = (bf16[768,512]{1,0:T(8,128)(2,1)}, bf16[768,512]{1,0:T(8,128)(2,1)}, u32[]{:S(2)}, u32[]{:S(2)}) collective-permute-start(bf16[768,512]{1,0:T(8,128)(2,1)} %get-tuple-element.52.refs_2_), channel_id=1, source_target_pairs={{4,8},{8,4},{5,9},{9,5},{6,10},{10,6},{7,11},{11,7},{20,24},{24,20... | collective-permute-start | bytes 2359304 | tf_op jit(solution)/shard_map/ppermute | solution.py:44
  48.0 4.5 %shard_map.79 = (bf16[384,256]{1,0:T(8,128)(2,1)S(1)}, bf16[384,256]{1,0:T(8,128)(2,1)S(1)}) custom-call(s32[6]{0:T(128)S(1)} %stack.55.tiles_ref, s32[2,7]{1,0:T(2,128)S(1)} %pad_add_fusion.lists_ref, bf16[768,768]{1,0:T(8,128)(2,1)S(1)} %shard_map.74.queries, bf16[768,512]{1,0:T(8,128)(2,1)S(1)} %collective-permute-done.7.refs_0_, ...), custom_call_target="tpu_custom_call" | custom-call | tf_op jit(solution)/shard_map/pallas_call | solution.py:199
  52.5 1.9 %collective-permute-start.9 = (bf16[384,256]{1,0:T(8,128)(2,1)S(1)}, bf16[384,256]{1,0:T(8,128)(2,1)S(1)}, u32[]{:S(2)}, u32[]{:S(2)}) collective-permute-start(bf16[384,256]{1,0:T(8,128)(2,1)S(1)} %get-tuple-element.51), channel_id=1, source_target_pairs={{0,1},{1,0},{2,3},{3,2},{4,5},{5,4},{6,7},{7,6},{8,9},{9,8},{10,11... | collective-permute-start | bytes 589832 | tf_op jit(solution)/shard_map/ppermute | solution.py:39
  54.4 0.7 constant_dynamic-update-slice_fusion.3
  55.1 0.4 collective-permute-done.9
  55.5 0.7 constant_dynamic-update-slice_fusion.2.refs_1_
  56.2 0.7 copy-done.9
  56.9 0.3 collective-permute-start.13
  57.2 0.1 stack.48.place_ref
  57.3 2.3 %copy-done = bf16[1536,1536]{1,0:T(8,128)(2,1)S(1)} copy-done((bf16[1536,1536]{1,0:T(8,128)(2,1)S(1)}, bf16[1536,1536]{1,0:T(8,128)(2,1)}, u32[]{:S(2)}) %copy-start) | copy-done | bytes 4718616
  59.6 2.9 %shard_map.80.refs_0_ = f32[384,1536]{1,0:T(8,128)S(1)} custom-call(s32[6]{0:T(128)S(1)} %stack.48.place_ref, bf16[384,512]{1,0:T(8,128)(2,1)S(1)} %constant_dynamic-update-slice_fusion.refs_0_, bf16[384,512]{1,0:T(8,128)(2,1)} %constant_dynamic-update-slice_fusion.2.refs_1_, bf16[1536,1536]{1,0:T(8,128)(2,1)S(1)} %copy-done), custom_call_target="tpu_custom_call" | custom-call | tf_op jit(solution)/shard_map/pallas_call | solution.py:245
  62.6 1.6 %collective-permute-done.11.refs_1_ = bf16[768,512]{1,0:T(8,128)(2,1)} collective-permute-done((bf16[768,512]{1,0:T(8,128)(2,1)}, bf16[768,512]{1,0:T(8,128)(2,1)}, u32[]{:S(2)}, u32[]{:S(2)}) %collective-permute-start.11) | collective-permute-done | bytes 786464 | tf_op jit(solution)/shard_map/ppermute | solution.py:44
  64.2 3.4 %collective-permute-done.13.refs_5_ = bf16[384,512]{1,0:T(8,128)(2,1)} collective-permute-done((bf16[384,512]{1,0:T(8,128)(2,1)}, bf16[384,512]{1,0:T(8,128)(2,1)}, u32[]{:S(2)}, u32[]{:S(2)}) %collective-permute-start.13) | collective-permute-done | bytes 393248 | tf_op jit(solution)/shard_map/ppermute | solution.py:381
  67.6 1.2 %collective-permute-start.16 = (bf16[1536,384]{1,0:T(8,128)(2,1)}, bf16[1536,384]{1,0:T(8,128)(2,1)S(1)}, u32[]{:S(2)}, u32[]{:S(2)}) collective-permute-start(bf16[1536,384]{1,0:T(8,128)(2,1)} %collective-permute-done.5.refs_6_), channel_id=1, source_target_pairs={{0,1},{1,0},{2,3},{3,2},{4,5},{5,4},{6,7},{7,6},{8,9},{9,8},{10,11... | collective-permute-start | bytes 3538952 | tf_op jit(solution)/shard_map/ppermute | solution.py:39
  68.8 5.2 %shard_map.81 = (bf16[384,256]{1,0:T(8,128)(2,1)S(1)}, bf16[384,256]{1,0:T(8,128)(2,1)S(1)}) custom-call(s32[6]{0:T(128)S(1)} %stack.55.tiles_ref, s32[2,7]{1,0:T(2,128)S(1)} %pad_add_fusion.lists_ref, bf16[768,768]{1,0:T(8,128)(2,1)S(1)} %shard_map.74.queries, bf16[768,512]{1,0:T(8,128)(2,1)} %collective-permute-done.10.refs_0_, ...), custom_call_target="tpu_custom_call" | custom-call | tf_op jit(solution)/shard_map/pallas_call | solution.py:199
  74.0 0.6 collective-permute-start.15
  74.6 0.3 collective-permute-start.18
  74.9 1.4 %collective-permute-start.19 = (bf16[384,256]{1,0:T(8,128)(2,1)S(1)}, bf16[384,256]{1,0:T(8,128)(2,1)S(1)}, u32[]{:S(2)}, u32[]{:S(2)}) collective-permute-start(bf16[384,256]{1,0:T(8,128)(2,1)S(1)} %get-tuple-element.60), channel_id=1, source_target_pairs={{0,3},{1,2},{2,1},{3,0},{4,7},{5,6},{6,5},{7,4},{8,11},{9,10},{10,... | collective-permute-start | bytes 589832 | tf_op jit(solution)/shard_map/ppermute | solution.py:394
  76.4 4.1 %shard_map.82 = (f32[384,1536]{1,0:T(8,128)S(1)}, bf16[512,1536]{1,0:T(8,128)(2,1)S(1)}) custom-call(s32[6]{0:T(128)S(1)} %stack.48.place_ref, f32[384,1536]{1,0:T(8,128)S(1)} %shard_map.80.refs_0_, bf16[384,256]{1,0:T(8,128)(2,1)S(1)} %get-tuple-element.59.refs_1_, bf16[384,256]{1,0:T(8,128)(2,1)S(1)} %collective-permute-done.15.refs_2_, ...), custom_call_target="tpu_custom_call" | custom-call | tf_op jit(solution)/shard_map/pallas_call | solution.py:245
  80.5 0.6 collective-permute-done.18.refs_0_
  81.1 4.4 %collective-permute-done.19.refs_1_ = bf16[384,256]{1,0:T(8,128)(2,1)S(1)} collective-permute-done((bf16[384,256]{1,0:T(8,128)(2,1)S(1)}, bf16[384,256]{1,0:T(8,128)(2,1)S(1)}, u32[]{:S(2)}, u32[]{:S(2)}) %collective-permute-start.19) | collective-permute-done | bytes 196640 | tf_op jit(solution)/shard_map/ppermute | solution.py:394
  85.5 1.6 %shard_map.83 = bf16[384,1536]{1,0:T(8,128)(2,1)} custom-call(f32[384,1536]{1,0:T(8,128)S(1)} %get-tuple-element.63.total_ref, bf16[512,1536]{1,0:T(8,128)(2,1)S(1)} %get-tuple-element.64.weights_ref, f32[1,1536]{1,0:T(1,128)S(1)} %reshape.7.gate_ref, bf16[384,256]{1,0:T(8,128)(2,1)S(1)} %collective-permute-done.18.refs_0_, ...), custom_call_target="tpu_custom_call" | custom-call | tf_op jit(solution)/shard_map/pallas_call | solution.py:277
  (45 shorter events, 0.4 us)
Async XLA Ops:
  2.6 5.3 %collective-permute-start.2 = (bf16[384,1536]{1,0:T(8,128)(2,1)}, bf16[384,1536]{1,0:T(8,128)(2,1)S(1)}, u32[]{:S(2)}, u32[]{:S(2)}) collective-permute-start(bf16[384,1536]{1,0:T(8,128)(2,1)} %get-tuple-element.36), channel_id=1, source_target_pairs={{0,1},{1,0},{2,3},{3,2},{4,5},{5,4},{6,7},{7,6},{8,9},{9,8},{10,11... | collective-permute-start | bytes 3538952 | tf_op jit(solution)/shard_map/ppermute | solution.py:39
  3.3 12.6 %collective-permute-start.1 = (bf16[384,768]{1,0:T(8,128)(2,1)}, bf16[384,768]{1,0:T(8,128)(2,1)S(1)}, u32[]{:S(2)}, u32[]{:S(2)}) collective-permute-start(bf16[384,768]{1,0:T(8,128)(2,1)} %get-tuple-element.35), channel_id=1, source_target_pairs={{0,1},{1,0},{2,3},{3,2},{4,5},{5,4},{6,7},{7,6},{8,9},{9,8},{10,11... | collective-permute-start | bytes 1769480 | tf_op jit(solution)/shard_map/ppermute | solution.py:39
  3.4 4.5 %copy-start.3 = (bf16[384,1536]{1,0:T(8,128)(2,1)S(1)}, bf16[384,1536]{1,0:T(8,128)(2,1)}, u32[]{:S(2)}) copy-start(bf16[384,1536]{1,0:T(8,128)(2,1)} %refs_0_.7) | copy-start | bytes 3538948
  3.4 4.5 %copy-start.4 = (bf16[384,1536]{1,0:T(8,128)(2,1)S(1)}, bf16[384,1536]{1,0:T(8,128)(2,1)}, u32[]{:S(2)}) copy-start(bf16[384,1536]{1,0:T(8,128)(2,1)} %refs_1_.5) | copy-start | bytes 3538948
  5.9 27.6 %collective-permute-start.5 = (bf16[1536,384]{1,0:T(8,128)(2,1)}, bf16[1536,384]{1,0:T(8,128)(2,1)}, u32[]{:S(2)}, u32[]{:S(2)}) collective-permute-start(bf16[1536,384]{1,0:T(8,128)(2,1)} %constant_dynamic-slice_fusion), channel_id=1, source_target_pairs={{0,2},{2,0},{1,3},{3,1},{4,6},{6,4},{5,7},{7,5},{8,10},{10,8},{9,1... | collective-permute-start | bytes 3538952 | tf_op jit(solution)/shard_map/ppermute | solution.py:349
  7.8 5.8 %copy-start.12 = (s32[1,6]{1,0:T(1,128)S(1)}, s32[1,6]{1,0:T(1,128)}, u32[]{:S(2)}) copy-start(s32[1,6]{1,0:T(1,128)} %param.10) | copy-start | bytes 76
  7.9 1.3 %copy-start.7 = (bf16[384,1536]{1,0:T(8,128)(2,1)}, bf16[384,1536]{1,0:T(8,128)(2,1)S(1)}, u32[]{:S(2)}) copy-start(bf16[384,1536]{1,0:T(8,128)(2,1)S(1)} %collective-permute-done.2.refs_2_) | copy-start | bytes 3538948
  9.1 24.4 %collective-permute-start.3 = (bf16[768,512]{1,0:T(8,128)(2,1)}, bf16[768,512]{1,0:T(8,128)(2,1)}, u32[]{:S(2)}, u32[]{:S(2)}) collective-permute-start(bf16[768,512]{1,0:T(8,128)(2,1)} %shard_map.75.refs_0_), channel_id=1, source_target_pairs={{0,4},{8,12},{4,0},{12,8},{1,5},{9,13},{5,1},{13,9},{2,6},{10,14},... | collective-permute-start | bytes 2359304 | tf_op jit(solution)/shard_map/ppermute | solution.py:44
  9.3 24.3 %collective-permute-start.4 = (bf16[768,512]{1,0:T(8,128)(2,1)}, bf16[768,512]{1,0:T(8,128)(2,1)}, u32[]{:S(2)}, u32[]{:S(2)}) collective-permute-start(bf16[768,512]{1,0:T(8,128)(2,1)} %shard_map.75.refs_0_), channel_id=1, source_target_pairs={{4,8},{8,4},{5,9},{9,5},{6,10},{10,6},{7,11},{11,7},{20,24},{24,20... | collective-permute-start | bytes 2359304 | tf_op jit(solution)/shard_map/ppermute | solution.py:44
  13.7 2.1 %collective-permute-start = (s32[1,7]{1,0:T(1,128)S(1)}, s32[1,7]{1,0:T(1,128)S(1)}, u32[]{:S(2)}, u32[]{:S(2)}) collective-permute-start(s32[1,7]{1,0:T(1,128)S(1)} %pad_add_fusion.1), channel_id=1, source_target_pairs={{0,1},{1,0},{2,3},{3,2},{4,5},{5,4},{6,7},{7,6},{8,9},{9,8},{10,11... | collective-permute-start | bytes 92 | tf_op jit(solution)/shard_map/ppermute | solution.py:39
  15.9 1.6 %copy-start.5 = (bf16[384,1536]{1,0:T(8,128)(2,1)S(1)}, bf16[384,1536]{1,0:T(8,128)(2,1)}, u32[]{:S(2)}) copy-start(bf16[384,1536]{1,0:T(8,128)(2,1)} %refs_1_.5) | copy-start | bytes 3538948
  15.9 1.4 %copy-start.6 = (bf16[384,1536]{1,0:T(8,128)(2,1)S(1)}, bf16[384,1536]{1,0:T(8,128)(2,1)}, u32[]{:S(2)}) copy-start(bf16[384,1536]{1,0:T(8,128)(2,1)} %refs_0_.5) | copy-start | bytes 3538948
  17.3 1.3 %copy-start.8 = (bf16[384,1536]{1,0:T(8,128)(2,1)S(1)}, bf16[384,1536]{1,0:T(8,128)(2,1)}, u32[]{:S(2)}) copy-start(bf16[384,1536]{1,0:T(8,128)(2,1)} %copy-done.7) | copy-start | bytes 3538948
  19.6 25.0 %collective-permute-start.7 = (bf16[768,512]{1,0:T(8,128)(2,1)S(1)}, bf16[768,512]{1,0:T(8,128)(2,1)S(1)}, u32[]{:S(2)}, u32[]{:S(2)}) collective-permute-start(bf16[768,512]{1,0:T(8,128)(2,1)S(1)} %get-tuple-element.37.refs_1_), channel_id=1, source_target_pairs={{0,4},{8,12},{4,0},{12,8},{1,5},{9,13},{5,1},{13,9},{2,6},{10,14},... | collective-permute-start | bytes 2359304 | tf_op jit(solution)/shard_map/ppermute | solution.py:44
  19.6 28.4 %collective-permute-start.8 = (bf16[768,512]{1,0:T(8,128)(2,1)S(1)}, bf16[768,512]{1,0:T(8,128)(2,1)S(1)}, u32[]{:S(2)}, u32[]{:S(2)}) collective-permute-start(bf16[768,512]{1,0:T(8,128)(2,1)S(1)} %get-tuple-element.37.refs_1_), channel_id=1, source_target_pairs={{4,8},{8,4},{5,9},{9,5},{6,10},{10,6},{7,11},{11,7},{20,24},{24,20... | collective-permute-start | bytes 2359304 | tf_op jit(solution)/shard_map/ppermute | solution.py:44
  27.9 20.0 %copy-start.1 = (f32[768,768]{1,0:T(8,128)}, f32[768,768]{1,0:T(8,128)S(1)}, u32[]{:S(2)}) copy-start(f32[768,768]{1,0:T(8,128)S(1)} %get-tuple-element.39.refs_2_) | copy-start | bytes 7077892
  33.6 34.0 %collective-permute-start.14 = (bf16[1536,384]{1,0:T(8,128)(2,1)}, bf16[1536,384]{1,0:T(8,128)(2,1)S(1)}, u32[]{:S(2)}, u32[]{:S(2)}) collective-permute-start(bf16[1536,384]{1,0:T(8,128)(2,1)} %collective-permute-done.5.refs_6_), channel_id=1, source_target_pairs={{0,16},{16,0},{1,17},{17,1},{2,18},{18,2},{3,19},{19,3},{4,20},{20... | collective-permute-start | bytes 3538952 | tf_op jit(solution)/shard_map/ppermute | solution.py:367
  39.1 2.4 %collective-permute-start.6 = (bf16[384,256]{1,0:T(8,128)(2,1)S(1)}, bf16[384,256]{1,0:T(8,128)(2,1)S(1)}, u32[]{:S(2)}, u32[]{:S(2)}) collective-permute-start(bf16[384,256]{1,0:T(8,128)(2,1)S(1)} %get-tuple-element.47), channel_id=1, source_target_pairs={{0,1},{1,0},{2,3},{3,2},{4,5},{5,4},{6,7},{7,6},{8,9},{9,8},{10,11... | collective-permute-start | bytes 589832 | tf_op jit(solution)/shard_map/ppermute | solution.py:39
  41.6 14.6 %collective-permute-start.12 = (bf16[384,512]{1,0:T(8,128)(2,1)S(1)}, bf16[384,512]{1,0:T(8,128)(2,1)S(1)}, u32[]{:S(2)}, u32[]{:S(2)}) collective-permute-start(bf16[384,512]{1,0:T(8,128)(2,1)S(1)} %constant_dynamic-update-slice_fusion.refs_0_), channel_id=1, source_target_pairs={{0,2},{2,0},{1,3},{3,1},{4,6},{6,4},{5,7},{7,5},{8,10},{10,8},{9,1... | collective-permute-start | bytes 1179656 | tf_op jit(solution)/shard_map/ppermute | solution.py:381
  42.8 19.8 %collective-permute-start.10 = (bf16[768,512]{1,0:T(8,128)(2,1)}, bf16[768,512]{1,0:T(8,128)(2,1)}, u32[]{:S(2)}, u32[]{:S(2)}) collective-permute-start(bf16[768,512]{1,0:T(8,128)(2,1)} %get-tuple-element.52.refs_2_), channel_id=1, source_target_pairs={{0,4},{8,12},{4,0},{12,8},{1,5},{9,13},{5,1},{13,9},{2,6},{10,14},... | collective-permute-start | bytes 2359304 | tf_op jit(solution)/shard_map/ppermute | solution.py:44
  44.6 19.6 %collective-permute-start.11 = (bf16[768,512]{1,0:T(8,128)(2,1)}, bf16[768,512]{1,0:T(8,128)(2,1)}, u32[]{:S(2)}, u32[]{:S(2)}) collective-permute-start(bf16[768,512]{1,0:T(8,128)(2,1)} %get-tuple-element.52.refs_2_), channel_id=1, source_target_pairs={{4,8},{8,4},{5,9},{9,5},{6,10},{10,6},{7,11},{11,7},{20,24},{24,20... | collective-permute-start | bytes 2359304 | tf_op jit(solution)/shard_map/ppermute | solution.py:44
  48.0 28.4 %slice-start = ((s8[4718592]{0:T(1024)(128)(4,1)}), s8[524288]{0:T(1024)(128)(4,1)S(1)}, s32[]{:S(2)}) async-start(s8[4718592]{0:T(1024)(128)(4,1)} %bitcast.15), calls=%async_computation | async-start | bytes 1048576
  52.5 3.0 %collective-permute-start.9 = (bf16[384,256]{1,0:T(8,128)(2,1)S(1)}, bf16[384,256]{1,0:T(8,128)(2,1)S(1)}, u32[]{:S(2)}, u32[]{:S(2)}) collective-permute-start(bf16[384,256]{1,0:T(8,128)(2,1)S(1)} %get-tuple-element.51), channel_id=1, source_target_pairs={{0,1},{1,0},{2,3},{3,2},{4,5},{5,4},{6,7},{7,6},{8,9},{9,8},{10,11... | collective-permute-start | bytes 589832 | tf_op jit(solution)/shard_map/ppermute | solution.py:39
  56.2 0.8 copy-start.9
  56.9 10.6 %collective-permute-start.13 = (bf16[384,512]{1,0:T(8,128)(2,1)}, bf16[384,512]{1,0:T(8,128)(2,1)}, u32[]{:S(2)}, u32[]{:S(2)}) collective-permute-start(bf16[384,512]{1,0:T(8,128)(2,1)} %constant_dynamic-update-slice_fusion.2.refs_1_), channel_id=1, source_target_pairs={{0,2},{2,0},{1,3},{3,1},{4,6},{6,4},{5,7},{7,5},{8,10},{10,8},{9,1... | collective-permute-start | bytes 1179656 | tf_op jit(solution)/shard_map/ppermute | solution.py:381
  57.3 2.3 %copy-start = (bf16[1536,1536]{1,0:T(8,128)(2,1)S(1)}, bf16[1536,1536]{1,0:T(8,128)(2,1)}, u32[]{:S(2)}) copy-start(bf16[1536,1536]{1,0:T(8,128)(2,1)} %constant_dynamic-slice_fusion.1.refs_2_.refs_3_) | copy-start | bytes 14155780
  59.6 9.2 %copy-start.2 = (f32[768,768]{1,0:T(8,128)S(1)}, f32[768,768]{1,0:T(8,128)}, u32[]{:S(2)}) copy-start(f32[768,768]{1,0:T(8,128)} %copy-done.1) | copy-start | bytes 7077892
  59.6 16.8 %slice-start.1 = ((s8[4718592]{0:T(1024)(128)(4,1)}), s8[4194304]{0:T(1024)(128)(4,1)S(1)}, s32[]{:S(2)}) async-start(s8[4718592]{0:T(1024)(128)(4,1)} %bitcast.15), calls=%async_computation.1 | async-start | bytes 8388608
  62.6 13.8 %copy-start.11 = (f32[1536]{0:T(1024)S(1)}, f32[1536]{0:T(1024)}, u32[]{:S(2)}) copy-start(f32[1536]{0:T(1024)} %param.13) | copy-start | bytes 18436
  62.6 13.8 %copy-start.10 = (bf16[384,512]{1,0:T(8,128)(2,1)S(1)}, bf16[384,512]{1,0:T(8,128)(2,1)}, u32[]{:S(2)}) copy-start(bf16[384,512]{1,0:T(8,128)(2,1)} %copy-done.9) | copy-start | bytes 1179652
  67.6 8.8 %collective-permute-start.16 = (bf16[1536,384]{1,0:T(8,128)(2,1)}, bf16[1536,384]{1,0:T(8,128)(2,1)S(1)}, u32[]{:S(2)}, u32[]{:S(2)}) collective-permute-start(bf16[1536,384]{1,0:T(8,128)(2,1)} %collective-permute-done.5.refs_6_), channel_id=1, source_target_pairs={{0,1},{1,0},{2,3},{3,2},{4,5},{5,4},{6,7},{7,6},{8,9},{9,8},{10,11... | collective-permute-start | bytes 3538952 | tf_op jit(solution)/shard_map/ppermute | solution.py:39
  68.8 7.6 %collective-permute-start.17 = (bf16[1536,384]{1,0:T(8,128)(2,1)S(1)}, bf16[1536,384]{1,0:T(8,128)(2,1)S(1)}, u32[]{:S(2)}, u32[]{:S(2)}) collective-permute-start(bf16[1536,384]{1,0:T(8,128)(2,1)S(1)} %collective-permute-done.14.refs_8_), channel_id=1, source_target_pairs={{0,1},{1,0},{2,3},{3,2},{4,5},{5,4},{6,7},{7,6},{8,9},{9,8},{10,11... | collective-permute-start | bytes 3538952 | tf_op jit(solution)/shard_map/ppermute | solution.py:39
  74.0 2.3 %collective-permute-start.15 = (bf16[384,256]{1,0:T(8,128)(2,1)S(1)}, bf16[384,256]{1,0:T(8,128)(2,1)S(1)}, u32[]{:S(2)}, u32[]{:S(2)}) collective-permute-start(bf16[384,256]{1,0:T(8,128)(2,1)S(1)} %get-tuple-element.60), channel_id=1, source_target_pairs={{0,1},{1,0},{2,3},{3,2},{4,5},{5,4},{6,7},{7,6},{8,9},{9,8},{10,11... | collective-permute-start | bytes 589832 | tf_op jit(solution)/shard_map/ppermute | solution.py:39
  74.6 6.5 %collective-permute-start.18 = (bf16[384,256]{1,0:T(8,128)(2,1)S(1)}, bf16[384,256]{1,0:T(8,128)(2,1)S(1)}, u32[]{:S(2)}, u32[]{:S(2)}) collective-permute-start(bf16[384,256]{1,0:T(8,128)(2,1)S(1)} %get-tuple-element.59.refs_1_), channel_id=1, source_target_pairs={{0,2},{2,0},{1,3},{3,1},{4,6},{6,4},{5,7},{7,5},{8,10},{10,8},{9,1... | collective-permute-start | bytes 589832 | tf_op jit(solution)/shard_map/ppermute | solution.py:394
  74.9 10.6 %collective-permute-start.19 = (bf16[384,256]{1,0:T(8,128)(2,1)S(1)}, bf16[384,256]{1,0:T(8,128)(2,1)S(1)}, u32[]{:S(2)}, u32[]{:S(2)}) collective-permute-start(bf16[384,256]{1,0:T(8,128)(2,1)S(1)} %get-tuple-element.60), channel_id=1, source_target_pairs={{0,3},{1,2},{2,1},{3,0},{4,7},{5,6},{6,5},{7,4},{8,11},{9,10},{10,... | collective-permute-start | bytes 589832 | tf_op jit(solution)/shard_map/ppermute | solution.py:394
